TPU v7x, 128 devices: a whole 4x4x4 slice. The times are simulated.
128 devices in a mesh: dp: 8 (over x, core), tensor: 16 (over z, y).
Axes of the slice: x: 4, y: 4, z: 4, core: 2. Of those that a mesh axis runs over, the one named last changes fastest.
Arguments:
- acts: bfloat16 [16384, 8192], P(('dp', 'tensor')), may hold values from -6 to 6
- cot_kv: bfloat16 [16384, 2048], P('dp', 'tensor'), may hold values from -0.09375 to 0.09375
- w_kv: bfloat16 [8192, 2048], P(None, 'tensor'), may hold values from -4 to 4
- feedback: bfloat16 [65536, 2048], P('dp', 'tensor'), may hold values from -3 to 3
- q_init: float32 [2048, 64], P('tensor'), may hold values from -6 to 6
Outputs:
- input_grad: bfloat16 [16384, 8192], P(('dp', 'tensor'))
- update: bfloat16 [8192, 2048], P(None, 'tensor')
- q_factor: float32 [2048, 64], P('tensor')
- new_feedback: bfloat16 [65536, 2048], P('dp', 'tensor')
All inputs are finite; a program needn't handle non-finite values.
Results may differ from a plain program's by a relative error of at most 0.019.
Values may be sent and summed in bfloat16 or wider, within the bound.
No kernel may reach another device: no remote copies, remote signals or barrier semaphores. Data moves between devices by JAX's collectives and lax.ppermute only.
A program may use at most 192 MiB of HBM per device.

v0:
```python
import jax
import jax.numpy as jnp
from jax import lax
from jax.experimental import pallas as pl
from jax.experimental.pallas import tpu as pltpu
from jax.sharding import PartitionSpec as P

HD = 128
RANK = 64
SIDE = 4
TILE = 2048
WIDE = 2048
LONG = 4096
VMEM = 40 * 1024 * 1024
PART = 1024
F32 = jnp.float32
BF16 = jnp.bfloat16
HI = lax.Precision.HIGHEST
NN = (((1,), (0,)), ((), ()))
NT = (((1,), (1,)), ((), ()))
TN = (((0,), (0,)), ((), ()))


def along_tensor(array, dz, dy):
    perm = [
        (z * SIDE + y, (z + dz) % SIDE * SIDE + (y + dy) % SIDE)
        for z in range(SIDE)
        for y in range(SIDE)
    ]
    return lax.ppermute(array, "tensor", perm)


def along_dp(array, target):
    perm = []
    for x in range(SIDE):
        for c in range(2):
            to_x, to_c = target(x, c)
            perm.append((x * 2 + c, to_x % SIDE * 2 + to_c))
    return lax.ppermute(array, "dp", perm)


def other_core(array):
    return along_dp(array, lambda x, c: (x, 1 - c))


def cost(flops, moved):
    return pl.CostEstimate(flops=int(flops), bytes_accessed=int(moved), transcendentals=0)


def cols_spec(rows, cols):
    return pl.BlockSpec((rows, cols), lambda j: (0, j))


def rows_spec(rows, cols):
    return pl.BlockSpec((rows, cols), lambda j: (j, 0))


def whole_spec(rows, cols):
    return pl.BlockSpec((rows, cols), lambda j: (0, 0))


ANY_SPEC = pl.BlockSpec(memory_space=pl.ANY)
SMEM_SPEC = pl.BlockSpec(memory_space=pltpu.SMEM)


def halves(array):
    high = array.astype(BF16)
    return high, (array - high.astype(F32)).astype(BF16)


def dot3(left, right, dims):
    dot = lambda a, b: lax.dot_general(a, b, dims, preferred_element_type=F32)
    return dot(left[0], right[0]) + (dot(left[0], right[1]) + dot(left[1], right[0]))


def turn_kernel(spots, cots, cturn):
    for r in range(SIDE):
        block = cots.at[(spots[0] + r) % SIDE]
        for s in range(SIDE):
            rows = pl.ds(pl.multiple_of((spots[1] + s) % SIDE * HD, HD), HD)
            cturn[r * HD : (r + 1) * HD, s * HD : (s + 1) * HD] = block[rows, :].T


def turn_cots(spots, cots):
    flat = cots.shape[1]
    return pl.pallas_call(
        turn_kernel,
        in_specs=[SMEM_SPEC, pl.BlockSpec(memory_space=pltpu.VMEM)],
        out_specs=pl.BlockSpec(memory_space=pltpu.VMEM),
        out_shape=jax.ShapeDtypeStruct((SIDE * HD, flat), BF16),
        cost_estimate=cost(0, 4 * SIDE * HD * flat),
        name="turn_cots",
    )(spots, cots)


def grad_kernel(a0, a1, a2lo, a2hi, a3, cturn, own, up, down, rest):
    j = pl.program_id(0)
    mid = pl.num_programs(0) // 2
    tokens = jnp.concatenate([a0[...], a1[...], a2lo[...], a2hi[...], a3[...]], axis=0)
    grads = lax.dot_general(cturn[...], tokens, NN, preferred_element_type=F32)
    own[...] = grads[:HD]
    ahead = grads[HD : 2 * HD].astype(BF16)
    across = grads[2 * HD : 3 * HD].astype(BF16)
    behind = grads[3 * HD :].astype(BF16)

    @pl.when(j < mid)
    def _():
        up[...] = across
        down[...] = behind
        rest[...] = ahead

    @pl.when(j >= mid)
    def _():
        up[...] = ahead
        down[...] = across
        rest[...] = behind


def grad_parts(pieces, cturn):
    rows, width = pieces[0].shape
    flat = SIDE * rows
    mid = width // TILE // 2
    stacked = pl.BlockSpec((HD, TILE), lambda j: (j // mid, j % mid))
    return pl.pallas_call(
        grad_kernel,
        grid=(width // TILE,),
        in_specs=[cols_spec(piece.shape[0], TILE) for piece in pieces]
        + [whole_spec(SIDE * HD, flat)],
        out_specs=[cols_spec(HD, TILE)] + [stacked] * 3,
        out_shape=[jax.ShapeDtypeStruct((HD, width), F32)]
        + [jax.ShapeDtypeStruct((2 * HD, width // 2), BF16)] * 3,
        cost_estimate=cost(2 * width * SIDE * flat * HD, 9 * width * HD * 2),
        name="grad_parts",
    )(*pieces, cturn)


def input_product(mine, theirs, cots):
    first = pl.program_id(0) < pl.num_programs(0) // 2
    weights = jnp.concatenate(
        [jnp.where(first, mine[k], theirs[k]) for k in range(SIDE)], axis=1
    )
    return lax.dot_general(cots, weights, NT, preferred_element_type=F32)


def input_kernel(spots, mine, theirs, cots, out):
    lined = jnp.concatenate([cots[k] for k in range(SIDE)], axis=1)
    out[...] = input_product(mine, theirs, lined).astype(BF16)


def input_parts(spots, gathered, cots):
    piece = gathered[0].shape[1]
    flat = cots.shape[1]
    mid = piece // PART
    place = lambda j, spots: (spots[2] + j // mid) % 2 * mid + j % mid
    return pl.pallas_call(
        input_kernel,
        grid_spec=pltpu.PrefetchScalarGridSpec(
            num_scalar_prefetch=1,
            grid=(2 * mid,),
            in_specs=[
                pl.BlockSpec((SIDE, PART, HD), lambda j, spots: (0, jnp.minimum(j, mid - 1), 0)),
                pl.BlockSpec((SIDE, PART, HD), lambda j, spots: (0, jnp.maximum(j - mid, 0), 0)),
                pl.BlockSpec((SIDE, flat, HD), lambda j, spots: (0, 0, 0)),
            ],
            out_specs=pl.BlockSpec((flat, PART), lambda j, spots: (0, place(j, spots))),
        ),
        out_shape=jax.ShapeDtypeStruct((flat, 2 * piece), BF16),
        cost_estimate=cost(4 * piece * SIDE * flat * HD, 18 * piece * HD * 2),
        name="input_parts",
    )(spots, *gathered, cots)


def merge_kernel(fb, own, pl_lo, pl_hi, su_lo, su_hi, qrows, *refs):
    merged, keep, give = refs[-3:]
    j = pl.program_id(0)
    mid = pl.num_programs(0) // 2
    base = fb[...].astype(F32) + own[...]

    def finish(plain, summed):
        total = base + (plain[...].astype(F32) + summed[...].astype(F32))
        merged[...] = total
        share = dot3(halves(qrows[...]), halves(total), NN)
        keep[...] = share[: RANK // 2]
        give[...] = share[RANK // 2 :]

    @pl.when(j < mid)
    def _():
        finish(pl_lo, su_lo)

    @pl.when(j >= mid)
    def _():
        finish(pl_hi, su_hi)


def merge(feedback, own, sums, qrows, part, before):
    got_up, got_down, sum_up, sum_down = sums
    width = own.shape[1]
    steps = width // WIDE
    mid = steps // 2
    first = part * steps
    shifted = lambda rows: pl.BlockSpec((rows, WIDE), lambda j: (0, first + j))
    low = pl.BlockSpec((HD, WIDE), lambda j: (0, jnp.minimum(j, mid - 1)))
    high = pl.BlockSpec((HD, WIDE), lambda j: (1, jnp.maximum(j - mid, 0)))
    high_from = pl.BlockSpec((HD, WIDE), lambda j: (0, jnp.maximum(j - mid, 0)))
    return pl.pallas_call(
        merge_kernel,
        grid=(steps,),
        in_specs=[shifted(HD), cols_spec(HD, WIDE), low, high, low, high_from, whole_spec(RANK, HD)]
        + [ANY_SPEC] * len(before),
        out_specs=[shifted(HD), shifted(RANK // 2), shifted(RANK // 2)],
        out_shape=[
            jax.ShapeDtypeStruct((HD, 2 * width), F32),
            jax.ShapeDtypeStruct((RANK // 2, 2 * width), F32),
            jax.ShapeDtypeStruct((RANK // 2, 2 * width), F32),
        ],
        input_output_aliases={7 + k: k for k in range(len(before))},
        cost_estimate=cost(6 * width * RANK * HD, 14 * width * HD),
        name="merge",
    )(feedback, own, got_down, got_up, sum_up, sum_down, qrows, *before)


def ordered(core, mine, theirs):
    first = jnp.where(core == 0, mine[...], theirs[...])
    second = jnp.where(core == 0, theirs[...], mine[...])
    return jnp.concatenate([first, second], axis=0)


def gram_kernel(spots, mine, theirs, merged, right, gram):
    @pl.when(pl.program_id(0) == 0)
    def _():
        gram[...] = jnp.zeros_like(gram)
        right[...] = jnp.zeros_like(right)

    pt = halves(ordered(spots[2], mine, theirs))
    right[...] += dot3(halves(merged[...]), pt, NT)
    gram[...] += dot3(pt, pt, NT)


def gram_of(spots, mine, theirs, merged):
    width = merged.shape[1]
    half = RANK // 2
    return pl.pallas_call(
        gram_kernel,
        grid=(width // LONG,),
        in_specs=[SMEM_SPEC, cols_spec(half, LONG), cols_spec(half, LONG), cols_spec(HD, LONG)],
        out_specs=[whole_spec(HD, RANK), whole_spec(RANK, RANK)],
        out_shape=[
            jax.ShapeDtypeStruct((HD, RANK), F32),
            jax.ShapeDtypeStruct((RANK, RANK), F32),
        ],
        cost_estimate=cost(6 * width * RANK * (RANK + HD), 6 * width * HD),
        compiler_params=pltpu.CompilerParams(vmem_limit_bytes=VMEM),
        name="gram",
    )(spots, mine, theirs, merged)


def inverse_kernel(gram, out):
    row = lax.broadcasted_iota(jnp.int32, (RANK, RANK), 0)
    col = lax.broadcasted_iota(jnp.int32, (RANK, RANK), 1)
    eye = jnp.where(row == col, 1.0, 0.0).astype(F32)
    mat = jnp.concatenate([gram[...], eye], axis=1)
    below = lax.broadcasted_iota(jnp.int32, (RANK, 1), 0)
    for k in range(RANK - 1):
        pivot = mat[k : k + 1, :]
        column = mat[:, k : k + 1]
        factor = jnp.where(below > k, column / mat[k : k + 1, k : k + 1], 0.0)
        mat = mat - factor * pivot
    diag = jnp.sum(jnp.where(row == col, mat[:, :RANK], 0.0), axis=1, keepdims=True)
    out[...] = mat[:, RANK:] / jnp.sqrt(diag)


def inverse_factor(gram):
    return pl.pallas_call(
        inverse_kernel,
        out_shape=jax.ShapeDtypeStruct((RANK, RANK), F32),
        cost_estimate=cost(RANK * RANK * RANK * 400, RANK * RANK * 16),
        name="inverse_factor",
    )(gram)


def final_kernel(replicas, spots, inv, rsum, mine, theirs, merged, qt, update, newfb, zhi, zlo):
    @pl.when(pl.program_id(0) == 0)
    def _():
        right = lax.dot_general(inv[...], rsum[...], NT, precision=HI, preferred_element_type=F32)
        right = right * (1.0 / replicas)
        qt[...] = right
        zturn = lax.dot_general(right, inv[...], TN, precision=HI, preferred_element_type=F32)
        zhi[...], zlo[...] = halves(zturn)

    pt = halves(ordered(spots[2], mine, theirs))
    approx = dot3((zhi[...], zlo[...]), pt, NN)
    update[...] = approx.astype(BF16).T
    newfb[...] = (merged[...] - approx).astype(BF16).T


def final(spots, inv, rsum, mine, theirs, merged, replicas):
    width = merged.shape[1]
    half = RANK // 2
    return pl.pallas_call(
        lambda *refs: final_kernel(replicas, *refs),
        grid=(width // WIDE,),
        in_specs=[
            SMEM_SPEC,
            whole_spec(RANK, RANK),
            whole_spec(HD, RANK),
            cols_spec(half, WIDE),
            cols_spec(half, WIDE),
            cols_spec(HD, WIDE),
        ],
        out_specs=[whole_spec(RANK, HD), rows_spec(WIDE, HD), rows_spec(WIDE, HD)],
        out_shape=[
            jax.ShapeDtypeStruct((RANK, HD), F32),
            jax.ShapeDtypeStruct((width, HD), BF16),
            jax.ShapeDtypeStruct((width, HD), BF16),
        ],
        scratch_shapes=[pltpu.VMEM((HD, RANK), BF16)] * 2,
        cost_estimate=cost(6 * width * RANK * HD, 12 * width * HD),
        name="final",
    )(spots, inv, rsum, mine, theirs, merged)


def tied(arrays, others):
    return lax.optimization_barrier((arrays, others))[0]


def neighbours(block, step):
    return step(block, 1), step(block, -1)


def to_pass_on(before, after):
    rows = before.shape[0]
    return before[: rows // 2], after[rows // 2 :]


def gather_line(block, before, after, passed, step):
    return block, after, step(passed[0], 1), step(passed[1], -1), before


def scatter_near(up, down, step):
    return step(up, 1), step(down, -1)


def scatter_far(got_up, got_down, rest, step):
    mid = rest.shape[0] // 2
    low = lambda array: array[:mid].astype(F32)
    high = lambda array: array[mid:].astype(F32)
    sum_up = step((low(rest) + low(got_up)).astype(BF16), 1)
    sum_down = step((high(rest) + high(got_down)).astype(BF16), -1)
    return got_up, got_down, sum_up, sum_down


def sum_left(keep, give):
    chip = (keep + other_core(give)).astype(BF16)
    mid = chip.shape[0] // 2
    near = lambda array: along_dp(array, lambda x, c: (x ^ 1, c))
    far = lambda array: along_dp(array, lambda x, c: (3 - x, c))
    add = lambda a, b: a.astype(F32) + b.astype(F32)
    first, second = chip[:mid], chip[mid:]
    first_pair = add(first, near(first)).astype(BF16)
    second_pair = add(second, far(second)).astype(BF16)
    mine = jnp.concatenate(
        [add(first_pair, far(first_pair)), add(second_pair, near(second_pair))], axis=0
    )
    return mine, other_core(mine)


def sum_right(part):
    chip = part + other_core(part)
    ahead = along_dp(chip, lambda x, c: (x + 1, c))
    behind = along_dp(chip, lambda x, c: (x - 1, c))
    across = along_dp(chip, lambda x, c: (x + 2, c))
    return (chip + across) + (ahead + behind)


def local(acts, cot_kv, w_kv, feedback, q_init):
    tokens, width = acts.shape
    half = width // 2
    replicas = lax.axis_size("dp")
    place = lax.axis_index("dp")
    core = place % 2
    spot = lax.axis_index("tensor")
    z, y = spot // SIDE, spot % SIDE
    spots = jnp.stack([z, y, core]).astype(jnp.int32)
    in_y = lambda array, k: along_tensor(array, 0, k)
    in_z = lambda array, k: along_tensor(array, k, 0)
    lines_z = [[z * SIDE + y for z in range(SIDE)] for y in range(SIDE)]
    lines_y = [[z * SIDE + y for y in range(SIDE)] for z in range(SIDE)]
    flat = SIDE * tokens

    blocks = acts[:, :half], acts[:, half:]
    near = neighbours(blocks[0], in_y)
    cots = lax.all_to_all(
        cot_kv, "tensor", 0, 0, axis_index_groups=lines_z, tiled=True
    ).reshape(SIDE, flat, HD)
    share = lax.dynamic_slice(w_kv, (core * half, 0), (half, HD))
    weights = lax.all_gather(share, "tensor", axis=0, axis_index_groups=lines_z)

    fb_turned = feedback.T
    qcols = q_init.T
    qrows = jnp.where(
        core == 0, qcols, jnp.concatenate([qcols[RANK // 2 :], qcols[: RANK // 2]], axis=0)
    )
    near, fb_turned, qrows, cots = lax.optimization_barrier((near, fb_turned, qrows, cots))
    cturn = turn_cots(spots, cots)
    pieces = gather_line(blocks[0], *near, to_pass_on(*near), in_y)
    near = neighbours(tied(blocks[1], pieces), in_y)
    own_a, up, down, rest_a = grad_parts(pieces, cturn)
    got_a = scatter_near(up, down, in_z)
    near, up = lax.optimization_barrier((near, up))
    passed = tied(to_pass_on(*near), got_a)
    pieces = gather_line(blocks[1], *near, passed, in_y)

    weights = tied(weights, (near, got_a))
    shares = input_parts(spots, (weights, other_core(weights)), cots)
    sums_a = scatter_far(*got_a, rest_a, in_z)

    pieces, sums_a, shares = lax.optimization_barrier((pieces, sums_a, shares))
    own_b, up, down, rest_b = grad_parts(pieces, cturn)
    got_b = scatter_near(up, down, in_z)
    input_grad = lax.psum_scatter(
        tied(shares, up), "tensor", scatter_dimension=0, axis_index_groups=lines_y, tiled=True
    )

    left = merge(fb_turned, own_a, tied(sums_a, got_b), qrows, 0, ())
    sums_b = scatter_far(*got_b, rest_b, in_z)
    sums_b, left = lax.optimization_barrier((sums_b, left))
    merged, keep, give = merge(fb_turned, own_b, sums_b, qrows, 1, left)
    mine, theirs = sum_left(keep, give)
    right, gram = gram_of(spots, mine, theirs, merged)
    inv = inverse_factor(gram)
    rsum = sum_right(right)
    qt, update, new_feedback = final(spots, inv, rsum, mine, theirs, merged, replicas)
    return input_grad, update, qt.T, new_feedback


def solution(mesh):
    placed = (
        P(("dp", "tensor"), None),
        P("dp", "tensor"),
        P(None, "tensor"),
        P("dp", "tensor"),
        P("tensor", None),
    )
    return jax.shard_map(
        local,
        mesh=mesh,
        in_specs=placed,
        out_specs=(
            P(("dp", "tensor"), None),
            P(None, "tensor"),
            P("tensor", None),
            P("dp", "tensor"),
        ),
        check_vma=False,
    )
```

profile of v0, /device:TPU:1, one launch (start us, length us, event | category | flops | bytes accessed | tf_op | source)
XLA Modules:
  0.0 228.4 jit_solution(13019603772129791039)
XLA Ops:
  7.2 1.5 copy-done
  9.8 2.7 %fusion = (bf16[128,4096]{1,0:T(8,128)(2,1)S(1)}, bf16[128,4096]{1,0:T(8,128)(2,1)}) fusion(bf16[128,8192]{1,0:T(8,128)(2,1)} %param.5), kind=kLoop, calls=%fused_computation.14 | loop fusion | bytes 4194304 | tf_op jit(solution)/shard_map/slice | solution.py:390
  12.5 3.6 %collective-permute-start.1 = (bf16[128,4096]{1,0:T(8,128)(2,1)S(1)}, bf16[128,4096]{1,0:T(8,128)(2,1)S(1)}, u32[]{:S(2)}, u32[]{:S(2)}) collective-permute-start(bf16[128,4096]{1,0:T(8,128)(2,1)S(1)} %get-tuple-element.108.a0), channel_id=1, source_target_pairs={{0,3},{1,0},{2,1},{3,2},{4,7},{5,4},{6,5},{7,6},{8,11},{9,8},{10,9... | collective-permute-start | bytes 3145736 | tf_op jit(solution)/shard_map/ppermute | solution.py:30
  16.1 5.0 %all-to-all-start = ((bf16[4,512,128]{2,1,0:T(8,128)(2,1)}), bf16[4,512,128]{2,1,0:T(8,128)(2,1)S(1)}, u32[]{:S(2)}, u32[]{:S(2)}) async-start(bf16[4,512,128]{2,1,0:T(8,128)(2,1)} %bitcast.2), calls=%async_computation | async-start | bytes 1048576 | tf_op jit(solution)/shard_map/all_to_all | solution.py:392
  21.1 4.2 %copy.12 = bf16[8192,128]{0,1:T(8,128)(2,1)} copy(bf16[8192,128]{1,0:T(8,128)(2,1)} %param.8) | data formatting | bytes 4194304 | tf_op args[3]
  26.0 4.1 %all-to-all-done.cots = bf16[4,512,128]{2,1,0:T(8,128)(2,1)S(1)} async-done(((bf16[4,512,128]{2,1,0:T(8,128)(2,1)}), bf16[4,512,128]{2,1,0:T(8,128)(2,1)S(1)}, u32[]{:S(2)}, u32[]{:S(2)}) %all-to-all-start) | async-done | bytes 524320 | tf_op jit(solution)/shard_map/all_to_all | solution.py:392
  30.1 7.8 %collective-permute-done.1.a1 = bf16[128,4096]{1,0:T(8,128)(2,1)S(1)} collective-permute-done((bf16[128,4096]{1,0:T(8,128)(2,1)S(1)}, bf16[128,4096]{1,0:T(8,128)(2,1)S(1)}, u32[]{:S(2)}, u32[]{:S(2)}) %collective-permute-start.1) | collective-permute-done | bytes 1048608 | tf_op jit(solution)/shard_map/ppermute | solution.py:30
  37.9 3.2 %collective-permute-done.a3 = bf16[128,4096]{1,0:T(8,128)(2,1)} collective-permute-done((bf16[128,4096]{1,0:T(8,128)(2,1)S(1)}, bf16[128,4096]{1,0:T(8,128)(2,1)}, u32[]{:S(2)}, u32[]{:S(2)}) %collective-permute-start) | collective-permute-done | bytes 1048608 | tf_op jit(solution)/shard_map/ppermute | solution.py:30
  42.3 2.7 %collective-permute-start.3 = (bf16[64,4096]{1,0:T(8,128)(2,1)S(1)}, bf16[64,4096]{1,0:T(8,128)(2,1)}, u32[]{:S(2)}, u32[]{:S(2)}) collective-permute-start(bf16[64,4096]{1,0:T(8,128)(2,1)S(1)} %slice.59), channel_id=1, source_target_pairs={{0,3},{1,0},{2,1},{3,2},{4,7},{5,4},{6,5},{7,6},{8,11},{9,8},{10,9... | collective-permute-start | bytes 1572872 | tf_op jit(solution)/shard_map/ppermute | solution.py:30
  45.6 2.1 turn_cots.1.cturn
  47.7 7.5 %collective-permute-done.2.a2lo = bf16[64,4096]{1,0:T(8,128)(2,1)S(1)} collective-permute-done((bf16[64,4096]{1,0:T(8,128)(2,1)S(1)}, bf16[64,4096]{1,0:T(8,128)(2,1)S(1)}, u32[]{:S(2)}, u32[]{:S(2)}) %collective-permute-start.2) | collective-permute-done | bytes 524320 | tf_op jit(solution)/shard_map/ppermute | solution.py:30
  55.2 2.4 %collective-permute-start.5 = (bf16[128,4096]{1,0:T(8,128)(2,1)}, bf16[128,4096]{1,0:T(8,128)(2,1)}, u32[]{:S(2)}, u32[]{:S(2)}) collective-permute-start(bf16[128,4096]{1,0:T(8,128)(2,1)} %get-tuple-element.69.a0), channel_id=1, source_target_pairs={{0,3},{1,0},{2,1},{3,2},{4,7},{5,4},{6,5},{7,6},{8,11},{9,8},{10,9... | collective-permute-start | bytes 3145736 | tf_op jit(solution)/shard_map/ppermute | solution.py:30
  57.6 6.4 %grad_parts.2 = (f32[128,4096]{1,0:T(8,128)}, bf16[256,2048]{1,0:T(8,128)(2,1)}, bf16[256,2048]{1,0:T(8,128)(2,1)}, bf16[256,2048]{1,0:T(8,128)(2,1)}) custom-call(bf16[128,4096]{1,0:T(8,128)(2,1)} %copy-done.14, bf16[128,4096]{1,0:T(8,128)(2,1)} %copy-done.19, bf16[64,4096]{1,0:T(8,128)(2,1)} %copy-done.21, bf16[64,4096]{1,0:T(8,128)(2,1)} %collective-permute-done.3.a2hi, ...), custom_call_target="tpu_custom_call" | custom-call | flops 2147483648 | bytes 9437184 | tf_op jit(solution)/shard_map/grad_parts/pallas_call | solution.py:124
  64.0 3.8 %collective-permute-start.7 = (bf16[256,2048]{1,0:T(8,128)(2,1)}, bf16[256,2048]{1,0:T(8,128)(2,1)S(1)}, u32[]{:S(2)}, u32[]{:S(2)}) collective-permute-start(bf16[256,2048]{1,0:T(8,128)(2,1)} %get-tuple-element.63), channel_id=1, source_target_pairs={{0,12},{1,13},{2,14},{3,15},{4,0},{5,1},{6,2},{7,3},{8,4},{9,5},{1... | collective-permute-start | bytes 3145736 | tf_op jit(solution)/shard_map/ppermute | solution.py:30
  67.8 9.7 %collective-permute-done.5.a1 = bf16[128,4096]{1,0:T(8,128)(2,1)} collective-permute-done((bf16[128,4096]{1,0:T(8,128)(2,1)}, bf16[128,4096]{1,0:T(8,128)(2,1)}, u32[]{:S(2)}, u32[]{:S(2)}) %collective-permute-start.5) | collective-permute-done | bytes 1048608 | tf_op jit(solution)/shard_map/ppermute | solution.py:30
  77.5 2.9 %collective-permute-done.4.a3 = bf16[128,4096]{1,0:T(8,128)(2,1)} collective-permute-done((bf16[128,4096]{1,0:T(8,128)(2,1)}, bf16[128,4096]{1,0:T(8,128)(2,1)}, u32[]{:S(2)}, u32[]{:S(2)}) %collective-permute-start.4) | collective-permute-done | bytes 1048608 | tf_op jit(solution)/shard_map/ppermute | solution.py:30
  80.4 6.7 %collective-permute-done.7.pl_lo = bf16[256,2048]{1,0:T(8,128)(2,1)S(1)} collective-permute-done((bf16[256,2048]{1,0:T(8,128)(2,1)}, bf16[256,2048]{1,0:T(8,128)(2,1)S(1)}, u32[]{:S(2)}, u32[]{:S(2)}) %collective-permute-start.7) | collective-permute-done | bytes 1048608 | tf_op jit(solution)/shard_map/ppermute | solution.py:30
  87.2 3.0 %collective-permute-done.6.pl_hi = bf16[256,2048]{1,0:T(8,128)(2,1)S(1)} collective-permute-done((bf16[256,2048]{1,0:T(8,128)(2,1)}, bf16[256,2048]{1,0:T(8,128)(2,1)S(1)}, u32[]{:S(2)}, u32[]{:S(2)}) %collective-permute-start.6) | collective-permute-done | bytes 1048608 | tf_op jit(solution)/shard_map/ppermute | solution.py:30
  90.2 4.6 %collective-permute-start.12 = (bf16[4,4096,128]{2,1,0:T(8,128)(2,1)}, bf16[4,4096,128]{2,1,0:T(8,128)(2,1)}, u32[]{:S(2)}, u32[]{:S(2)}) collective-permute-start(bf16[4,4096,128]{2,1,0:T(8,128)(2,1)} %bitcast.11), channel_id=1, source_target_pairs={{0,16},{16,0},{32,48},{48,32},{64,80},{80,64},{96,112},{112,96},{1... | collective-permute-start | bytes 12582920 | tf_op jit(solution)/shard_map/ppermute | solution.py:39
  94.8 1.9 slice.61
  96.6 1.9 slice.60
  98.5 2.7 %collective-permute-start.9 = (bf16[64,4096]{1,0:T(8,128)(2,1)}, bf16[64,4096]{1,0:T(8,128)(2,1)}, u32[]{:S(2)}, u32[]{:S(2)}) collective-permute-start(bf16[64,4096]{1,0:T(8,128)(2,1)} %slice.61), channel_id=1, source_target_pairs={{0,3},{1,0},{2,1},{3,2},{4,7},{5,4},{6,5},{7,6},{8,11},{9,8},{10,9... | collective-permute-start | bytes 1572872 | tf_op jit(solution)/shard_map/ppermute | solution.py:30
  101.2 1.4 add_convert_fusion.3
  102.7 1.4 collective-permute-start.10
  104.0 12.2 %input_parts.1 = bf16[512,8192]{1,0:T(8,128)(2,1)} custom-call(s32[3]{0:T(128)} %pad_add_fusion.spots.refs_0_, bf16[4,4096,128]{2,1,0:T(8,128)(2,1)} %bitcast.12, bf16[4,4096,128]{2,1,0:T(8,128)(2,1)} %collective-permute-done.12.theirs, bf16[4,512,128]{2,1,0:T(8,128)(2,1)} %copy-done.7), custom_call_target="tpu_custom_call" | custom-call | flops 4294967296 | bytes 18874368 | tf_op jit(solution)/shard_map/input_parts/pallas_call | solution.py:155
  116.3 6.6 %grad_parts.3 = (f32[128,4096]{1,0:T(8,128)}, bf16[256,2048]{1,0:T(8,128)(2,1)}, bf16[256,2048]{1,0:T(8,128)(2,1)}, bf16[256,2048]{1,0:T(8,128)(2,1)}) custom-call(bf16[128,4096]{1,0:T(8,128)(2,1)} %get-tuple-element.69.a0, bf16[128,4096]{1,0:T(8,128)(2,1)} %collective-permute-done.5.a1, bf16[64,4096]{1,0:T(8,128)(2,1)} %collective-permute-done.8.a2lo, ...), custom_call_target="tpu_custom_call" | custom-call | flops 2147483648 | bytes 9437184 | tf_op jit(solution)/shard_map/grad_parts/pallas_call | solution.py:124
  123.0 1.4 collective-permute-start.14
  124.5 21.5 %collective-permute-done.14.pl_lo = bf16[256,2048]{1,0:T(8,128)(2,1)S(1)} collective-permute-done((bf16[256,2048]{1,0:T(8,128)(2,1)}, bf16[256,2048]{1,0:T(8,128)(2,1)S(1)}, u32[]{:S(2)}, u32[]{:S(2)}) %collective-permute-start.14) | collective-permute-done | bytes 1048608 | tf_op jit(solution)/shard_map/ppermute | solution.py:30
  146.1 2.7 %collective-permute-done.13.pl_hi = bf16[256,2048]{1,0:T(8,128)(2,1)S(1)} collective-permute-done((bf16[256,2048]{1,0:T(8,128)(2,1)}, bf16[256,2048]{1,0:T(8,128)(2,1)S(1)}, u32[]{:S(2)}, u32[]{:S(2)}) %collective-permute-start.13) | collective-permute-done | bytes 1048608 | tf_op jit(solution)/shard_map/ppermute | solution.py:30
  148.8 1.4 add_convert_fusion.1
  151.6 5.0 %merge.2 = (f32[128,8192]{1,0:T(8,128)}, f32[32,8192]{1,0:T(8,128)}, f32[32,8192]{1,0:T(8,128)}) custom-call(bf16[128,8192]{1,0:T(8,128)(2,1)} %bitcast.9, f32[128,4096]{1,0:T(8,128)} %get-tuple-element.80.own, bf16[256,2048]{1,0:T(8,128)(2,1)} %copy-done.8, bf16[256,2048]{1,0:T(8,128)(2,1)} %copy-done.9, bf16[128,2048]{1,0:T(8,128)(2,1)} %copy-done.16, ...), custom_call_target="tpu_custom_call" | custom-call | flops 201326592 | bytes 7340032 | tf_op jit(solution)/shard_map/merge/pallas_call | solution.py:205
  156.6 4.7 %collective-permute-done.16.su_hi = bf16[128,2048]{1,0:T(8,128)(2,1)S(1)} collective-permute-done((bf16[128,2048]{1,0:T(8,128)(2,1)}, bf16[128,2048]{1,0:T(8,128)(2,1)S(1)}, u32[]{:S(2)}, u32[]{:S(2)}) %collective-permute-start.16) | collective-permute-done | bytes 524320 | tf_op jit(solution)/shard_map/ppermute | solution.py:30
  161.3 1.8 collective-permute-done.15.su_lo
  163.9 4.8 %merge.3 = (f32[128,8192]{1,0:T(8,128)}, f32[32,8192]{1,0:T(8,128)}, f32[32,8192]{1,0:T(8,128)}) custom-call(bf16[128,8192]{1,0:T(8,128)(2,1)} %bitcast.10, f32[128,4096]{1,0:T(8,128)} %get-tuple-element.77.own, bf16[256,2048]{1,0:T(8,128)(2,1)} %copy-done.10, ...), custom_call_target="tpu_custom_call", output_to_operand_aliasing={{0}: (7, {}), {1}: (8, {}), {2}: (9, {})} | custom-call | flops 201326592 | bytes 7340032 | tf_op jit(solution)/shard_map/merge/pallas_call | solution.py:205
  168.7 3.4 %collective-permute-start.17 = (f32[32,8192]{1,0:T(8,128)}, f32[32,8192]{1,0:T(8,128)S(1)}, u32[]{:S(2)}, u32[]{:S(2)}) collective-permute-start(f32[32,8192]{1,0:T(8,128)} %get-tuple-element.101), channel_id=1, source_target_pairs={{0,16},{16,0},{32,48},{48,32},{64,80},{80,64},{96,112},{112,96},{1... | collective-permute-start | bytes 3145736 | tf_op jit(solution)/shard_map/ppermute | solution.py:39
  172.1 2.5 %collective-permute-done.17 = f32[32,8192]{1,0:T(8,128)S(1)} collective-permute-done((f32[32,8192]{1,0:T(8,128)}, f32[32,8192]{1,0:T(8,128)S(1)}, u32[]{:S(2)}, u32[]{:S(2)}) %collective-permute-start.17) | collective-permute-done | bytes 1048608 | tf_op jit(solution)/shard_map/ppermute | solution.py:39
  174.6 1.4 add_convert_fusion
  177.3 1.8 collective-permute-start.20
  179.1 4.6 %collective-permute-done.18 = bf16[16,8192]{1,0:T(8,128)(2,1)S(1)} collective-permute-done((bf16[16,8192]{1,0:T(8,128)(2,1)S(1)}, bf16[16,8192]{1,0:T(8,128)(2,1)S(1)}, u32[]{:S(2)}, u32[]{:S(2)}) %collective-permute-start.18) | collective-permute-done | bytes 262176 | tf_op jit(solution)/shard_map/ppermute | solution.py:39
  183.7 2.1 collective-permute-done.20
  185.9 1.9 collective-permute-start.19
  187.8 5.9 %collective-permute-done.19 = bf16[16,8192]{1,0:T(8,128)(2,1)S(1)} collective-permute-done((bf16[16,8192]{1,0:T(8,128)(2,1)S(1)}, bf16[16,8192]{1,0:T(8,128)(2,1)S(1)}, u32[]{:S(2)}, u32[]{:S(2)}) %collective-permute-start.19) | collective-permute-done | bytes 262176 | tf_op jit(solution)/shard_map/ppermute | solution.py:39
  194.2 2.6 %collective-permute-start.22 = (f32[32,8192]{1,0:T(8,128)S(1)}, f32[32,8192]{1,0:T(8,128)S(1)}, u32[]{:S(2)}, u32[]{:S(2)}) collective-permute-start(f32[32,8192]{1,0:T(8,128)S(1)} %pad_maximum_fusion.mine.refs_3_), channel_id=1, source_target_pairs={{0,16},{16,0},{32,48},{48,32},{64,80},{80,64},{96,112},{112,96},{1... | collective-permute-start | bytes 3145736 | tf_op jit(solution)/shard_map/ppermute | solution.py:39
  196.8 2.3 %collective-permute-done.22.theirs.refs_4_ = f32[32,8192]{1,0:T(8,128)S(1)} collective-permute-done((f32[32,8192]{1,0:T(8,128)S(1)}, f32[32,8192]{1,0:T(8,128)S(1)}, u32[]{:S(2)}, u32[]{:S(2)}) %collective-permute-start.22) | collective-permute-done | bytes 1048608 | tf_op jit(solution)/shard_map/ppermute | solution.py:39
  199.1 3.7 %gram.1 = (f32[128,64]{1,0:T(8,128)S(1)}, f32[64,64]{1,0:T(8,128)S(1)}) custom-call(s32[3]{0:T(128)S(1)} %copy-done.5, f32[32,8192]{1,0:T(8,128)S(1)} %pad_maximum_fusion.mine.refs_3_, f32[32,8192]{1,0:T(8,128)S(1)} %collective-permute-done.22.theirs.refs_4_, f32[128,8192]{1,0:T(8,128)S(1)} %copy-done.2), custom_call_target="tpu_custom_call" | custom-call | flops 603979776 | bytes 6291456 | tf_op jit(solution)/shard_map/gram/pallas_call | solution.py:242
  204.2 1.3 collective-permute-start.26
  206.8 6.8 %inverse_factor.1.refs_1_ = f32[64,64]{1,0:T(8,128)} custom-call(f32[64,64]{1,0:T(8,128)} %copy-done.6), custom_call_target="tpu_custom_call" | custom-call | flops 104857600 | bytes 65536 | tf_op jit(solution)/shard_map/inverse_factor/pallas_call | solution.py:273
  214.3 7.2 %final.1 = (f32[64,128]{1,0:T(8,128)}, bf16[8192,128]{1,0:T(8,128)(2,1)}, bf16[8192,128]{1,0:T(8,128)(2,1)}) custom-call(s32[3]{0:T(128)} %pad_add_fusion.spots.refs_0_, f32[64,64]{1,0:T(8,128)} %inverse_factor.1.refs_1_, f32[128,64]{1,0:T(8,128)} %add_add_fusion.refs_2_, f32[32,8192]{1,0:T(8,128)} %copy-done.3, f32[32,8192]{1,0:T(8,128)} %copy-done.4, ...), custom_call_target="tpu_custom_call" | custom-call | flops 402653184 | bytes 12582912 | tf_op jit(solution)/shard_map/final/pallas_call | solution.py:299
  (87 shorter events, 11.4 us)
Async XLA Ops:
  7.2 83.0 %all-gather.3.cloned.1.call-start = ((), (), s32[]{:S(2)}) async-start(), calls=%async_computation.3 | async-start | bytes 5242880 | tf_op jit(solution)/shard_map/all_gather | solution.py:396
  12.5 12.8 %copy-start.14 = (bf16[128,4096]{1,0:T(8,128)(2,1)}, bf16[128,4096]{1,0:T(8,128)(2,1)S(1)}, u32[]{:S(2)}) copy-start(bf16[128,4096]{1,0:T(8,128)(2,1)S(1)} %get-tuple-element.108.a0) | copy-start | bytes 3145732
  12.5 25.4 %collective-permute-start.1 = (bf16[128,4096]{1,0:T(8,128)(2,1)S(1)}, bf16[128,4096]{1,0:T(8,128)(2,1)S(1)}, u32[]{:S(2)}, u32[]{:S(2)}) collective-permute-start(bf16[128,4096]{1,0:T(8,128)(2,1)S(1)} %get-tuple-element.108.a0), channel_id=1, source_target_pairs={{0,3},{1,0},{2,1},{3,2},{4,7},{5,4},{6,5},{7,6},{8,11},{9,8},{10,9... | collective-permute-start | bytes 3145736 | tf_op jit(solution)/shard_map/ppermute | solution.py:30
  16.1 25.0 %collective-permute-start = (bf16[128,4096]{1,0:T(8,128)(2,1)S(1)}, bf16[128,4096]{1,0:T(8,128)(2,1)}, u32[]{:S(2)}, u32[]{:S(2)}) collective-permute-start(bf16[128,4096]{1,0:T(8,128)(2,1)S(1)} %get-tuple-element.108.a0), channel_id=1, source_target_pairs={{0,1},{1,2},{2,3},{3,0},{4,5},{5,6},{6,7},{7,4},{8,9},{9,10},{10,1... | collective-permute-start | bytes 3145736 | tf_op jit(solution)/shard_map/ppermute | solution.py:30
  16.1 14.0 %all-to-all-start = ((bf16[4,512,128]{2,1,0:T(8,128)(2,1)}), bf16[4,512,128]{2,1,0:T(8,128)(2,1)S(1)}, u32[]{:S(2)}, u32[]{:S(2)}) async-start(bf16[4,512,128]{2,1,0:T(8,128)(2,1)} %bitcast.2), calls=%async_computation | async-start | bytes 1048576 | tf_op jit(solution)/shard_map/all_to_all | solution.py:392
  21.1 200.4 %reduce-scatter.2.cloned.1.call-start = ((), (), s32[]{:S(2)}) async-start(), calls=%async_computation.2 | async-start | bytes 10485760 | tf_op jit(solution)/shard_map/reduce_scatter | solution.py:420
  21.1 4.2 %copy-start.20 = (f32[128,64]{0,1:T(8,128)S(1)}, f32[128,64]{0,1:T(8,128)}, u32[]{:S(2)}) copy-start(f32[128,64]{0,1:T(8,128)} %param.9) | copy-start | bytes 98308
  30.1 15.5 %copy-start.7 = (bf16[4,512,128]{2,1,0:T(8,128)(2,1)}, bf16[4,512,128]{2,1,0:T(8,128)(2,1)S(1)}, u32[]{:S(2)}) copy-start(bf16[4,512,128]{2,1,0:T(8,128)(2,1)S(1)} %all-to-all-done.cots) | copy-start | bytes 1572868
  37.9 19.7 %copy-start.19 = (bf16[128,4096]{1,0:T(8,128)(2,1)}, bf16[128,4096]{1,0:T(8,128)(2,1)S(1)}, u32[]{:S(2)}) copy-start(bf16[128,4096]{1,0:T(8,128)(2,1)S(1)} %collective-permute-done.1.a1) | copy-start | bytes 3145732
  42.2 12.9 %collective-permute-start.2 = (bf16[64,4096]{1,0:T(8,128)(2,1)S(1)}, bf16[64,4096]{1,0:T(8,128)(2,1)S(1)}, u32[]{:S(2)}, u32[]{:S(2)}) collective-permute-start(bf16[64,4096]{1,0:T(8,128)(2,1)S(1)} %slice.58), channel_id=1, source_target_pairs={{0,1},{1,2},{2,3},{3,0},{4,5},{5,6},{6,7},{7,4},{8,9},{9,10},{10,1... | collective-permute-start | bytes 1572872 | tf_op jit(solution)/shard_map/ppermute | solution.py:30
  42.3 12.9 %collective-permute-start.3 = (bf16[64,4096]{1,0:T(8,128)(2,1)S(1)}, bf16[64,4096]{1,0:T(8,128)(2,1)}, u32[]{:S(2)}, u32[]{:S(2)}) collective-permute-start(bf16[64,4096]{1,0:T(8,128)(2,1)S(1)} %slice.59), channel_id=1, source_target_pairs={{0,3},{1,0},{2,1},{3,2},{4,7},{5,4},{6,5},{7,6},{8,11},{9,8},{10,9... | collective-permute-start | bytes 1572872 | tf_op jit(solution)/shard_map/ppermute | solution.py:30
  55.2 2.4 %copy-start.21 = (bf16[64,4096]{1,0:T(8,128)(2,1)}, bf16[64,4096]{1,0:T(8,128)(2,1)S(1)}, u32[]{:S(2)}) copy-start(bf16[64,4096]{1,0:T(8,128)(2,1)S(1)} %collective-permute-done.2.a2lo) | copy-start | bytes 1572868
  55.2 22.3 %collective-permute-start.5 = (bf16[128,4096]{1,0:T(8,128)(2,1)}, bf16[128,4096]{1,0:T(8,128)(2,1)}, u32[]{:S(2)}, u32[]{:S(2)}) collective-permute-start(bf16[128,4096]{1,0:T(8,128)(2,1)} %get-tuple-element.69.a0), channel_id=1, source_target_pairs={{0,3},{1,0},{2,1},{3,2},{4,7},{5,4},{6,5},{7,6},{8,11},{9,8},{10,9... | collective-permute-start | bytes 3145736 | tf_op jit(solution)/shard_map/ppermute | solution.py:30
  57.6 22.8 %collective-permute-start.4 = (bf16[128,4096]{1,0:T(8,128)(2,1)}, bf16[128,4096]{1,0:T(8,128)(2,1)}, u32[]{:S(2)}, u32[]{:S(2)}) collective-permute-start(bf16[128,4096]{1,0:T(8,128)(2,1)} %get-tuple-element.69.a0), channel_id=1, source_target_pairs={{0,1},{1,2},{2,3},{3,0},{4,5},{5,6},{6,7},{7,4},{8,9},{9,10},{10,1... | collective-permute-start | bytes 3145736 | tf_op jit(solution)/shard_map/ppermute | solution.py:30
  64.0 37.2 %copy-start.12 = (bf16[256,2048]{1,0:T(8,128)(2,1)S(1)}, bf16[256,2048]{1,0:T(8,128)(2,1)}, u32[]{:S(2)}) copy-start(bf16[256,2048]{1,0:T(8,128)(2,1)} %get-tuple-element.66) | copy-start | bytes 3145732
  64.0 23.2 %collective-permute-start.7 = (bf16[256,2048]{1,0:T(8,128)(2,1)}, bf16[256,2048]{1,0:T(8,128)(2,1)S(1)}, u32[]{:S(2)}, u32[]{:S(2)}) collective-permute-start(bf16[256,2048]{1,0:T(8,128)(2,1)} %get-tuple-element.63), channel_id=1, source_target_pairs={{0,12},{1,13},{2,14},{3,15},{4,0},{5,1},{6,2},{7,3},{8,4},{9,5},{1... | collective-permute-start | bytes 3145736 | tf_op jit(solution)/shard_map/ppermute | solution.py:30
  67.8 22.4 %collective-permute-start.6 = (bf16[256,2048]{1,0:T(8,128)(2,1)}, bf16[256,2048]{1,0:T(8,128)(2,1)S(1)}, u32[]{:S(2)}, u32[]{:S(2)}) collective-permute-start(bf16[256,2048]{1,0:T(8,128)(2,1)} %get-tuple-element.60), channel_id=1, source_target_pairs={{0,4},{1,5},{2,6},{3,7},{4,8},{5,9},{6,10},{7,11},{8,12},{9,13},{1... | collective-permute-start | bytes 3145736 | tf_op jit(solution)/shard_map/ppermute | solution.py:30
  87.2 15.4 %copy-start.8 = (bf16[256,2048]{1,0:T(8,128)(2,1)}, bf16[256,2048]{1,0:T(8,128)(2,1)S(1)}, u32[]{:S(2)}) copy-start(bf16[256,2048]{1,0:T(8,128)(2,1)S(1)} %collective-permute-done.7.pl_lo) | copy-start | bytes 3145732
  90.2 12.4 %copy-start.9 = (bf16[256,2048]{1,0:T(8,128)(2,1)}, bf16[256,2048]{1,0:T(8,128)(2,1)S(1)}, u32[]{:S(2)}) copy-start(bf16[256,2048]{1,0:T(8,128)(2,1)S(1)} %collective-permute-done.6.pl_hi) | copy-start | bytes 3145732
  90.2 13.8 %collective-permute-start.12 = (bf16[4,4096,128]{2,1,0:T(8,128)(2,1)}, bf16[4,4096,128]{2,1,0:T(8,128)(2,1)}, u32[]{:S(2)}, u32[]{:S(2)}) collective-permute-start(bf16[4,4096,128]{2,1,0:T(8,128)(2,1)} %bitcast.11), channel_id=1, source_target_pairs={{0,16},{16,0},{32,48},{48,32},{64,80},{80,64},{96,112},{112,96},{1... | collective-permute-start | bytes 12582920 | tf_op jit(solution)/shard_map/ppermute | solution.py:39
  98.5 17.8 %collective-permute-start.8 = (bf16[64,4096]{1,0:T(8,128)(2,1)}, bf16[64,4096]{1,0:T(8,128)(2,1)}, u32[]{:S(2)}, u32[]{:S(2)}) collective-permute-start(bf16[64,4096]{1,0:T(8,128)(2,1)} %slice.60), channel_id=1, source_target_pairs={{0,1},{1,2},{2,3},{3,0},{4,5},{5,6},{6,7},{7,4},{8,9},{9,10},{10,1... | collective-permute-start | bytes 1572872 | tf_op jit(solution)/shard_map/ppermute | solution.py:30
  98.5 17.8 %collective-permute-start.9 = (bf16[64,4096]{1,0:T(8,128)(2,1)}, bf16[64,4096]{1,0:T(8,128)(2,1)}, u32[]{:S(2)}, u32[]{:S(2)}) collective-permute-start(bf16[64,4096]{1,0:T(8,128)(2,1)} %slice.61), channel_id=1, source_target_pairs={{0,3},{1,0},{2,1},{3,2},{4,7},{5,4},{6,5},{7,6},{8,11},{9,8},{10,9... | collective-permute-start | bytes 1572872 | tf_op jit(solution)/shard_map/ppermute | solution.py:30
  102.6 13.7 %collective-permute-start.11 = (bf16[128,2048]{1,0:T(8,128)(2,1)}, bf16[128,2048]{1,0:T(8,128)(2,1)S(1)}, u32[]{:S(2)}, u32[]{:S(2)}) collective-permute-start(bf16[128,2048]{1,0:T(8,128)(2,1)} %get-tuple-element.112), channel_id=1, source_target_pairs={{0,12},{1,13},{2,14},{3,15},{4,0},{5,1},{6,2},{7,3},{8,4},{9,5},{1... | collective-permute-start | bytes 1572872 | tf_op jit(solution)/shard_map/ppermute | solution.py:30
  102.7 13.6 %collective-permute-start.10 = (bf16[128,2048]{1,0:T(8,128)(2,1)}, bf16[128,2048]{1,0:T(8,128)(2,1)S(1)}, u32[]{:S(2)}, u32[]{:S(2)}) collective-permute-start(bf16[128,2048]{1,0:T(8,128)(2,1)} %get-tuple-element.113), channel_id=1, source_target_pairs={{0,4},{1,5},{2,6},{3,7},{4,8},{5,9},{6,10},{7,11},{8,12},{9,13},{1... | collective-permute-start | bytes 1572872 | tf_op jit(solution)/shard_map/ppermute | solution.py:30
  116.3 6.7 %copy-start.15 = (bf16[128,2048]{1,0:T(8,128)(2,1)}, bf16[128,2048]{1,0:T(8,128)(2,1)S(1)}, u32[]{:S(2)}) copy-start(bf16[128,2048]{1,0:T(8,128)(2,1)S(1)} %collective-permute-done.11.su_hi) | copy-start | bytes 1572868
  116.3 6.7 %copy-start.16 = (bf16[128,2048]{1,0:T(8,128)(2,1)}, bf16[128,2048]{1,0:T(8,128)(2,1)S(1)}, u32[]{:S(2)}) copy-start(bf16[128,2048]{1,0:T(8,128)(2,1)S(1)} %collective-permute-done.10.su_lo) | copy-start | bytes 1572868
  123.0 25.9 %copy-start.13 = (bf16[256,2048]{1,0:T(8,128)(2,1)S(1)}, bf16[256,2048]{1,0:T(8,128)(2,1)}, u32[]{:S(2)}) copy-start(bf16[256,2048]{1,0:T(8,128)(2,1)} %get-tuple-element.79) | copy-start | bytes 3145732
  123.0 23.1 %collective-permute-start.14 = (bf16[256,2048]{1,0:T(8,128)(2,1)}, bf16[256,2048]{1,0:T(8,128)(2,1)S(1)}, u32[]{:S(2)}, u32[]{:S(2)}) collective-permute-start(bf16[256,2048]{1,0:T(8,128)(2,1)} %get-tuple-element.78), channel_id=1, source_target_pairs={{0,12},{1,13},{2,14},{3,15},{4,0},{5,1},{6,2},{7,3},{8,4},{9,5},{1... | collective-permute-start | bytes 3145736 | tf_op jit(solution)/shard_map/ppermute | solution.py:30
  124.4 24.4 %collective-permute-start.13 = (bf16[256,2048]{1,0:T(8,128)(2,1)}, bf16[256,2048]{1,0:T(8,128)(2,1)S(1)}, u32[]{:S(2)}, u32[]{:S(2)}) collective-permute-start(bf16[256,2048]{1,0:T(8,128)(2,1)} %get-tuple-element.74), channel_id=1, source_target_pairs={{0,4},{1,5},{2,6},{3,7},{4,8},{5,9},{6,10},{7,11},{8,12},{9,13},{1... | collective-permute-start | bytes 3145736 | tf_op jit(solution)/shard_map/ppermute | solution.py:30
  146.1 10.6 %copy-start.10 = (bf16[256,2048]{1,0:T(8,128)(2,1)}, bf16[256,2048]{1,0:T(8,128)(2,1)S(1)}, u32[]{:S(2)}) copy-start(bf16[256,2048]{1,0:T(8,128)(2,1)S(1)} %collective-permute-done.14.pl_lo) | copy-start | bytes 3145732
  148.8 7.8 %copy-start.11 = (bf16[256,2048]{1,0:T(8,128)(2,1)}, bf16[256,2048]{1,0:T(8,128)(2,1)S(1)}, u32[]{:S(2)}) copy-start(bf16[256,2048]{1,0:T(8,128)(2,1)S(1)} %collective-permute-done.13.pl_hi) | copy-start | bytes 3145732
  150.2 11.2 %collective-permute-start.16 = (bf16[128,2048]{1,0:T(8,128)(2,1)}, bf16[128,2048]{1,0:T(8,128)(2,1)S(1)}, u32[]{:S(2)}, u32[]{:S(2)}) collective-permute-start(bf16[128,2048]{1,0:T(8,128)(2,1)} %get-tuple-element.110), channel_id=1, source_target_pairs={{0,12},{1,13},{2,14},{3,15},{4,0},{5,1},{6,2},{7,3},{8,4},{9,5},{1... | collective-permute-start | bytes 1572872 | tf_op jit(solution)/shard_map/ppermute | solution.py:30
  150.7 12.4 %collective-permute-start.15 = (bf16[128,2048]{1,0:T(8,128)(2,1)}, bf16[128,2048]{1,0:T(8,128)(2,1)S(1)}, u32[]{:S(2)}, u32[]{:S(2)}) collective-permute-start(bf16[128,2048]{1,0:T(8,128)(2,1)} %get-tuple-element.111), channel_id=1, source_target_pairs={{0,4},{1,5},{2,6},{3,7},{4,8},{5,9},{6,10},{7,11},{8,12},{9,13},{1... | collective-permute-start | bytes 1572872 | tf_op jit(solution)/shard_map/ppermute | solution.py:30
  168.7 5.9 %collective-permute-start.17 = (f32[32,8192]{1,0:T(8,128)}, f32[32,8192]{1,0:T(8,128)S(1)}, u32[]{:S(2)}, u32[]{:S(2)}) collective-permute-start(f32[32,8192]{1,0:T(8,128)} %get-tuple-element.101), channel_id=1, source_target_pairs={{0,16},{16,0},{32,48},{48,32},{64,80},{80,64},{96,112},{112,96},{1... | collective-permute-start | bytes 3145736 | tf_op jit(solution)/shard_map/ppermute | solution.py:39
  176.0 7.7 %collective-permute-start.18 = (bf16[16,8192]{1,0:T(8,128)(2,1)S(1)}, bf16[16,8192]{1,0:T(8,128)(2,1)S(1)}, u32[]{:S(2)}, u32[]{:S(2)}) collective-permute-start(bf16[16,8192]{1,0:T(8,128)(2,1)S(1)} %get-tuple-element.116), channel_id=1, source_target_pairs={{0,32},{16,48},{32,0},{48,16},{64,96},{80,112},{96,64},{112,80},{1... | collective-permute-start | bytes 786440 | tf_op jit(solution)/shard_map/ppermute | solution.py:39
  177.3 8.5 %collective-permute-start.20 = (bf16[16,8192]{1,0:T(8,128)(2,1)S(1)}, bf16[16,8192]{1,0:T(8,128)(2,1)S(1)}, u32[]{:S(2)}, u32[]{:S(2)}) collective-permute-start(bf16[16,8192]{1,0:T(8,128)(2,1)S(1)} %get-tuple-element.117), channel_id=1, source_target_pairs={{0,96},{16,112},{32,64},{48,80},{64,32},{80,48},{96,0},{112,16},{1... | collective-permute-start | bytes 786440 | tf_op jit(solution)/shard_map/ppermute | solution.py:39
  185.9 7.8 %collective-permute-start.19 = (bf16[16,8192]{1,0:T(8,128)(2,1)S(1)}, bf16[16,8192]{1,0:T(8,128)(2,1)S(1)}, u32[]{:S(2)}, u32[]{:S(2)}) collective-permute-start(bf16[16,8192]{1,0:T(8,128)(2,1)S(1)} %get-tuple-element.114), channel_id=1, source_target_pairs={{0,96},{16,112},{32,64},{48,80},{64,32},{80,48},{96,0},{112,16},{1... | collective-permute-start | bytes 786440 | tf_op jit(solution)/shard_map/ppermute | solution.py:39
  187.8 11.3 %copy-start.2 = (f32[128,8192]{1,0:T(8,128)S(1)}, f32[128,8192]{1,0:T(8,128)}, u32[]{:S(2)}) copy-start(f32[128,8192]{1,0:T(8,128)} %get-tuple-element.102.merged.refs_5_) | copy-start | bytes 12582916
  187.8 11.3 %copy-start.5 = (s32[3]{0:T(128)S(1)}, s32[3]{0:T(128)}, u32[]{:S(2)}) copy-start(s32[3]{0:T(128)} %pad_add_fusion.spots.refs_0_) | copy-start | bytes 40
  187.8 6.2 %collective-permute-start.21 = (bf16[16,8192]{1,0:T(8,128)(2,1)S(1)}, bf16[16,8192]{1,0:T(8,128)(2,1)S(1)}, u32[]{:S(2)}, u32[]{:S(2)}) collective-permute-start(bf16[16,8192]{1,0:T(8,128)(2,1)S(1)} %get-tuple-element.115), channel_id=1, source_target_pairs={{0,32},{16,48},{32,0},{48,16},{64,96},{80,112},{96,64},{112,80},{1... | collective-permute-start | bytes 786440 | tf_op jit(solution)/shard_map/ppermute | solution.py:39
  194.2 8.6 %copy-start.3 = (f32[32,8192]{1,0:T(8,128)}, f32[32,8192]{1,0:T(8,128)S(1)}, u32[]{:S(2)}) copy-start(f32[32,8192]{1,0:T(8,128)S(1)} %pad_maximum_fusion.mine.refs_3_) | copy-start | bytes 3145732
  194.2 4.9 %collective-permute-start.22 = (f32[32,8192]{1,0:T(8,128)S(1)}, f32[32,8192]{1,0:T(8,128)S(1)}, u32[]{:S(2)}, u32[]{:S(2)}) collective-permute-start(f32[32,8192]{1,0:T(8,128)S(1)} %pad_maximum_fusion.mine.refs_3_), channel_id=1, source_target_pairs={{0,16},{16,0},{32,48},{48,32},{64,80},{80,64},{96,112},{112,96},{1... | collective-permute-start | bytes 3145736 | tf_op jit(solution)/shard_map/ppermute | solution.py:39
  199.1 3.7 %copy-start.4 = (f32[32,8192]{1,0:T(8,128)}, f32[32,8192]{1,0:T(8,128)S(1)}, u32[]{:S(2)}) copy-start(f32[32,8192]{1,0:T(8,128)S(1)} %collective-permute-done.22.theirs.refs_4_) | copy-start | bytes 3145732
  202.8 1.4 collective-permute-start.23
  204.2 9.4 %collective-permute-start.26 = (f32[128,64]{1,0:T(8,128)S(1)}, f32[128,64]{1,0:T(8,128)S(1)}, u32[]{:S(2)}, u32[]{:S(2)}) collective-permute-start(f32[128,64]{1,0:T(8,128)S(1)} %add.64), channel_id=1, source_target_pairs={{0,96},{16,112},{32,0},{48,16},{64,32},{80,48},{96,64},{112,80},{1... | collective-permute-start | bytes 98312 | tf_op jit(solution)/shard_map/ppermute | solution.py:39
  205.5 8.1 %collective-permute-start.25 = (f32[128,64]{1,0:T(8,128)S(1)}, f32[128,64]{1,0:T(8,128)S(1)}, u32[]{:S(2)}, u32[]{:S(2)}) collective-permute-start(f32[128,64]{1,0:T(8,128)S(1)} %add.64), channel_id=1, source_target_pairs={{0,32},{16,48},{32,64},{48,80},{64,96},{80,112},{96,0},{112,16},{1... | collective-permute-start | bytes 98312 | tf_op jit(solution)/shard_map/ppermute | solution.py:39
  205.7 7.9 %collective-permute-start.24 = (f32[128,64]{1,0:T(8,128)S(1)}, f32[128,64]{1,0:T(8,128)S(1)}, u32[]{:S(2)}, u32[]{:S(2)}) collective-permute-start(f32[128,64]{1,0:T(8,128)S(1)} %add.64), channel_id=1, source_target_pairs={{0,64},{16,80},{32,96},{48,112},{64,0},{80,16},{96,32},{112,48},{1... | collective-permute-start | bytes 98312 | tf_op jit(solution)/shard_map/ppermute | solution.py:39
  213.6 7.9 %copy-start.1 = (bf16[8192,128]{1,0:T(8,128)(2,1)S(1)}, bf16[8192,128]{1,0:T(8,128)(2,1)}, u32[]{:S(2)}) copy-start(bf16[8192,128]{1,0:T(8,128)(2,1)} %param.7) | copy-start | bytes 6291460
  (4 other events, 5.6 us)
Sparse Core Ops, SparseCore 0:
  10.3 54.8 all-gather.2
  123.1 79.8 reduce-scatter.1
where the time goes:
time: 230 us; the launch traced here: 228 us
  waiting for transfers between devices  94.4 us (41%)
  Pallas kernels  54.8 us (24%)
  starting transfers between devices  43.3 us (19%)
  local copies, waits for them, and re-layouts  15.2 us (7%)
  between operations  14.3 us (6%)
  other arithmetic  6.27 us (3%)
    ppermute x16, waiting for transfers between devices, along_tensor(): return lax.ppermute(array, 'tensor', perm)  71.7 us
    ppermute x16, starting transfers between devices, along_tensor(): return lax.ppermute(array, 'tensor', perm)  19.6 us
    ppermute x11, starting transfers between devices, along_dp(): return lax.ppermute(array, 'dp', perm)  18.6 us
    ppermute x11, waiting for transfers between devices, along_dp(): return lax.ppermute(array, 'dp', perm)  18.5 us
    pallas_call x2, Pallas kernels, grad_parts(): pl.pallas_call(grad_kernel, grid=(width // TILE,), in_specs=[cols_spec(pi...  13 us
    pallas_call x1, Pallas kernels, input_parts(): pl.pallas_call(input_kernel, grid_spec=pltpu.PrefetchScalarGridSpec(num_s...  12.2 us
    pallas_call x2, Pallas kernels, merge(): pl.pallas_call(merge_kernel, grid=(steps,), in_specs=[shifted(HD), cols_s...  9.79 us
    pallas_call x1, Pallas kernels, final(): pl.pallas_call(lambda *refs: final_kernel(replicas, *refs), grid=(width /...  7.23 us
  transfers between devices with their start and end apart: 30, of which 19 were waited for; matrix products, arithmetic and copies ran while one was open for 8% of the time, Pallas kernels for 21%

commit v1 on v0

--- a/solution.py
+++ b/solution.py
@@ -93,15 +93,33 @@
     )(spots, cots)
 
 
-def grad_kernel(a0, a1, a2lo, a2hi, a3, cturn, own, up, down, rest):
+def own_kernel(a0, a1, a2lo, a2hi, a3, cturn, own):
+    tokens = jnp.concatenate([a0[...], a1[...], a2lo[...], a2hi[...], a3[...]], axis=0)
+    own[...] = lax.dot_general(cturn[:HD], tokens, NN, preferred_element_type=F32)
+
+
+def own_part(pieces, cturn):
+    rows, width = pieces[0].shape
+    flat = SIDE * rows
+    return pl.pallas_call(
+        own_kernel,
+        grid=(width // TILE,),
+        in_specs=[cols_spec(piece.shape[0], TILE) for piece in pieces] + [whole_spec(HD, flat)],
+        out_specs=cols_spec(HD, TILE),
+        out_shape=jax.ShapeDtypeStruct((HD, width), F32),
+        cost_estimate=cost(2 * width * flat * HD, 12 * width * HD),
+        name="own_part",
+    )(*pieces, cturn)
+
+
+def grad_kernel(a0, a1, a2lo, a2hi, a3, cturn, up, down, rest):
     j = pl.program_id(0)
     mid = pl.num_programs(0) // 2
     tokens = jnp.concatenate([a0[...], a1[...], a2lo[...], a2hi[...], a3[...]], axis=0)
-    grads = lax.dot_general(cturn[...], tokens, NN, preferred_element_type=F32)
-    own[...] = grads[:HD]
-    ahead = grads[HD : 2 * HD].astype(BF16)
-    across = grads[2 * HD : 3 * HD].astype(BF16)
-    behind = grads[3 * HD :].astype(BF16)
+    grads = lax.dot_general(cturn[HD:], tokens, NN, preferred_element_type=F32)
+    ahead = grads[:HD].astype(BF16)
+    across = grads[HD : 2 * HD].astype(BF16)
+    behind = grads[2 * HD :].astype(BF16)
 
     @pl.when(j < mid)
     def _():
@@ -126,9 +144,8 @@
         grid=(width // TILE,),
         in_specs=[cols_spec(piece.shape[0], TILE) for piece in pieces]
         + [whole_spec(SIDE * HD, flat)],
-        out_specs=[cols_spec(HD, TILE)] + [stacked] * 3,
-        out_shape=[jax.ShapeDtypeStruct((HD, width), F32)]
-        + [jax.ShapeDtypeStruct((2 * HD, width // 2), BF16)] * 3,
+        out_specs=[stacked] * 3,
+        out_shape=[jax.ShapeDtypeStruct((2 * HD, width // 2), BF16)] * 3,
         cost_estimate=cost(2 * width * SIDE * flat * HD, 9 * width * HD * 2),
         name="grad_parts",
     )(*pieces, cturn)
@@ -404,7 +421,8 @@
     cturn = turn_cots(spots, cots)
     pieces = gather_line(blocks[0], *near, to_pass_on(*near), in_y)
     near = neighbours(tied(blocks[1], pieces), in_y)
-    own_a, up, down, rest_a = grad_parts(pieces, cturn)
+    up, down, rest_a = grad_parts(pieces, cturn)
+    pieces_a = pieces
     got_a = scatter_near(up, down, in_z)
     near, up = lax.optimization_barrier((near, up))
     passed = tied(to_pass_on(*near), got_a)
@@ -415,12 +433,15 @@
     sums_a = scatter_far(*got_a, rest_a, in_z)
 
     pieces, sums_a, shares = lax.optimization_barrier((pieces, sums_a, shares))
-    own_b, up, down, rest_b = grad_parts(pieces, cturn)
+    up, down, rest_b = grad_parts(pieces, cturn)
+    later, up = lax.optimization_barrier(((pieces_a, pieces), up))
+    own_a, own_b = own_part(later[0], cturn), own_part(later[1], cturn)
     got_b = scatter_near(up, down, in_z)
     input_grad = lax.psum_scatter(
         tied(shares, up), "tensor", scatter_dimension=0, axis_index_groups=lines_y, tiled=True
     )
 
+    got_b, own_a, own_b = lax.optimization_barrier((got_b, own_a, own_b))
     left = merge(fb_turned, own_a, tied(sums_a, got_b), qrows, 0, ())
     sums_b = scatter_far(*got_b, rest_b, in_z)
     sums_b, left = lax.optimization_barrier((sums_b, left))

time: 230 us -> 225 us (0.978)
  waiting for transfers between devices: 94.4 us -> 78.1 us
  Pallas kernels: 54.8 us -> 60.6 us
  starting transfers between devices: 43.3 us -> 47.9 us
    ppermute x16, waiting for transfers between devices: 71.7 us -> 56.4 us  [along_tensor(): return lax.ppermute(array, 'tensor', perm)]
    pallas_call x0 -> x2, Pallas kernels: none -> 8.02 us  [own_part(): pl.pallas_call(own_kernel, grid=(width // TILE,), in_specs=[cols_spec(pie...]
    ppermute x16, starting transfers between devices: 19.6 us -> 24.5 us  [along_tensor(): return lax.ppermute(array, 'tensor', perm)]
    unnamed x45 -> x49, local copies, waits for them, and re-layouts: 6.61 us -> 8.34 us
  transfers between devices with their start and end apart: 30 -> 30, of which waited for: 19 -> 14; matrix products, arithmetic and copies ran while one was open for 8% -> 8% of each run, Pallas kernels for 21% -> 25%
where the time goes in v1:
time: 225 us
  waiting for transfers between devices  78.1 us (35%)
  Pallas kernels  60.6 us (27%)
  starting transfers between devices  47.9 us (21%)
  local copies, waits for them, and re-layouts  17 us (8%)
  between operations  14.3 us (6%)
  other arithmetic  6.56 us (3%)
    ppermute x16, waiting for transfers between devices, along_tensor(): return lax.ppermute(array, 'tensor', perm)  56.4 us
    ppermute x16, starting transfers between devices, along_tensor(): return lax.ppermute(array, 'tensor', perm)  24.5 us
    ppermute x11, waiting for transfers between devices, along_dp(): return lax.ppermute(array, 'dp', perm)  18.6 us
    ppermute x11, starting transfers between devices, along_dp(): return lax.ppermute(array, 'dp', perm)  18.4 us
    pallas_call x1, Pallas kernels, input_parts(): pl.pallas_call(input_kernel, grid_spec=pltpu.PrefetchScalarGridSpec(num_s...  12.2 us
    pallas_call x2, Pallas kernels, grad_parts(): pl.pallas_call(grad_kernel, grid=(width // TILE,), in_specs=[cols_spec(pi...  10.8 us
    pallas_call x2, Pallas kernels, merge(): pl.pallas_call(merge_kernel, grid=(steps,), in_specs=[shifted(HD), cols_s...  9.92 us
    unnamed x49, local copies, waits for them, and re-layouts  8.34 us
  transfers between devices with their start and end apart: 30, of which 14 were waited for; matrix products, arithmetic and copies ran while one was open for 8% of the time, Pallas kernels for 25%

profile of v1, /device:TPU:1, one launch (start us, length us, event | category | flops | bytes accessed | tf_op | source)
XLA Modules:
  0.0 224.5 jit_solution(2641084256080195707)
XLA Ops:
  7.2 1.5 copy-done
  9.8 1.7 fusion
  11.6 2.2 collective-permute-start
  13.8 1.5 collective-permute-start.1
  15.3 5.0 %all-to-all-start = ((bf16[4,512,128]{2,1,0:T(8,128)(2,1)}), bf16[4,512,128]{2,1,0:T(8,128)(2,1)S(1)}, u32[]{:S(2)}, u32[]{:S(2)}) async-start(bf16[4,512,128]{2,1,0:T(8,128)(2,1)} %bitcast.2), calls=%async_computation | async-start | bytes 1048576 | tf_op jit(solution)/shard_map/all_to_all | solution.py:409
  20.3 4.1 %copy.12 = bf16[8192,128]{0,1:T(8,128)(2,1)} copy(bf16[8192,128]{1,0:T(8,128)(2,1)} %param.8) | data formatting | bytes 4194304 | tf_op args[3]
  25.1 3.1 %all-to-all-done.cots = bf16[4,512,128]{2,1,0:T(8,128)(2,1)S(1)} async-done(((bf16[4,512,128]{2,1,0:T(8,128)(2,1)}), bf16[4,512,128]{2,1,0:T(8,128)(2,1)S(1)}, u32[]{:S(2)}, u32[]{:S(2)}) %all-to-all-start) | async-done | bytes 524320 | tf_op jit(solution)/shard_map/all_to_all | solution.py:409
  28.2 9.9 %collective-permute-done.a3 = bf16[128,4096]{1,0:T(8,128)(2,1)} collective-permute-done((bf16[128,4096]{1,0:T(8,128)(2,1)S(1)}, bf16[128,4096]{1,0:T(8,128)(2,1)}, u32[]{:S(2)}, u32[]{:S(2)}) %collective-permute-start) | collective-permute-done | bytes 1048608 | tf_op jit(solution)/shard_map/ppermute | solution.py:30
  41.1 1.9 collective-permute-start.3
  43.7 2.0 turn_cots.1.cturn
  45.7 6.8 %collective-permute-done.2.a2lo = bf16[64,4096]{1,0:T(8,128)(2,1)S(1)} collective-permute-done((bf16[64,4096]{1,0:T(8,128)(2,1)S(1)}, bf16[64,4096]{1,0:T(8,128)(2,1)S(1)}, u32[]{:S(2)}, u32[]{:S(2)}) %collective-permute-start.2) | collective-permute-done | bytes 524320 | tf_op jit(solution)/shard_map/ppermute | solution.py:30
  53.7 2.4 %collective-permute-start.5 = (bf16[128,4096]{1,0:T(8,128)(2,1)S(1)}, bf16[128,4096]{1,0:T(8,128)(2,1)}, u32[]{:S(2)}, u32[]{:S(2)}) collective-permute-start(bf16[128,4096]{1,0:T(8,128)(2,1)S(1)} %get-tuple-element.97.a0), channel_id=1, source_target_pairs={{0,3},{1,0},{2,1},{3,2},{4,7},{5,4},{6,5},{7,6},{8,11},{9,8},{10,9... | collective-permute-start | bytes 3145736 | tf_op jit(solution)/shard_map/ppermute | solution.py:30
  56.1 5.4 %grad_parts.2 = (bf16[256,2048]{1,0:T(8,128)(2,1)}, bf16[256,2048]{1,0:T(8,128)(2,1)}, bf16[256,2048]{1,0:T(8,128)(2,1)}) custom-call(bf16[128,4096]{1,0:T(8,128)(2,1)} %copy-done.8, bf16[128,4096]{1,0:T(8,128)(2,1)} %collective-permute-done.1.a1, bf16[64,4096]{1,0:T(8,128)(2,1)} %copy-done.18, bf16[64,4096]{1,0:T(8,128)(2,1)} %collective-permute-done.3.a2hi, ...), custom_call_target="tpu_custom_call" | custom-call | flops 2147483648 | bytes 9437184 | tf_op jit(solution)/shard_map/grad_parts/pallas_call | solution.py:142
  61.5 1.4 collective-permute-start.6
  62.9 2.2 collective-permute-start.7
  65.1 12.0 %collective-permute-done.4.a3 = bf16[128,4096]{1,0:T(8,128)(2,1)} collective-permute-done((bf16[128,4096]{1,0:T(8,128)(2,1)S(1)}, bf16[128,4096]{1,0:T(8,128)(2,1)}, u32[]{:S(2)}, u32[]{:S(2)}) %collective-permute-start.4) | collective-permute-done | bytes 1048608 | tf_op jit(solution)/shard_map/ppermute | solution.py:30
  77.1 8.6 %collective-permute-done.6.pl_hi = bf16[256,2048]{1,0:T(8,128)(2,1)S(1)} collective-permute-done((bf16[256,2048]{1,0:T(8,128)(2,1)}, bf16[256,2048]{1,0:T(8,128)(2,1)S(1)}, u32[]{:S(2)}, u32[]{:S(2)}) %collective-permute-start.6) | collective-permute-done | bytes 1048608 | tf_op jit(solution)/shard_map/ppermute | solution.py:30
  85.7 3.7 %collective-permute-start.12 = (bf16[4,4096,128]{2,1,0:T(8,128)(2,1)}, bf16[4,4096,128]{2,1,0:T(8,128)(2,1)}, u32[]{:S(2)}, u32[]{:S(2)}) collective-permute-start(bf16[4,4096,128]{2,1,0:T(8,128)(2,1)} %bitcast.11), channel_id=1, source_target_pairs={{0,16},{16,0},{32,48},{48,32},{64,80},{80,64},{96,112},{112,96},{1... | collective-permute-start | bytes 12582920 | tf_op jit(solution)/shard_map/ppermute | solution.py:39
  89.4 1.9 slice.60
  91.3 1.9 slice.61
  93.2 1.4 add_convert_fusion.3
  95.4 1.8 collective-permute-start.11
  97.3 2.7 %collective-permute-start.9 = (bf16[64,4096]{1,0:T(8,128)(2,1)}, bf16[64,4096]{1,0:T(8,128)(2,1)S(1)}, u32[]{:S(2)}, u32[]{:S(2)}) collective-permute-start(bf16[64,4096]{1,0:T(8,128)(2,1)} %slice.61), channel_id=1, source_target_pairs={{0,3},{1,0},{2,1},{3,2},{4,7},{5,4},{6,5},{7,6},{8,11},{9,8},{10,9... | collective-permute-start | bytes 1572872 | tf_op jit(solution)/shard_map/ppermute | solution.py:30
  100.0 12.2 %input_parts.1 = bf16[512,8192]{1,0:T(8,128)(2,1)} custom-call(s32[3]{0:T(128)} %pad_add_fusion.spots.refs_0_, bf16[4,4096,128]{2,1,0:T(8,128)(2,1)} %bitcast.12, bf16[4,4096,128]{2,1,0:T(8,128)(2,1)} %collective-permute-done.12.theirs, bf16[4,512,128]{2,1,0:T(8,128)(2,1)} %copy-done.7), custom_call_target="tpu_custom_call" | custom-call | flops 4294967296 | bytes 18874368 | tf_op jit(solution)/shard_map/input_parts/pallas_call | solution.py:172
  113.8 5.4 %grad_parts.3 = (bf16[256,2048]{1,0:T(8,128)(2,1)}, bf16[256,2048]{1,0:T(8,128)(2,1)}, bf16[256,2048]{1,0:T(8,128)(2,1)}) custom-call(bf16[128,4096]{1,0:T(8,128)(2,1)} %copy-done.9, bf16[128,4096]{1,0:T(8,128)(2,1)} %collective-permute-done.5.a1, bf16[64,4096]{1,0:T(8,128)(2,1)} %copy-done.19, bf16[64,4096]{1,0:T(8,128)(2,1)} %copy-done.20, ...), custom_call_target="tpu_custom_call" | custom-call | flops 2147483648 | bytes 9437184 | tf_op jit(solution)/shard_map/grad_parts/pallas_call | solution.py:142
  119.4 2.7 %collective-permute-start.14 = (bf16[256,2048]{1,0:T(8,128)(2,1)}, bf16[256,2048]{1,0:T(8,128)(2,1)S(1)}, u32[]{:S(2)}, u32[]{:S(2)}) collective-permute-start(bf16[256,2048]{1,0:T(8,128)(2,1)} %get-tuple-element.91), channel_id=1, source_target_pairs={{0,12},{1,13},{2,14},{3,15},{4,0},{5,1},{6,2},{7,3},{8,4},{9,5},{1... | collective-permute-start | bytes 3145736 | tf_op jit(solution)/shard_map/ppermute | solution.py:30
  122.0 3.7 %own_part.3.own = f32[128,4096]{1,0:T(8,128)} custom-call(bf16[128,4096]{1,0:T(8,128)(2,1)} %copy-done.9, bf16[128,4096]{1,0:T(8,128)(2,1)} %collective-permute-done.5.a1, bf16[64,4096]{1,0:T(8,128)(2,1)} %copy-done.19, bf16[64,4096]{1,0:T(8,128)(2,1)} %copy-done.20, bf16[128,4096]{1,0:T(8,128)(2,1)} %collective-permute-done.4.a3, ...), custom_call_target="tpu_custom_call" | custom-call | flops 536870912 | bytes 6291456 | tf_op jit(solution)/shard_map/own_part/pallas_call | solution.py:104
  125.7 4.3 %own_part.2.own = f32[128,4096]{1,0:T(8,128)} custom-call(bf16[128,4096]{1,0:T(8,128)(2,1)} %copy-done.8, bf16[128,4096]{1,0:T(8,128)(2,1)} %collective-permute-done.1.a1, bf16[64,4096]{1,0:T(8,128)(2,1)} %copy-done.18, bf16[64,4096]{1,0:T(8,128)(2,1)} %collective-permute-done.3.a2hi, bf16[128,4096]{1,0:T(8,128)(2,1)} %collective-permute-done.a3, ...), custom_call_target="tpu_custom_call" | custom-call | flops 536870912 | bytes 6291456 | tf_op jit(solution)/shard_map/own_part/pallas_call | solution.py:104
  130.0 14.0 %collective-permute-done.13.pl_hi = bf16[256,2048]{1,0:T(8,128)(2,1)S(1)} collective-permute-done((bf16[256,2048]{1,0:T(8,128)(2,1)}, bf16[256,2048]{1,0:T(8,128)(2,1)S(1)}, u32[]{:S(2)}, u32[]{:S(2)}) %collective-permute-start.13) | collective-permute-done | bytes 1048608 | tf_op jit(solution)/shard_map/ppermute | solution.py:30
  144.1 1.6 add_convert_fusion.1
  145.7 2.7 %collective-permute-start.16 = (bf16[128,2048]{1,0:T(8,128)(2,1)}, bf16[128,2048]{1,0:T(8,128)(2,1)S(1)}, u32[]{:S(2)}, u32[]{:S(2)}) collective-permute-start(bf16[128,2048]{1,0:T(8,128)(2,1)} %get-tuple-element.136), channel_id=1, source_target_pairs={{0,12},{1,13},{2,14},{3,15},{4,0},{5,1},{6,2},{7,3},{8,4},{9,5},{1... | collective-permute-start | bytes 1572872 | tf_op jit(solution)/shard_map/ppermute | solution.py:30
  148.4 5.0 %merge.2 = (f32[128,8192]{1,0:T(8,128)}, f32[32,8192]{1,0:T(8,128)}, f32[32,8192]{1,0:T(8,128)}) custom-call(bf16[128,8192]{1,0:T(8,128)(2,1)} %bitcast.9, f32[128,4096]{1,0:T(8,128)} %own_part.2.own, bf16[256,2048]{1,0:T(8,128)(2,1)} %copy-done.11, bf16[256,2048]{1,0:T(8,128)(2,1)} %copy-done.10, bf16[128,2048]{1,0:T(8,128)(2,1)} %copy-done.16, ...), custom_call_target="tpu_custom_call" | custom-call | flops 201326592 | bytes 7340032 | tf_op jit(solution)/shard_map/merge/pallas_call | solution.py:222
  153.3 5.0 %collective-permute-done.15.su_lo = bf16[128,2048]{1,0:T(8,128)(2,1)S(1)} collective-permute-done((bf16[128,2048]{1,0:T(8,128)(2,1)}, bf16[128,2048]{1,0:T(8,128)(2,1)S(1)}, u32[]{:S(2)}, u32[]{:S(2)}) %collective-permute-start.15) | collective-permute-done | bytes 524320 | tf_op jit(solution)/shard_map/ppermute | solution.py:30
  159.3 5.0 %merge.3 = (f32[128,8192]{1,0:T(8,128)}, f32[32,8192]{1,0:T(8,128)}, f32[32,8192]{1,0:T(8,128)}) custom-call(bf16[128,8192]{1,0:T(8,128)(2,1)} %bitcast.10, f32[128,4096]{1,0:T(8,128)} %own_part.3.own, bf16[256,2048]{1,0:T(8,128)(2,1)} %copy-done.13, bf16[256,2048]{1,0:T(8,128)(2,1)} %copy-done.12, ...), custom_call_target="tpu_custom_call", output_to_operand_aliasing={{0}: (7, {}), {1}: (8, {}), {2}: (9, {})} | custom-call | flops 201326592 | bytes 7340032 | tf_op jit(solution)/shard_map/merge/pallas_call | solution.py:222
  164.3 3.2 %collective-permute-start.17 = (f32[32,8192]{1,0:T(8,128)}, f32[32,8192]{1,0:T(8,128)S(1)}, u32[]{:S(2)}, u32[]{:S(2)}) collective-permute-start(f32[32,8192]{1,0:T(8,128)} %get-tuple-element.127), channel_id=1, source_target_pairs={{0,16},{16,0},{32,48},{48,32},{64,80},{80,64},{96,112},{112,96},{1... | collective-permute-start | bytes 3145736 | tf_op jit(solution)/shard_map/ppermute | solution.py:39
  167.5 2.5 %collective-permute-done.17 = f32[32,8192]{1,0:T(8,128)S(1)} collective-permute-done((f32[32,8192]{1,0:T(8,128)}, f32[32,8192]{1,0:T(8,128)S(1)}, u32[]{:S(2)}, u32[]{:S(2)}) %collective-permute-start.17) | collective-permute-done | bytes 1048608 | tf_op jit(solution)/shard_map/ppermute | solution.py:39
  170.0 1.3 add_convert_fusion
  172.7 1.8 collective-permute-start.20
  174.5 4.6 %collective-permute-done.18 = bf16[16,8192]{1,0:T(8,128)(2,1)S(1)} collective-permute-done((bf16[16,8192]{1,0:T(8,128)(2,1)S(1)}, bf16[16,8192]{1,0:T(8,128)(2,1)S(1)}, u32[]{:S(2)}, u32[]{:S(2)}) %collective-permute-start.18) | collective-permute-done | bytes 262176 | tf_op jit(solution)/shard_map/ppermute | solution.py:39
  179.1 2.1 collective-permute-done.20
  181.4 1.9 collective-permute-start.19
  183.3 5.9 %collective-permute-done.19 = bf16[16,8192]{1,0:T(8,128)(2,1)S(1)} collective-permute-done((bf16[16,8192]{1,0:T(8,128)(2,1)S(1)}, bf16[16,8192]{1,0:T(8,128)(2,1)S(1)}, u32[]{:S(2)}, u32[]{:S(2)}) %collective-permute-start.19) | collective-permute-done | bytes 262176 | tf_op jit(solution)/shard_map/ppermute | solution.py:39
  189.7 2.6 %collective-permute-start.22 = (f32[32,8192]{1,0:T(8,128)S(1)}, f32[32,8192]{1,0:T(8,128)S(1)}, u32[]{:S(2)}, u32[]{:S(2)}) collective-permute-start(f32[32,8192]{1,0:T(8,128)S(1)} %pad_maximum_fusion.mine.refs_3_), channel_id=1, source_target_pairs={{0,16},{16,0},{32,48},{48,32},{64,80},{80,64},{96,112},{112,96},{1... | collective-permute-start | bytes 3145736 | tf_op jit(solution)/shard_map/ppermute | solution.py:39
  192.2 2.3 %collective-permute-done.22.theirs.refs_4_ = f32[32,8192]{1,0:T(8,128)S(1)} collective-permute-done((f32[32,8192]{1,0:T(8,128)S(1)}, f32[32,8192]{1,0:T(8,128)S(1)}, u32[]{:S(2)}, u32[]{:S(2)}) %collective-permute-start.22) | collective-permute-done | bytes 1048608 | tf_op jit(solution)/shard_map/ppermute | solution.py:39
  194.5 3.7 %gram.1 = (f32[128,64]{1,0:T(8,128)S(1)}, f32[64,64]{1,0:T(8,128)S(1)}) custom-call(s32[3]{0:T(128)S(1)} %copy-done.5, f32[32,8192]{1,0:T(8,128)S(1)} %pad_maximum_fusion.mine.refs_3_, f32[32,8192]{1,0:T(8,128)S(1)} %collective-permute-done.22.theirs.refs_4_, f32[128,8192]{1,0:T(8,128)S(1)} %copy-done.2), custom_call_target="tpu_custom_call" | custom-call | flops 603979776 | bytes 6291456 | tf_op jit(solution)/shard_map/gram/pallas_call | solution.py:259
  201.6 1.4 collective-permute-start.26
  203.0 6.8 %inverse_factor.1.refs_1_ = f32[64,64]{1,0:T(8,128)} custom-call(f32[64,64]{1,0:T(8,128)} %copy-done.6), custom_call_target="tpu_custom_call" | custom-call | flops 104857600 | bytes 65536 | tf_op jit(solution)/shard_map/inverse_factor/pallas_call | solution.py:290
  210.4 7.2 %final.1 = (f32[64,128]{1,0:T(8,128)}, bf16[8192,128]{1,0:T(8,128)(2,1)}, bf16[8192,128]{1,0:T(8,128)(2,1)}) custom-call(s32[3]{0:T(128)} %pad_add_fusion.spots.refs_0_, f32[64,64]{1,0:T(8,128)} %inverse_factor.1.refs_1_, f32[128,64]{1,0:T(8,128)} %add_add_fusion.refs_2_, f32[32,8192]{1,0:T(8,128)} %copy-done.3, f32[32,8192]{1,0:T(8,128)} %copy-done.4, ...), custom_call_target="tpu_custom_call" | custom-call | flops 402653184 | bytes 12582912 | tf_op jit(solution)/shard_map/final/pallas_call | solution.py:316
  (93 shorter events, 16.2 us)
Async XLA Ops:
  7.2 78.5 %all-gather.3.cloned.1.call-start = ((), (), s32[]{:S(2)}) async-start(), calls=%async_computation.3 | async-start | bytes 5242880 | tf_op jit(solution)/shard_map/all_gather | solution.py:413
  11.6 12.9 %copy-start.8 = (bf16[128,4096]{1,0:T(8,128)(2,1)}, bf16[128,4096]{1,0:T(8,128)(2,1)S(1)}, u32[]{:S(2)}) copy-start(bf16[128,4096]{1,0:T(8,128)(2,1)S(1)} %get-tuple-element.92.a0) | copy-start | bytes 3145732
  11.6 42.2 %copy-start.9 = (bf16[128,4096]{1,0:T(8,128)(2,1)}, bf16[128,4096]{1,0:T(8,128)(2,1)S(1)}, u32[]{:S(2)}) copy-start(bf16[128,4096]{1,0:T(8,128)(2,1)S(1)} %get-tuple-element.97.a0) | copy-start | bytes 3145732
  11.6 26.5 %collective-permute-start = (bf16[128,4096]{1,0:T(8,128)(2,1)S(1)}, bf16[128,4096]{1,0:T(8,128)(2,1)}, u32[]{:S(2)}, u32[]{:S(2)}) collective-permute-start(bf16[128,4096]{1,0:T(8,128)(2,1)S(1)} %get-tuple-element.92.a0), channel_id=1, source_target_pairs={{0,1},{1,2},{2,3},{3,0},{4,5},{5,6},{6,7},{7,4},{8,9},{9,10},{10,1... | collective-permute-start | bytes 3145736 | tf_op jit(solution)/shard_map/ppermute | solution.py:30
  13.8 24.3 %collective-permute-start.1 = (bf16[128,4096]{1,0:T(8,128)(2,1)S(1)}, bf16[128,4096]{1,0:T(8,128)(2,1)}, u32[]{:S(2)}, u32[]{:S(2)}) collective-permute-start(bf16[128,4096]{1,0:T(8,128)(2,1)S(1)} %get-tuple-element.92.a0), channel_id=1, source_target_pairs={{0,3},{1,0},{2,1},{3,2},{4,7},{5,4},{6,5},{7,6},{8,11},{9,8},{10,9... | collective-permute-start | bytes 3145736 | tf_op jit(solution)/shard_map/ppermute | solution.py:30
  15.3 12.9 %all-to-all-start = ((bf16[4,512,128]{2,1,0:T(8,128)(2,1)}), bf16[4,512,128]{2,1,0:T(8,128)(2,1)S(1)}, u32[]{:S(2)}, u32[]{:S(2)}) async-start(bf16[4,512,128]{2,1,0:T(8,128)(2,1)} %bitcast.2), calls=%async_computation | async-start | bytes 1048576 | tf_op jit(solution)/shard_map/all_to_all | solution.py:409
  20.3 197.4 %reduce-scatter.2.cloned.1.call-start = ((), (), s32[]{:S(2)}) async-start(), calls=%async_computation.2 | async-start | bytes 10485760 | tf_op jit(solution)/shard_map/reduce_scatter | solution.py:440
  20.3 4.1 %copy-start.23 = (f32[128,64]{0,1:T(8,128)S(1)}, f32[128,64]{0,1:T(8,128)}, u32[]{:S(2)}) copy-start(f32[128,64]{0,1:T(8,128)} %param.9) | copy-start | bytes 98308
  28.2 15.5 %copy-start.7 = (bf16[4,512,128]{2,1,0:T(8,128)(2,1)}, bf16[4,512,128]{2,1,0:T(8,128)(2,1)S(1)}, u32[]{:S(2)}) copy-start(bf16[4,512,128]{2,1,0:T(8,128)(2,1)S(1)} %all-to-all-done.cots) | copy-start | bytes 1572868
  39.1 13.4 %collective-permute-start.2 = (bf16[64,4096]{1,0:T(8,128)(2,1)S(1)}, bf16[64,4096]{1,0:T(8,128)(2,1)S(1)}, u32[]{:S(2)}, u32[]{:S(2)}) collective-permute-start(bf16[64,4096]{1,0:T(8,128)(2,1)S(1)} %slice.58), channel_id=1, source_target_pairs={{0,1},{1,2},{2,3},{3,0},{4,5},{5,6},{6,7},{7,4},{8,9},{9,10},{10,1... | collective-permute-start | bytes 1572872 | tf_op jit(solution)/shard_map/ppermute | solution.py:30
  41.1 11.5 %collective-permute-start.3 = (bf16[64,4096]{1,0:T(8,128)(2,1)S(1)}, bf16[64,4096]{1,0:T(8,128)(2,1)}, u32[]{:S(2)}, u32[]{:S(2)}) collective-permute-start(bf16[64,4096]{1,0:T(8,128)(2,1)S(1)} %slice.59), channel_id=1, source_target_pairs={{0,3},{1,0},{2,1},{3,2},{4,7},{5,4},{6,5},{7,6},{8,11},{9,8},{10,9... | collective-permute-start | bytes 1572872 | tf_op jit(solution)/shard_map/ppermute | solution.py:30
  52.5 3.6 %copy-start.18 = (bf16[64,4096]{1,0:T(8,128)(2,1)}, bf16[64,4096]{1,0:T(8,128)(2,1)S(1)}, u32[]{:S(2)}) copy-start(bf16[64,4096]{1,0:T(8,128)(2,1)S(1)} %collective-permute-done.2.a2lo) | copy-start | bytes 1572868
  52.6 24.5 %collective-permute-start.4 = (bf16[128,4096]{1,0:T(8,128)(2,1)S(1)}, bf16[128,4096]{1,0:T(8,128)(2,1)}, u32[]{:S(2)}, u32[]{:S(2)}) collective-permute-start(bf16[128,4096]{1,0:T(8,128)(2,1)S(1)} %get-tuple-element.97.a0), channel_id=1, source_target_pairs={{0,1},{1,2},{2,3},{3,0},{4,5},{5,6},{6,7},{7,4},{8,9},{9,10},{10,1... | collective-permute-start | bytes 3145736 | tf_op jit(solution)/shard_map/ppermute | solution.py:30
  53.7 23.3 %collective-permute-start.5 = (bf16[128,4096]{1,0:T(8,128)(2,1)S(1)}, bf16[128,4096]{1,0:T(8,128)(2,1)}, u32[]{:S(2)}, u32[]{:S(2)}) collective-permute-start(bf16[128,4096]{1,0:T(8,128)(2,1)S(1)} %get-tuple-element.97.a0), channel_id=1, source_target_pairs={{0,3},{1,0},{2,1},{3,2},{4,7},{5,4},{6,5},{7,6},{8,11},{9,8},{10,9... | collective-permute-start | bytes 3145736 | tf_op jit(solution)/shard_map/ppermute | solution.py:30
  61.5 24.2 %collective-permute-start.6 = (bf16[256,2048]{1,0:T(8,128)(2,1)}, bf16[256,2048]{1,0:T(8,128)(2,1)S(1)}, u32[]{:S(2)}, u32[]{:S(2)}) collective-permute-start(bf16[256,2048]{1,0:T(8,128)(2,1)} %get-tuple-element.73), channel_id=1, source_target_pairs={{0,4},{1,5},{2,6},{3,7},{4,8},{5,9},{6,10},{7,11},{8,12},{9,13},{1... | collective-permute-start | bytes 3145736 | tf_op jit(solution)/shard_map/ppermute | solution.py:30
  62.9 22.8 %collective-permute-start.7 = (bf16[256,2048]{1,0:T(8,128)(2,1)}, bf16[256,2048]{1,0:T(8,128)(2,1)S(1)}, u32[]{:S(2)}, u32[]{:S(2)}) collective-permute-start(bf16[256,2048]{1,0:T(8,128)(2,1)} %get-tuple-element.76), channel_id=1, source_target_pairs={{0,12},{1,13},{2,14},{3,15},{4,0},{5,1},{6,2},{7,3},{8,4},{9,5},{1... | collective-permute-start | bytes 3145736 | tf_op jit(solution)/shard_map/ppermute | solution.py:30
  77.1 16.1 %copy-start.15 = (bf16[256,2048]{1,0:T(8,128)(2,1)S(1)}, bf16[256,2048]{1,0:T(8,128)(2,1)}, u32[]{:S(2)}) copy-start(bf16[256,2048]{1,0:T(8,128)(2,1)} %get-tuple-element.79) | copy-start | bytes 3145732
  85.7 8.9 %copy-start.10 = (bf16[256,2048]{1,0:T(8,128)(2,1)}, bf16[256,2048]{1,0:T(8,128)(2,1)S(1)}, u32[]{:S(2)}) copy-start(bf16[256,2048]{1,0:T(8,128)(2,1)S(1)} %collective-permute-done.6.pl_hi) | copy-start | bytes 3145732
  85.7 8.8 %copy-start.11 = (bf16[256,2048]{1,0:T(8,128)(2,1)}, bf16[256,2048]{1,0:T(8,128)(2,1)S(1)}, u32[]{:S(2)}) copy-start(bf16[256,2048]{1,0:T(8,128)(2,1)S(1)} %collective-permute-done.7.pl_lo) | copy-start | bytes 3145732
  85.7 14.2 %collective-permute-start.12 = (bf16[4,4096,128]{2,1,0:T(8,128)(2,1)}, bf16[4,4096,128]{2,1,0:T(8,128)(2,1)}, u32[]{:S(2)}, u32[]{:S(2)}) collective-permute-start(bf16[4,4096,128]{2,1,0:T(8,128)(2,1)} %bitcast.11), channel_id=1, source_target_pairs={{0,16},{16,0},{32,48},{48,32},{64,80},{80,64},{96,112},{112,96},{1... | collective-permute-start | bytes 12582920 | tf_op jit(solution)/shard_map/ppermute | solution.py:39
  94.6 17.6 %collective-permute-start.10 = (bf16[128,2048]{1,0:T(8,128)(2,1)}, bf16[128,2048]{1,0:T(8,128)(2,1)S(1)}, u32[]{:S(2)}, u32[]{:S(2)}) collective-permute-start(bf16[128,2048]{1,0:T(8,128)(2,1)} %get-tuple-element.139), channel_id=1, source_target_pairs={{0,4},{1,5},{2,6},{3,7},{4,8},{5,9},{6,10},{7,11},{8,12},{9,13},{1... | collective-permute-start | bytes 1572872 | tf_op jit(solution)/shard_map/ppermute | solution.py:30
  95.4 16.7 %collective-permute-start.11 = (bf16[128,2048]{1,0:T(8,128)(2,1)}, bf16[128,2048]{1,0:T(8,128)(2,1)S(1)}, u32[]{:S(2)}, u32[]{:S(2)}) collective-permute-start(bf16[128,2048]{1,0:T(8,128)(2,1)} %get-tuple-element.138), channel_id=1, source_target_pairs={{0,12},{1,13},{2,14},{3,15},{4,0},{5,1},{6,2},{7,3},{8,4},{9,5},{1... | collective-permute-start | bytes 1572872 | tf_op jit(solution)/shard_map/ppermute | solution.py:30
  97.3 14.9 %collective-permute-start.8 = (bf16[64,4096]{1,0:T(8,128)(2,1)}, bf16[64,4096]{1,0:T(8,128)(2,1)S(1)}, u32[]{:S(2)}, u32[]{:S(2)}) collective-permute-start(bf16[64,4096]{1,0:T(8,128)(2,1)} %slice.60), channel_id=1, source_target_pairs={{0,1},{1,2},{2,3},{3,0},{4,5},{5,6},{6,7},{7,4},{8,9},{9,10},{10,1... | collective-permute-start | bytes 1572872 | tf_op jit(solution)/shard_map/ppermute | solution.py:30
  97.3 14.9 %collective-permute-start.9 = (bf16[64,4096]{1,0:T(8,128)(2,1)}, bf16[64,4096]{1,0:T(8,128)(2,1)S(1)}, u32[]{:S(2)}, u32[]{:S(2)}) collective-permute-start(bf16[64,4096]{1,0:T(8,128)(2,1)} %slice.61), channel_id=1, source_target_pairs={{0,3},{1,0},{2,1},{3,2},{4,7},{5,4},{6,5},{7,6},{8,11},{9,8},{10,9... | collective-permute-start | bytes 1572872 | tf_op jit(solution)/shard_map/ppermute | solution.py:30
  112.2 7.1 %copy-start.16 = (bf16[128,2048]{1,0:T(8,128)(2,1)}, bf16[128,2048]{1,0:T(8,128)(2,1)S(1)}, u32[]{:S(2)}) copy-start(bf16[128,2048]{1,0:T(8,128)(2,1)S(1)} %collective-permute-done.10.su_lo) | copy-start | bytes 1572868
  112.2 7.1 %copy-start.17 = (bf16[128,2048]{1,0:T(8,128)(2,1)}, bf16[128,2048]{1,0:T(8,128)(2,1)S(1)}, u32[]{:S(2)}) copy-start(bf16[128,2048]{1,0:T(8,128)(2,1)S(1)} %collective-permute-done.11.su_hi) | copy-start | bytes 1572868
  119.3 24.8 %collective-permute-start.13 = (bf16[256,2048]{1,0:T(8,128)(2,1)}, bf16[256,2048]{1,0:T(8,128)(2,1)S(1)}, u32[]{:S(2)}, u32[]{:S(2)}) collective-permute-start(bf16[256,2048]{1,0:T(8,128)(2,1)} %get-tuple-element.88), channel_id=1, source_target_pairs={{0,4},{1,5},{2,6},{3,7},{4,8},{5,9},{6,10},{7,11},{8,12},{9,13},{1... | collective-permute-start | bytes 3145736 | tf_op jit(solution)/shard_map/ppermute | solution.py:30
  119.4 24.7 %collective-permute-start.14 = (bf16[256,2048]{1,0:T(8,128)(2,1)}, bf16[256,2048]{1,0:T(8,128)(2,1)S(1)}, u32[]{:S(2)}, u32[]{:S(2)}) collective-permute-start(bf16[256,2048]{1,0:T(8,128)(2,1)} %get-tuple-element.91), channel_id=1, source_target_pairs={{0,12},{1,13},{2,14},{3,15},{4,0},{5,1},{6,2},{7,3},{8,4},{9,5},{1... | collective-permute-start | bytes 3145736 | tf_op jit(solution)/shard_map/ppermute | solution.py:30
  125.7 18.3 %copy-start.14 = (bf16[256,2048]{1,0:T(8,128)(2,1)S(1)}, bf16[256,2048]{1,0:T(8,128)(2,1)}, u32[]{:S(2)}) copy-start(bf16[256,2048]{1,0:T(8,128)(2,1)} %get-tuple-element.105) | copy-start | bytes 3145732
  144.0 9.3 %copy-start.12 = (bf16[256,2048]{1,0:T(8,128)(2,1)}, bf16[256,2048]{1,0:T(8,128)(2,1)S(1)}, u32[]{:S(2)}) copy-start(bf16[256,2048]{1,0:T(8,128)(2,1)S(1)} %collective-permute-done.13.pl_hi) | copy-start | bytes 3145732
  144.0 9.3 %copy-start.13 = (bf16[256,2048]{1,0:T(8,128)(2,1)}, bf16[256,2048]{1,0:T(8,128)(2,1)S(1)}, u32[]{:S(2)}) copy-start(bf16[256,2048]{1,0:T(8,128)(2,1)S(1)} %collective-permute-done.14.pl_lo) | copy-start | bytes 3145732
  145.7 12.7 %collective-permute-start.15 = (bf16[128,2048]{1,0:T(8,128)(2,1)}, bf16[128,2048]{1,0:T(8,128)(2,1)S(1)}, u32[]{:S(2)}, u32[]{:S(2)}) collective-permute-start(bf16[128,2048]{1,0:T(8,128)(2,1)} %get-tuple-element.137), channel_id=1, source_target_pairs={{0,4},{1,5},{2,6},{3,7},{4,8},{5,9},{6,10},{7,11},{8,12},{9,13},{1... | collective-permute-start | bytes 1572872 | tf_op jit(solution)/shard_map/ppermute | solution.py:30
  145.7 12.7 %collective-permute-start.16 = (bf16[128,2048]{1,0:T(8,128)(2,1)}, bf16[128,2048]{1,0:T(8,128)(2,1)S(1)}, u32[]{:S(2)}, u32[]{:S(2)}) collective-permute-start(bf16[128,2048]{1,0:T(8,128)(2,1)} %get-tuple-element.136), channel_id=1, source_target_pairs={{0,12},{1,13},{2,14},{3,15},{4,0},{5,1},{6,2},{7,3},{8,4},{9,5},{1... | collective-permute-start | bytes 1572872 | tf_op jit(solution)/shard_map/ppermute | solution.py:30
  164.3 5.7 %collective-permute-start.17 = (f32[32,8192]{1,0:T(8,128)}, f32[32,8192]{1,0:T(8,128)S(1)}, u32[]{:S(2)}, u32[]{:S(2)}) collective-permute-start(f32[32,8192]{1,0:T(8,128)} %get-tuple-element.127), channel_id=1, source_target_pairs={{0,16},{16,0},{32,48},{48,32},{64,80},{80,64},{96,112},{112,96},{1... | collective-permute-start | bytes 3145736 | tf_op jit(solution)/shard_map/ppermute | solution.py:39
  171.4 7.7 %collective-permute-start.18 = (bf16[16,8192]{1,0:T(8,128)(2,1)S(1)}, bf16[16,8192]{1,0:T(8,128)(2,1)S(1)}, u32[]{:S(2)}, u32[]{:S(2)}) collective-permute-start(bf16[16,8192]{1,0:T(8,128)(2,1)S(1)} %get-tuple-element.142), channel_id=1, source_target_pairs={{0,32},{16,48},{32,0},{48,16},{64,96},{80,112},{96,64},{112,80},{1... | collective-permute-start | bytes 786440 | tf_op jit(solution)/shard_map/ppermute | solution.py:39
  172.7 8.5 %collective-permute-start.20 = (bf16[16,8192]{1,0:T(8,128)(2,1)S(1)}, bf16[16,8192]{1,0:T(8,128)(2,1)S(1)}, u32[]{:S(2)}, u32[]{:S(2)}) collective-permute-start(bf16[16,8192]{1,0:T(8,128)(2,1)S(1)} %get-tuple-element.143), channel_id=1, source_target_pairs={{0,96},{16,112},{32,64},{48,80},{64,32},{80,48},{96,0},{112,16},{1... | collective-permute-start | bytes 786440 | tf_op jit(solution)/shard_map/ppermute | solution.py:39
  181.4 7.8 %collective-permute-start.19 = (bf16[16,8192]{1,0:T(8,128)(2,1)S(1)}, bf16[16,8192]{1,0:T(8,128)(2,1)S(1)}, u32[]{:S(2)}, u32[]{:S(2)}) collective-permute-start(bf16[16,8192]{1,0:T(8,128)(2,1)S(1)} %get-tuple-element.140), channel_id=1, source_target_pairs={{0,96},{16,112},{32,64},{48,80},{64,32},{80,48},{96,0},{112,16},{1... | collective-permute-start | bytes 786440 | tf_op jit(solution)/shard_map/ppermute | solution.py:39
  183.3 11.3 %copy-start.2 = (f32[128,8192]{1,0:T(8,128)S(1)}, f32[128,8192]{1,0:T(8,128)}, u32[]{:S(2)}) copy-start(f32[128,8192]{1,0:T(8,128)} %get-tuple-element.128.merged.refs_5_) | copy-start | bytes 12582916
  183.3 11.3 %copy-start.5 = (s32[3]{0:T(128)S(1)}, s32[3]{0:T(128)}, u32[]{:S(2)}) copy-start(s32[3]{0:T(128)} %pad_add_fusion.spots.refs_0_) | copy-start | bytes 40
  183.3 6.2 %collective-permute-start.21 = (bf16[16,8192]{1,0:T(8,128)(2,1)S(1)}, bf16[16,8192]{1,0:T(8,128)(2,1)S(1)}, u32[]{:S(2)}, u32[]{:S(2)}) collective-permute-start(bf16[16,8192]{1,0:T(8,128)(2,1)S(1)} %get-tuple-element.141), channel_id=1, source_target_pairs={{0,32},{16,48},{32,0},{48,16},{64,96},{80,112},{96,64},{112,80},{1... | collective-permute-start | bytes 786440 | tf_op jit(solution)/shard_map/ppermute | solution.py:39
  189.7 8.5 %copy-start.3 = (f32[32,8192]{1,0:T(8,128)}, f32[32,8192]{1,0:T(8,128)S(1)}, u32[]{:S(2)}) copy-start(f32[32,8192]{1,0:T(8,128)S(1)} %pad_maximum_fusion.mine.refs_3_) | copy-start | bytes 3145732
  189.7 4.9 %collective-permute-start.22 = (f32[32,8192]{1,0:T(8,128)S(1)}, f32[32,8192]{1,0:T(8,128)S(1)}, u32[]{:S(2)}, u32[]{:S(2)}) collective-permute-start(f32[32,8192]{1,0:T(8,128)S(1)} %pad_maximum_fusion.mine.refs_3_), channel_id=1, source_target_pairs={{0,16},{16,0},{32,48},{48,32},{64,80},{80,64},{96,112},{112,96},{1... | collective-permute-start | bytes 3145736 | tf_op jit(solution)/shard_map/ppermute | solution.py:39
  194.5 3.7 %copy-start.4 = (f32[32,8192]{1,0:T(8,128)}, f32[32,8192]{1,0:T(8,128)S(1)}, u32[]{:S(2)}) copy-start(f32[32,8192]{1,0:T(8,128)S(1)} %collective-permute-done.22.theirs.refs_4_) | copy-start | bytes 3145732
  198.2 1.4 collective-permute-start.23
  199.6 10.2 %collective-permute-start.24 = (f32[128,64]{1,0:T(8,128)S(1)}, f32[128,64]{1,0:T(8,128)S(1)}, u32[]{:S(2)}, u32[]{:S(2)}) collective-permute-start(f32[128,64]{1,0:T(8,128)S(1)} %add.64), channel_id=1, source_target_pairs={{0,64},{16,80},{32,96},{48,112},{64,0},{80,16},{96,32},{112,48},{1... | collective-permute-start | bytes 98312 | tf_op jit(solution)/shard_map/ppermute | solution.py:39
  200.3 9.5 %collective-permute-start.25 = (f32[128,64]{1,0:T(8,128)S(1)}, f32[128,64]{1,0:T(8,128)S(1)}, u32[]{:S(2)}, u32[]{:S(2)}) collective-permute-start(f32[128,64]{1,0:T(8,128)S(1)} %add.64), channel_id=1, source_target_pairs={{0,32},{16,48},{32,64},{48,80},{64,96},{80,112},{96,0},{112,16},{1... | collective-permute-start | bytes 98312 | tf_op jit(solution)/shard_map/ppermute | solution.py:39
  201.6 8.2 %collective-permute-start.26 = (f32[128,64]{1,0:T(8,128)S(1)}, f32[128,64]{1,0:T(8,128)S(1)}, u32[]{:S(2)}, u32[]{:S(2)}) collective-permute-start(f32[128,64]{1,0:T(8,128)S(1)} %add.64), channel_id=1, source_target_pairs={{0,96},{16,112},{32,0},{48,16},{64,32},{80,48},{96,64},{112,80},{1... | collective-permute-start | bytes 98312 | tf_op jit(solution)/shard_map/ppermute | solution.py:39
  209.8 7.9 %copy-start.1 = (bf16[8192,128]{1,0:T(8,128)(2,1)S(1)}, bf16[8192,128]{1,0:T(8,128)(2,1)}, u32[]{:S(2)}) copy-start(bf16[8192,128]{1,0:T(8,128)(2,1)} %param.7) | copy-start | bytes 6291460
  (6 other events, 6.4 us)
Sparse Core Ops, SparseCore 0:
  10.3 54.0 all-gather.2
  119.4 79.6 reduce-scatter.1

commit v2 on v1

--- a/solution.py
+++ b/solution.py
@@ -71,6 +71,11 @@
 def dot3(left, right, dims):
     dot = lambda a, b: lax.dot_general(a, b, dims, preferred_element_type=F32)
     return dot(left[0], right[0]) + (dot(left[0], right[1]) + dot(left[1], right[0]))
+
+
+def dot2(left, right, dims):
+    dot = lambda a: lax.dot_general(a, right, dims, preferred_element_type=F32)
+    return dot(left[0]) + dot(left[1])
 
 
 def turn_kernel(spots, cots, cturn):
@@ -198,7 +203,7 @@
         merged[...] = total
         share = dot3(halves(qrows[...]), halves(total), NN)
         keep[...] = share[: RANK // 2]
-        give[...] = share[RANK // 2 :]
+        give[...] = share[RANK // 2 :].astype(BF16)
 
     @pl.when(j < mid)
     def _():
@@ -228,7 +233,7 @@
         out_shape=[
             jax.ShapeDtypeStruct((HD, 2 * width), F32),
             jax.ShapeDtypeStruct((RANK // 2, 2 * width), F32),
-            jax.ShapeDtypeStruct((RANK // 2, 2 * width), F32),
+            jax.ShapeDtypeStruct((RANK // 2, 2 * width), BF16),
         ],
         input_output_aliases={7 + k: k for k in range(len(before))},
         cost_estimate=cost(6 * width * RANK * HD, 14 * width * HD),
@@ -248,9 +253,9 @@
         gram[...] = jnp.zeros_like(gram)
         right[...] = jnp.zeros_like(right)
 
-    pt = halves(ordered(spots[2], mine, theirs))
-    right[...] += dot3(halves(merged[...]), pt, NT)
-    gram[...] += dot3(pt, pt, NT)
+    pt = ordered(spots[2], mine, theirs)
+    right[...] += dot2(halves(merged[...]), pt, NT)
+    gram[...] += lax.dot_general(pt, pt, NT, preferred_element_type=F32)
 
 
 def gram_of(spots, mine, theirs, merged):
@@ -304,8 +309,8 @@
         zturn = lax.dot_general(right, inv[...], TN, precision=HI, preferred_element_type=F32)
         zhi[...], zlo[...] = halves(zturn)
 
-    pt = halves(ordered(spots[2], mine, theirs))
-    approx = dot3((zhi[...], zlo[...]), pt, NN)
+    pt = ordered(spots[2], mine, theirs)
+    approx = dot2((zhi[...], zlo[...]), pt, NN)
     update[...] = approx.astype(BF16).T
     newfb[...] = (merged[...] - approx).astype(BF16).T
 
@@ -367,7 +372,7 @@
 
 
 def sum_left(keep, give):
-    chip = (keep + other_core(give)).astype(BF16)
+    chip = (keep + other_core(give).astype(F32)).astype(BF16)
     mid = chip.shape[0] // 2
     near = lambda array: along_dp(array, lambda x, c: (x ^ 1, c))
     far = lambda array: along_dp(array, lambda x, c: (3 - x, c))
@@ -377,7 +382,7 @@
     second_pair = add(second, far(second)).astype(BF16)
     mine = jnp.concatenate(
         [add(first_pair, far(first_pair)), add(second_pair, near(second_pair))], axis=0
-    )
+    ).astype(BF16)
     return mine, other_core(mine)
 
 

time: 225 us -> 222 us (0.987)
  transfers between devices with their start and end apart: 30 -> 30, of which waited for: 14 -> 14; matrix products, arithmetic and copies ran while one was open for 8% -> 8% of each run, Pallas kernels for 25% -> 24%
where the time goes in v2:
time: 222 us; the launch traced here: 221 us
  waiting for transfers between devices  76.6 us (35%)
  Pallas kernels  59 us (27%)
  starting transfers between devices  48 us (22%)
  local copies, waits for them, and re-layouts  17 us (8%)
  between operations  14.3 us (6%)
  other arithmetic  6.55 us (3%)
    ppermute x16, waiting for transfers between devices, along_tensor(): return lax.ppermute(array, 'tensor', perm)  56.4 us
    ppermute x16, starting transfers between devices, along_tensor(): return lax.ppermute(array, 'tensor', perm)  24.5 us
    ppermute x11, starting transfers between devices, along_dp(): return lax.ppermute(array, 'dp', perm)  18.5 us
    ppermute x11, waiting for transfers between devices, along_dp(): return lax.ppermute(array, 'dp', perm)  17 us
    pallas_call x1, Pallas kernels, input_parts(): pl.pallas_call(input_kernel, grid_spec=pltpu.PrefetchScalarGridSpec(num_s...  12.2 us
    pallas_call x2, Pallas kernels, grad_parts(): pl.pallas_call(grad_kernel, grid=(width // TILE,), in_specs=[cols_spec(pi...  10.8 us
    pallas_call x2, Pallas kernels, merge(): pl.pallas_call(merge_kernel, grid=(steps,), in_specs=[shifted(HD), cols_s...  9.81 us
    unnamed x49, local copies, waits for them, and re-layouts  8.34 us
  transfers between devices with their start and end apart: 30, of which 14 were waited for; matrix products, arithmetic and copies ran while one was open for 8% of the time, Pallas kernels for 24%

profile of v2, /device:TPU:1, one launch (start us, length us, event | category | flops | bytes accessed | tf_op | source)
XLA Modules:
  0.0 221.5 jit_solution(8752052442697015707)
XLA Ops:
  7.2 1.5 copy-done
  9.8 1.7 fusion
  11.6 2.2 collective-permute-start
  13.8 1.5 collective-permute-start.1
  15.3 5.0 %all-to-all-start = ((bf16[4,512,128]{2,1,0:T(8,128)(2,1)}), bf16[4,512,128]{2,1,0:T(8,128)(2,1)S(1)}, u32[]{:S(2)}, u32[]{:S(2)}) async-start(bf16[4,512,128]{2,1,0:T(8,128)(2,1)} %bitcast.2), calls=%async_computation | async-start | bytes 1048576 | tf_op jit(solution)/shard_map/all_to_all | solution.py:414
  20.3 4.1 %copy.12 = bf16[8192,128]{0,1:T(8,128)(2,1)} copy(bf16[8192,128]{1,0:T(8,128)(2,1)} %param.8) | data formatting | bytes 4194304 | tf_op args[3]
  25.1 3.1 %all-to-all-done.cots = bf16[4,512,128]{2,1,0:T(8,128)(2,1)S(1)} async-done(((bf16[4,512,128]{2,1,0:T(8,128)(2,1)}), bf16[4,512,128]{2,1,0:T(8,128)(2,1)S(1)}, u32[]{:S(2)}, u32[]{:S(2)}) %all-to-all-start) | async-done | bytes 524320 | tf_op jit(solution)/shard_map/all_to_all | solution.py:414
  28.2 9.9 %collective-permute-done.a3 = bf16[128,4096]{1,0:T(8,128)(2,1)} collective-permute-done((bf16[128,4096]{1,0:T(8,128)(2,1)S(1)}, bf16[128,4096]{1,0:T(8,128)(2,1)}, u32[]{:S(2)}, u32[]{:S(2)}) %collective-permute-start) | collective-permute-done | bytes 1048608 | tf_op jit(solution)/shard_map/ppermute | solution.py:30
  41.1 1.9 collective-permute-start.3
  43.7 2.0 turn_cots.1.cturn
  45.7 6.8 %collective-permute-done.2.a2lo = bf16[64,4096]{1,0:T(8,128)(2,1)S(1)} collective-permute-done((bf16[64,4096]{1,0:T(8,128)(2,1)S(1)}, bf16[64,4096]{1,0:T(8,128)(2,1)S(1)}, u32[]{:S(2)}, u32[]{:S(2)}) %collective-permute-start.2) | collective-permute-done | bytes 524320 | tf_op jit(solution)/shard_map/ppermute | solution.py:30
  53.7 2.4 %collective-permute-start.5 = (bf16[128,4096]{1,0:T(8,128)(2,1)S(1)}, bf16[128,4096]{1,0:T(8,128)(2,1)}, u32[]{:S(2)}, u32[]{:S(2)}) collective-permute-start(bf16[128,4096]{1,0:T(8,128)(2,1)S(1)} %get-tuple-element.97.a0), channel_id=1, source_target_pairs={{0,3},{1,0},{2,1},{3,2},{4,7},{5,4},{6,5},{7,6},{8,11},{9,8},{10,9... | collective-permute-start | bytes 3145736 | tf_op jit(solution)/shard_map/ppermute | solution.py:30
  56.1 5.4 %grad_parts.2 = (bf16[256,2048]{1,0:T(8,128)(2,1)}, bf16[256,2048]{1,0:T(8,128)(2,1)}, bf16[256,2048]{1,0:T(8,128)(2,1)}) custom-call(bf16[128,4096]{1,0:T(8,128)(2,1)} %copy-done.8, bf16[128,4096]{1,0:T(8,128)(2,1)} %collective-permute-done.1.a1, bf16[64,4096]{1,0:T(8,128)(2,1)} %copy-done.20, bf16[64,4096]{1,0:T(8,128)(2,1)} %collective-permute-done.3.a2hi, ...), custom_call_target="tpu_custom_call" | custom-call | flops 2147483648 | bytes 9437184 | tf_op jit(solution)/shard_map/grad_parts/pallas_call | solution.py:147
  61.5 1.4 collective-permute-start.6
  62.9 2.2 collective-permute-start.7
  65.1 12.0 %collective-permute-done.4.a3 = bf16[128,4096]{1,0:T(8,128)(2,1)} collective-permute-done((bf16[128,4096]{1,0:T(8,128)(2,1)S(1)}, bf16[128,4096]{1,0:T(8,128)(2,1)}, u32[]{:S(2)}, u32[]{:S(2)}) %collective-permute-start.4) | collective-permute-done | bytes 1048608 | tf_op jit(solution)/shard_map/ppermute | solution.py:30
  77.1 8.6 %collective-permute-done.6.pl_hi = bf16[256,2048]{1,0:T(8,128)(2,1)S(1)} collective-permute-done((bf16[256,2048]{1,0:T(8,128)(2,1)}, bf16[256,2048]{1,0:T(8,128)(2,1)S(1)}, u32[]{:S(2)}, u32[]{:S(2)}) %collective-permute-start.6) | collective-permute-done | bytes 1048608 | tf_op jit(solution)/shard_map/ppermute | solution.py:30
  85.7 3.7 %collective-permute-start.12 = (bf16[4,4096,128]{2,1,0:T(8,128)(2,1)}, bf16[4,4096,128]{2,1,0:T(8,128)(2,1)}, u32[]{:S(2)}, u32[]{:S(2)}) collective-permute-start(bf16[4,4096,128]{2,1,0:T(8,128)(2,1)} %bitcast.11), channel_id=1, source_target_pairs={{0,16},{16,0},{32,48},{48,32},{64,80},{80,64},{96,112},{112,96},{1... | collective-permute-start | bytes 12582920 | tf_op jit(solution)/shard_map/ppermute | solution.py:39
  89.4 1.9 slice.60
  91.3 1.9 slice.61
  93.2 1.4 add_convert_fusion.3
  95.4 1.8 collective-permute-start.11
  97.3 2.7 %collective-permute-start.9 = (bf16[64,4096]{1,0:T(8,128)(2,1)}, bf16[64,4096]{1,0:T(8,128)(2,1)S(1)}, u32[]{:S(2)}, u32[]{:S(2)}) collective-permute-start(bf16[64,4096]{1,0:T(8,128)(2,1)} %slice.61), channel_id=1, source_target_pairs={{0,3},{1,0},{2,1},{3,2},{4,7},{5,4},{6,5},{7,6},{8,11},{9,8},{10,9... | collective-permute-start | bytes 1572872 | tf_op jit(solution)/shard_map/ppermute | solution.py:30
  100.0 12.2 %input_parts.1 = bf16[512,8192]{1,0:T(8,128)(2,1)} custom-call(s32[3]{0:T(128)} %pad_add_fusion.spots.refs_0_, bf16[4,4096,128]{2,1,0:T(8,128)(2,1)} %bitcast.12, bf16[4,4096,128]{2,1,0:T(8,128)(2,1)} %collective-permute-done.12.theirs, bf16[4,512,128]{2,1,0:T(8,128)(2,1)} %copy-done.7), custom_call_target="tpu_custom_call" | custom-call | flops 4294967296 | bytes 18874368 | tf_op jit(solution)/shard_map/input_parts/pallas_call | solution.py:177
  113.8 5.4 %grad_parts.3 = (bf16[256,2048]{1,0:T(8,128)(2,1)}, bf16[256,2048]{1,0:T(8,128)(2,1)}, bf16[256,2048]{1,0:T(8,128)(2,1)}) custom-call(bf16[128,4096]{1,0:T(8,128)(2,1)} %copy-done.9, bf16[128,4096]{1,0:T(8,128)(2,1)} %collective-permute-done.5.a1, bf16[64,4096]{1,0:T(8,128)(2,1)} %copy-done.21, bf16[64,4096]{1,0:T(8,128)(2,1)} %copy-done.22, ...), custom_call_target="tpu_custom_call" | custom-call | flops 2147483648 | bytes 9437184 | tf_op jit(solution)/shard_map/grad_parts/pallas_call | solution.py:147
  119.4 2.7 %collective-permute-start.14 = (bf16[256,2048]{1,0:T(8,128)(2,1)}, bf16[256,2048]{1,0:T(8,128)(2,1)S(1)}, u32[]{:S(2)}, u32[]{:S(2)}) collective-permute-start(bf16[256,2048]{1,0:T(8,128)(2,1)} %get-tuple-element.91), channel_id=1, source_target_pairs={{0,12},{1,13},{2,14},{3,15},{4,0},{5,1},{6,2},{7,3},{8,4},{9,5},{1... | collective-permute-start | bytes 3145736 | tf_op jit(solution)/shard_map/ppermute | solution.py:30
  122.0 3.7 %own_part.3.own = f32[128,4096]{1,0:T(8,128)} custom-call(bf16[128,4096]{1,0:T(8,128)(2,1)} %copy-done.9, bf16[128,4096]{1,0:T(8,128)(2,1)} %collective-permute-done.5.a1, bf16[64,4096]{1,0:T(8,128)(2,1)} %copy-done.21, bf16[64,4096]{1,0:T(8,128)(2,1)} %copy-done.22, bf16[128,4096]{1,0:T(8,128)(2,1)} %collective-permute-done.4.a3, ...), custom_call_target="tpu_custom_call" | custom-call | flops 536870912 | bytes 6291456 | tf_op jit(solution)/shard_map/own_part/pallas_call | solution.py:109
  125.7 4.3 %own_part.2.own = f32[128,4096]{1,0:T(8,128)} custom-call(bf16[128,4096]{1,0:T(8,128)(2,1)} %copy-done.8, bf16[128,4096]{1,0:T(8,128)(2,1)} %collective-permute-done.1.a1, bf16[64,4096]{1,0:T(8,128)(2,1)} %copy-done.20, bf16[64,4096]{1,0:T(8,128)(2,1)} %collective-permute-done.3.a2hi, bf16[128,4096]{1,0:T(8,128)(2,1)} %collective-permute-done.a3, ...), custom_call_target="tpu_custom_call" | custom-call | flops 536870912 | bytes 6291456 | tf_op jit(solution)/shard_map/own_part/pallas_call | solution.py:109
  130.0 14.0 %collective-permute-done.13.pl_hi = bf16[256,2048]{1,0:T(8,128)(2,1)S(1)} collective-permute-done((bf16[256,2048]{1,0:T(8,128)(2,1)}, bf16[256,2048]{1,0:T(8,128)(2,1)S(1)}, u32[]{:S(2)}, u32[]{:S(2)}) %collective-permute-start.13) | collective-permute-done | bytes 1048608 | tf_op jit(solution)/shard_map/ppermute | solution.py:30
  144.1 1.6 add_convert_fusion.1
  145.7 2.7 %collective-permute-start.16 = (bf16[128,2048]{1,0:T(8,128)(2,1)}, bf16[128,2048]{1,0:T(8,128)(2,1)S(1)}, u32[]{:S(2)}, u32[]{:S(2)}) collective-permute-start(bf16[128,2048]{1,0:T(8,128)(2,1)} %get-tuple-element.136), channel_id=1, source_target_pairs={{0,12},{1,13},{2,14},{3,15},{4,0},{5,1},{6,2},{7,3},{8,4},{9,5},{1... | collective-permute-start | bytes 1572872 | tf_op jit(solution)/shard_map/ppermute | solution.py:30
  148.4 4.9 %merge.2 = (f32[128,8192]{1,0:T(8,128)}, f32[32,8192]{1,0:T(8,128)}, bf16[32,8192]{1,0:T(8,128)(2,1)}) custom-call(bf16[128,8192]{1,0:T(8,128)(2,1)} %bitcast.9, f32[128,4096]{1,0:T(8,128)} %own_part.2.own, bf16[256,2048]{1,0:T(8,128)(2,1)} %copy-done.11, bf16[256,2048]{1,0:T(8,128)(2,1)} %copy-done.10, bf16[128,2048]{1,0:T(8,128)(2,1)} %copy-done.16, ...), custom_call_target="tpu_custom_call" | custom-call | flops 201326592 | bytes 7340032 | tf_op jit(solution)/shard_map/merge/pallas_call | solution.py:227
  153.3 5.0 %collective-permute-done.15.su_lo = bf16[128,2048]{1,0:T(8,128)(2,1)S(1)} collective-permute-done((bf16[128,2048]{1,0:T(8,128)(2,1)}, bf16[128,2048]{1,0:T(8,128)(2,1)S(1)}, u32[]{:S(2)}, u32[]{:S(2)}) %collective-permute-start.15) | collective-permute-done | bytes 524320 | tf_op jit(solution)/shard_map/ppermute | solution.py:30
  159.3 4.9 %merge.3 = (f32[128,8192]{1,0:T(8,128)}, f32[32,8192]{1,0:T(8,128)}, bf16[32,8192]{1,0:T(8,128)(2,1)}) custom-call(bf16[128,8192]{1,0:T(8,128)(2,1)} %bitcast.10, f32[128,4096]{1,0:T(8,128)} %own_part.3.own, bf16[256,2048]{1,0:T(8,128)(2,1)} %copy-done.13, bf16[256,2048]{1,0:T(8,128)(2,1)} %copy-done.12, ...), custom_call_target="tpu_custom_call", output_to_operand_aliasing={{0}: (7, {}), {1}: (8, {}), {2}: (9, {})} | custom-call | flops 201326592 | bytes 7340032 | tf_op jit(solution)/shard_map/merge/pallas_call | solution.py:227
  164.2 3.3 %collective-permute-start.17 = (bf16[32,8192]{1,0:T(8,128)(2,1)}, bf16[32,8192]{1,0:T(8,128)(2,1)S(1)}, u32[]{:S(2)}, u32[]{:S(2)}) collective-permute-start(bf16[32,8192]{1,0:T(8,128)(2,1)} %get-tuple-element.127), channel_id=1, source_target_pairs={{0,16},{16,0},{32,48},{48,32},{64,80},{80,64},{96,112},{112,96},{1... | collective-permute-start | bytes 1572872 | tf_op jit(solution)/shard_map/ppermute | solution.py:39
  167.5 1.7 collective-permute-done.17
  169.3 1.3 add_convert_fusion
  172.0 1.8 collective-permute-start.20
  173.8 4.6 %collective-permute-done.18 = bf16[16,8192]{1,0:T(8,128)(2,1)S(1)} collective-permute-done((bf16[16,8192]{1,0:T(8,128)(2,1)S(1)}, bf16[16,8192]{1,0:T(8,128)(2,1)S(1)}, u32[]{:S(2)}, u32[]{:S(2)}) %collective-permute-start.18) | collective-permute-done | bytes 262176 | tf_op jit(solution)/shard_map/ppermute | solution.py:39
  178.3 2.1 collective-permute-done.20
  180.6 1.9 collective-permute-start.19
  182.5 5.9 %collective-permute-done.19 = bf16[16,8192]{1,0:T(8,128)(2,1)S(1)} collective-permute-done((bf16[16,8192]{1,0:T(8,128)(2,1)S(1)}, bf16[16,8192]{1,0:T(8,128)(2,1)S(1)}, u32[]{:S(2)}, u32[]{:S(2)}) %collective-permute-start.19) | collective-permute-done | bytes 262176 | tf_op jit(solution)/shard_map/ppermute | solution.py:39
  188.8 2.6 %collective-permute-start.22 = (bf16[32,8192]{1,0:T(8,128)(2,1)S(1)}, bf16[32,8192]{1,0:T(8,128)(2,1)S(1)}, u32[]{:S(2)}, u32[]{:S(2)}) collective-permute-start(bf16[32,8192]{1,0:T(8,128)(2,1)S(1)} %pad_maximum_fusion.mine.refs_3_), channel_id=1, source_target_pairs={{0,16},{16,0},{32,48},{48,32},{64,80},{80,64},{96,112},{112,96},{1... | collective-permute-start | bytes 1572872 | tf_op jit(solution)/shard_map/ppermute | solution.py:39
  191.4 1.5 collective-permute-done.22.theirs.refs_4_
  193.0 2.5 %gram.1 = (f32[128,64]{1,0:T(8,128)S(1)}, f32[64,64]{1,0:T(8,128)S(1)}) custom-call(s32[3]{0:T(128)S(1)} %copy-done.5, bf16[32,8192]{1,0:T(8,128)(2,1)S(1)} %pad_maximum_fusion.mine.refs_3_, bf16[32,8192]{1,0:T(8,128)(2,1)S(1)} %collective-permute-done.22.theirs.refs_4_, f32[128,8192]{1,0:T(8,128)S(1)} %copy-done.2), custom_call_target="tpu_custom_call" | custom-call | flops 603979776 | bytes 6291456 | tf_op jit(solution)/shard_map/gram/pallas_call | solution.py:264
  198.8 1.4 collective-permute-start.26
  200.2 6.8 %inverse_factor.1.refs_1_ = f32[64,64]{1,0:T(8,128)} custom-call(f32[64,64]{1,0:T(8,128)} %copy-done.6), custom_call_target="tpu_custom_call" | custom-call | flops 104857600 | bytes 65536 | tf_op jit(solution)/shard_map/inverse_factor/pallas_call | solution.py:295
  207.7 6.9 %final.1 = (f32[64,128]{1,0:T(8,128)}, bf16[8192,128]{1,0:T(8,128)(2,1)}, bf16[8192,128]{1,0:T(8,128)(2,1)}) custom-call(s32[3]{0:T(128)} %pad_add_fusion.spots.refs_0_, f32[64,64]{1,0:T(8,128)} %inverse_factor.1.refs_1_, f32[128,64]{1,0:T(8,128)} %add_add_fusion.refs_2_, bf16[32,8192]{1,0:T(8,128)(2,1)} %copy-done.3, bf16[32,8192]{1,0:T(8,128)(2,1)} %copy-done.4, ...), custom_call_target="tpu_custom_call" | custom-call | flops 402653184 | bytes 12582912 | tf_op jit(solution)/shard_map/final/pallas_call | solution.py:321
  (93 shorter events, 16.2 us)
Async XLA Ops:
  7.2 78.5 %all-gather.3.cloned.1.call-start = ((), (), s32[]{:S(2)}) async-start(), calls=%async_computation.3 | async-start | bytes 5242880 | tf_op jit(solution)/shard_map/all_gather | solution.py:418
  11.6 12.9 %copy-start.8 = (bf16[128,4096]{1,0:T(8,128)(2,1)}, bf16[128,4096]{1,0:T(8,128)(2,1)S(1)}, u32[]{:S(2)}) copy-start(bf16[128,4096]{1,0:T(8,128)(2,1)S(1)} %get-tuple-element.92.a0) | copy-start | bytes 3145732
  11.6 42.2 %copy-start.9 = (bf16[128,4096]{1,0:T(8,128)(2,1)}, bf16[128,4096]{1,0:T(8,128)(2,1)S(1)}, u32[]{:S(2)}) copy-start(bf16[128,4096]{1,0:T(8,128)(2,1)S(1)} %get-tuple-element.97.a0) | copy-start | bytes 3145732
  11.6 26.5 %collective-permute-start = (bf16[128,4096]{1,0:T(8,128)(2,1)S(1)}, bf16[128,4096]{1,0:T(8,128)(2,1)}, u32[]{:S(2)}, u32[]{:S(2)}) collective-permute-start(bf16[128,4096]{1,0:T(8,128)(2,1)S(1)} %get-tuple-element.92.a0), channel_id=1, source_target_pairs={{0,1},{1,2},{2,3},{3,0},{4,5},{5,6},{6,7},{7,4},{8,9},{9,10},{10,1... | collective-permute-start | bytes 3145736 | tf_op jit(solution)/shard_map/ppermute | solution.py:30
  13.8 24.3 %collective-permute-start.1 = (bf16[128,4096]{1,0:T(8,128)(2,1)S(1)}, bf16[128,4096]{1,0:T(8,128)(2,1)}, u32[]{:S(2)}, u32[]{:S(2)}) collective-permute-start(bf16[128,4096]{1,0:T(8,128)(2,1)S(1)} %get-tuple-element.92.a0), channel_id=1, source_target_pairs={{0,3},{1,0},{2,1},{3,2},{4,7},{5,4},{6,5},{7,6},{8,11},{9,8},{10,9... | collective-permute-start | bytes 3145736 | tf_op jit(solution)/shard_map/ppermute | solution.py:30
  15.3 12.9 %all-to-all-start = ((bf16[4,512,128]{2,1,0:T(8,128)(2,1)}), bf16[4,512,128]{2,1,0:T(8,128)(2,1)S(1)}, u32[]{:S(2)}, u32[]{:S(2)}) async-start(bf16[4,512,128]{2,1,0:T(8,128)(2,1)} %bitcast.2), calls=%async_computation | async-start | bytes 1048576 | tf_op jit(solution)/shard_map/all_to_all | solution.py:414
  20.3 194.3 %reduce-scatter.2.cloned.1.call-start = ((), (), s32[]{:S(2)}) async-start(), calls=%async_computation.2 | async-start | bytes 10485760 | tf_op jit(solution)/shard_map/reduce_scatter | solution.py:445
  20.3 4.1 %copy-start.23 = (f32[128,64]{0,1:T(8,128)S(1)}, f32[128,64]{0,1:T(8,128)}, u32[]{:S(2)}) copy-start(f32[128,64]{0,1:T(8,128)} %param.9) | copy-start | bytes 98308
  28.2 15.5 %copy-start.7 = (bf16[4,512,128]{2,1,0:T(8,128)(2,1)}, bf16[4,512,128]{2,1,0:T(8,128)(2,1)S(1)}, u32[]{:S(2)}) copy-start(bf16[4,512,128]{2,1,0:T(8,128)(2,1)S(1)} %all-to-all-done.cots) | copy-start | bytes 1572868
  39.1 13.4 %collective-permute-start.2 = (bf16[64,4096]{1,0:T(8,128)(2,1)S(1)}, bf16[64,4096]{1,0:T(8,128)(2,1)S(1)}, u32[]{:S(2)}, u32[]{:S(2)}) collective-permute-start(bf16[64,4096]{1,0:T(8,128)(2,1)S(1)} %slice.58), channel_id=1, source_target_pairs={{0,1},{1,2},{2,3},{3,0},{4,5},{5,6},{6,7},{7,4},{8,9},{9,10},{10,1... | collective-permute-start | bytes 1572872 | tf_op jit(solution)/shard_map/ppermute | solution.py:30
  41.1 11.5 %collective-permute-start.3 = (bf16[64,4096]{1,0:T(8,128)(2,1)S(1)}, bf16[64,4096]{1,0:T(8,128)(2,1)}, u32[]{:S(2)}, u32[]{:S(2)}) collective-permute-start(bf16[64,4096]{1,0:T(8,128)(2,1)S(1)} %slice.59), channel_id=1, source_target_pairs={{0,3},{1,0},{2,1},{3,2},{4,7},{5,4},{6,5},{7,6},{8,11},{9,8},{10,9... | collective-permute-start | bytes 1572872 | tf_op jit(solution)/shard_map/ppermute | solution.py:30
  52.5 3.6 %copy-start.20 = (bf16[64,4096]{1,0:T(8,128)(2,1)}, bf16[64,4096]{1,0:T(8,128)(2,1)S(1)}, u32[]{:S(2)}) copy-start(bf16[64,4096]{1,0:T(8,128)(2,1)S(1)} %collective-permute-done.2.a2lo) | copy-start | bytes 1572868
  52.6 24.5 %collective-permute-start.4 = (bf16[128,4096]{1,0:T(8,128)(2,1)S(1)}, bf16[128,4096]{1,0:T(8,128)(2,1)}, u32[]{:S(2)}, u32[]{:S(2)}) collective-permute-start(bf16[128,4096]{1,0:T(8,128)(2,1)S(1)} %get-tuple-element.97.a0), channel_id=1, source_target_pairs={{0,1},{1,2},{2,3},{3,0},{4,5},{5,6},{6,7},{7,4},{8,9},{9,10},{10,1... | collective-permute-start | bytes 3145736 | tf_op jit(solution)/shard_map/ppermute | solution.py:30
  53.7 23.3 %collective-permute-start.5 = (bf16[128,4096]{1,0:T(8,128)(2,1)S(1)}, bf16[128,4096]{1,0:T(8,128)(2,1)}, u32[]{:S(2)}, u32[]{:S(2)}) collective-permute-start(bf16[128,4096]{1,0:T(8,128)(2,1)S(1)} %get-tuple-element.97.a0), channel_id=1, source_target_pairs={{0,3},{1,0},{2,1},{3,2},{4,7},{5,4},{6,5},{7,6},{8,11},{9,8},{10,9... | collective-permute-start | bytes 3145736 | tf_op jit(solution)/shard_map/ppermute | solution.py:30
  61.5 24.2 %collective-permute-start.6 = (bf16[256,2048]{1,0:T(8,128)(2,1)}, bf16[256,2048]{1,0:T(8,128)(2,1)S(1)}, u32[]{:S(2)}, u32[]{:S(2)}) collective-permute-start(bf16[256,2048]{1,0:T(8,128)(2,1)} %get-tuple-element.73), channel_id=1, source_target_pairs={{0,4},{1,5},{2,6},{3,7},{4,8},{5,9},{6,10},{7,11},{8,12},{9,13},{1... | collective-permute-start | bytes 3145736 | tf_op jit(solution)/shard_map/ppermute | solution.py:30
  62.9 22.8 %collective-permute-start.7 = (bf16[256,2048]{1,0:T(8,128)(2,1)}, bf16[256,2048]{1,0:T(8,128)(2,1)S(1)}, u32[]{:S(2)}, u32[]{:S(2)}) collective-permute-start(bf16[256,2048]{1,0:T(8,128)(2,1)} %get-tuple-element.76), channel_id=1, source_target_pairs={{0,12},{1,13},{2,14},{3,15},{4,0},{5,1},{6,2},{7,3},{8,4},{9,5},{1... | collective-permute-start | bytes 3145736 | tf_op jit(solution)/shard_map/ppermute | solution.py:30
  77.1 16.1 %copy-start.15 = (bf16[256,2048]{1,0:T(8,128)(2,1)S(1)}, bf16[256,2048]{1,0:T(8,128)(2,1)}, u32[]{:S(2)}) copy-start(bf16[256,2048]{1,0:T(8,128)(2,1)} %get-tuple-element.79) | copy-start | bytes 3145732
  85.7 8.9 %copy-start.10 = (bf16[256,2048]{1,0:T(8,128)(2,1)}, bf16[256,2048]{1,0:T(8,128)(2,1)S(1)}, u32[]{:S(2)}) copy-start(bf16[256,2048]{1,0:T(8,128)(2,1)S(1)} %collective-permute-done.6.pl_hi) | copy-start | bytes 3145732
  85.7 8.8 %copy-start.11 = (bf16[256,2048]{1,0:T(8,128)(2,1)}, bf16[256,2048]{1,0:T(8,128)(2,1)S(1)}, u32[]{:S(2)}) copy-start(bf16[256,2048]{1,0:T(8,128)(2,1)S(1)} %collective-permute-done.7.pl_lo) | copy-start | bytes 3145732
  85.7 14.2 %collective-permute-start.12 = (bf16[4,4096,128]{2,1,0:T(8,128)(2,1)}, bf16[4,4096,128]{2,1,0:T(8,128)(2,1)}, u32[]{:S(2)}, u32[]{:S(2)}) collective-permute-start(bf16[4,4096,128]{2,1,0:T(8,128)(2,1)} %bitcast.11), channel_id=1, source_target_pairs={{0,16},{16,0},{32,48},{48,32},{64,80},{80,64},{96,112},{112,96},{1... | collective-permute-start | bytes 12582920 | tf_op jit(solution)/shard_map/ppermute | solution.py:39
  94.6 17.6 %collective-permute-start.10 = (bf16[128,2048]{1,0:T(8,128)(2,1)}, bf16[128,2048]{1,0:T(8,128)(2,1)S(1)}, u32[]{:S(2)}, u32[]{:S(2)}) collective-permute-start(bf16[128,2048]{1,0:T(8,128)(2,1)} %get-tuple-element.139), channel_id=1, source_target_pairs={{0,4},{1,5},{2,6},{3,7},{4,8},{5,9},{6,10},{7,11},{8,12},{9,13},{1... | collective-permute-start | bytes 1572872 | tf_op jit(solution)/shard_map/ppermute | solution.py:30
  95.4 16.7 %collective-permute-start.11 = (bf16[128,2048]{1,0:T(8,128)(2,1)}, bf16[128,2048]{1,0:T(8,128)(2,1)S(1)}, u32[]{:S(2)}, u32[]{:S(2)}) collective-permute-start(bf16[128,2048]{1,0:T(8,128)(2,1)} %get-tuple-element.138), channel_id=1, source_target_pairs={{0,12},{1,13},{2,14},{3,15},{4,0},{5,1},{6,2},{7,3},{8,4},{9,5},{1... | collective-permute-start | bytes 1572872 | tf_op jit(solution)/shard_map/ppermute | solution.py:30
  97.3 14.9 %collective-permute-start.8 = (bf16[64,4096]{1,0:T(8,128)(2,1)}, bf16[64,4096]{1,0:T(8,128)(2,1)S(1)}, u32[]{:S(2)}, u32[]{:S(2)}) collective-permute-start(bf16[64,4096]{1,0:T(8,128)(2,1)} %slice.60), channel_id=1, source_target_pairs={{0,1},{1,2},{2,3},{3,0},{4,5},{5,6},{6,7},{7,4},{8,9},{9,10},{10,1... | collective-permute-start | bytes 1572872 | tf_op jit(solution)/shard_map/ppermute | solution.py:30
  97.3 14.9 %collective-permute-start.9 = (bf16[64,4096]{1,0:T(8,128)(2,1)}, bf16[64,4096]{1,0:T(8,128)(2,1)S(1)}, u32[]{:S(2)}, u32[]{:S(2)}) collective-permute-start(bf16[64,4096]{1,0:T(8,128)(2,1)} %slice.61), channel_id=1, source_target_pairs={{0,3},{1,0},{2,1},{3,2},{4,7},{5,4},{6,5},{7,6},{8,11},{9,8},{10,9... | collective-permute-start | bytes 1572872 | tf_op jit(solution)/shard_map/ppermute | solution.py:30
  112.2 7.1 %copy-start.16 = (bf16[128,2048]{1,0:T(8,128)(2,1)}, bf16[128,2048]{1,0:T(8,128)(2,1)S(1)}, u32[]{:S(2)}) copy-start(bf16[128,2048]{1,0:T(8,128)(2,1)S(1)} %collective-permute-done.10.su_lo) | copy-start | bytes 1572868
  112.2 7.1 %copy-start.17 = (bf16[128,2048]{1,0:T(8,128)(2,1)}, bf16[128,2048]{1,0:T(8,128)(2,1)S(1)}, u32[]{:S(2)}) copy-start(bf16[128,2048]{1,0:T(8,128)(2,1)S(1)} %collective-permute-done.11.su_hi) | copy-start | bytes 1572868
  119.3 24.8 %collective-permute-start.13 = (bf16[256,2048]{1,0:T(8,128)(2,1)}, bf16[256,2048]{1,0:T(8,128)(2,1)S(1)}, u32[]{:S(2)}, u32[]{:S(2)}) collective-permute-start(bf16[256,2048]{1,0:T(8,128)(2,1)} %get-tuple-element.88), channel_id=1, source_target_pairs={{0,4},{1,5},{2,6},{3,7},{4,8},{5,9},{6,10},{7,11},{8,12},{9,13},{1... | collective-permute-start | bytes 3145736 | tf_op jit(solution)/shard_map/ppermute | solution.py:30
  119.4 24.7 %collective-permute-start.14 = (bf16[256,2048]{1,0:T(8,128)(2,1)}, bf16[256,2048]{1,0:T(8,128)(2,1)S(1)}, u32[]{:S(2)}, u32[]{:S(2)}) collective-permute-start(bf16[256,2048]{1,0:T(8,128)(2,1)} %get-tuple-element.91), channel_id=1, source_target_pairs={{0,12},{1,13},{2,14},{3,15},{4,0},{5,1},{6,2},{7,3},{8,4},{9,5},{1... | collective-permute-start | bytes 3145736 | tf_op jit(solution)/shard_map/ppermute | solution.py:30
  125.7 18.3 %copy-start.14 = (bf16[256,2048]{1,0:T(8,128)(2,1)S(1)}, bf16[256,2048]{1,0:T(8,128)(2,1)}, u32[]{:S(2)}) copy-start(bf16[256,2048]{1,0:T(8,128)(2,1)} %get-tuple-element.105) | copy-start | bytes 3145732
  144.0 9.3 %copy-start.12 = (bf16[256,2048]{1,0:T(8,128)(2,1)}, bf16[256,2048]{1,0:T(8,128)(2,1)S(1)}, u32[]{:S(2)}) copy-start(bf16[256,2048]{1,0:T(8,128)(2,1)S(1)} %collective-permute-done.13.pl_hi) | copy-start | bytes 3145732
  144.0 9.3 %copy-start.13 = (bf16[256,2048]{1,0:T(8,128)(2,1)}, bf16[256,2048]{1,0:T(8,128)(2,1)S(1)}, u32[]{:S(2)}) copy-start(bf16[256,2048]{1,0:T(8,128)(2,1)S(1)} %collective-permute-done.14.pl_lo) | copy-start | bytes 3145732
  145.7 12.6 %collective-permute-start.15 = (bf16[128,2048]{1,0:T(8,128)(2,1)}, bf16[128,2048]{1,0:T(8,128)(2,1)S(1)}, u32[]{:S(2)}, u32[]{:S(2)}) collective-permute-start(bf16[128,2048]{1,0:T(8,128)(2,1)} %get-tuple-element.137), channel_id=1, source_target_pairs={{0,4},{1,5},{2,6},{3,7},{4,8},{5,9},{6,10},{7,11},{8,12},{9,13},{1... | collective-permute-start | bytes 1572872 | tf_op jit(solution)/shard_map/ppermute | solution.py:30
  145.7 12.6 %collective-permute-start.16 = (bf16[128,2048]{1,0:T(8,128)(2,1)}, bf16[128,2048]{1,0:T(8,128)(2,1)S(1)}, u32[]{:S(2)}, u32[]{:S(2)}) collective-permute-start(bf16[128,2048]{1,0:T(8,128)(2,1)} %get-tuple-element.136), channel_id=1, source_target_pairs={{0,12},{1,13},{2,14},{3,15},{4,0},{5,1},{6,2},{7,3},{8,4},{9,5},{1... | collective-permute-start | bytes 1572872 | tf_op jit(solution)/shard_map/ppermute | solution.py:30
  164.2 5.1 %collective-permute-start.17 = (bf16[32,8192]{1,0:T(8,128)(2,1)}, bf16[32,8192]{1,0:T(8,128)(2,1)S(1)}, u32[]{:S(2)}, u32[]{:S(2)}) collective-permute-start(bf16[32,8192]{1,0:T(8,128)(2,1)} %get-tuple-element.127), channel_id=1, source_target_pairs={{0,16},{16,0},{32,48},{48,32},{64,80},{80,64},{96,112},{112,96},{1... | collective-permute-start | bytes 1572872 | tf_op jit(solution)/shard_map/ppermute | solution.py:39
  170.6 7.7 %collective-permute-start.18 = (bf16[16,8192]{1,0:T(8,128)(2,1)S(1)}, bf16[16,8192]{1,0:T(8,128)(2,1)S(1)}, u32[]{:S(2)}, u32[]{:S(2)}) collective-permute-start(bf16[16,8192]{1,0:T(8,128)(2,1)S(1)} %get-tuple-element.142), channel_id=1, source_target_pairs={{0,32},{16,48},{32,0},{48,16},{64,96},{80,112},{96,64},{112,80},{1... | collective-permute-start | bytes 786440 | tf_op jit(solution)/shard_map/ppermute | solution.py:39
  172.0 21.0 %copy-start.2 = (f32[128,8192]{1,0:T(8,128)S(1)}, f32[128,8192]{1,0:T(8,128)}, u32[]{:S(2)}) copy-start(f32[128,8192]{1,0:T(8,128)} %get-tuple-element.128.merged.refs_5_) | copy-start | bytes 12582916
  172.0 21.0 %copy-start.5 = (s32[3]{0:T(128)S(1)}, s32[3]{0:T(128)}, u32[]{:S(2)}) copy-start(s32[3]{0:T(128)} %pad_add_fusion.spots.refs_0_) | copy-start | bytes 40
  172.0 8.5 %collective-permute-start.20 = (bf16[16,8192]{1,0:T(8,128)(2,1)S(1)}, bf16[16,8192]{1,0:T(8,128)(2,1)S(1)}, u32[]{:S(2)}, u32[]{:S(2)}) collective-permute-start(bf16[16,8192]{1,0:T(8,128)(2,1)S(1)} %get-tuple-element.143), channel_id=1, source_target_pairs={{0,96},{16,112},{32,64},{48,80},{64,32},{80,48},{96,0},{112,16},{1... | collective-permute-start | bytes 786440 | tf_op jit(solution)/shard_map/ppermute | solution.py:39
  180.6 7.8 %collective-permute-start.19 = (bf16[16,8192]{1,0:T(8,128)(2,1)S(1)}, bf16[16,8192]{1,0:T(8,128)(2,1)S(1)}, u32[]{:S(2)}, u32[]{:S(2)}) collective-permute-start(bf16[16,8192]{1,0:T(8,128)(2,1)S(1)} %get-tuple-element.140), channel_id=1, source_target_pairs={{0,96},{16,112},{32,64},{48,80},{64,32},{80,48},{96,0},{112,16},{1... | collective-permute-start | bytes 786440 | tf_op jit(solution)/shard_map/ppermute | solution.py:39
  182.5 6.2 %collective-permute-start.21 = (bf16[16,8192]{1,0:T(8,128)(2,1)S(1)}, bf16[16,8192]{1,0:T(8,128)(2,1)S(1)}, u32[]{:S(2)}, u32[]{:S(2)}) collective-permute-start(bf16[16,8192]{1,0:T(8,128)(2,1)S(1)} %get-tuple-element.141), channel_id=1, source_target_pairs={{0,32},{16,48},{32,0},{48,16},{64,96},{80,112},{96,64},{112,80},{1... | collective-permute-start | bytes 786440 | tf_op jit(solution)/shard_map/ppermute | solution.py:39
  188.8 6.6 %copy-start.3 = (bf16[32,8192]{1,0:T(8,128)(2,1)}, bf16[32,8192]{1,0:T(8,128)(2,1)S(1)}, u32[]{:S(2)}) copy-start(bf16[32,8192]{1,0:T(8,128)(2,1)S(1)} %pad_maximum_fusion.mine.refs_3_) | copy-start | bytes 1572868
  188.8 4.1 %collective-permute-start.22 = (bf16[32,8192]{1,0:T(8,128)(2,1)S(1)}, bf16[32,8192]{1,0:T(8,128)(2,1)S(1)}, u32[]{:S(2)}, u32[]{:S(2)}) collective-permute-start(bf16[32,8192]{1,0:T(8,128)(2,1)S(1)} %pad_maximum_fusion.mine.refs_3_), channel_id=1, source_target_pairs={{0,16},{16,0},{32,48},{48,32},{64,80},{80,64},{96,112},{112,96},{1... | collective-permute-start | bytes 1572872 | tf_op jit(solution)/shard_map/ppermute | solution.py:39
  192.9 2.5 %copy-start.4 = (bf16[32,8192]{1,0:T(8,128)(2,1)}, bf16[32,8192]{1,0:T(8,128)(2,1)S(1)}, u32[]{:S(2)}) copy-start(bf16[32,8192]{1,0:T(8,128)(2,1)S(1)} %collective-permute-done.22.theirs.refs_4_) | copy-start | bytes 1572868
  195.5 1.4 collective-permute-start.23
  196.9 10.2 %collective-permute-start.24 = (f32[128,64]{1,0:T(8,128)S(1)}, f32[128,64]{1,0:T(8,128)S(1)}, u32[]{:S(2)}, u32[]{:S(2)}) collective-permute-start(f32[128,64]{1,0:T(8,128)S(1)} %add.64), channel_id=1, source_target_pairs={{0,64},{16,80},{32,96},{48,112},{64,0},{80,16},{96,32},{112,48},{1... | collective-permute-start | bytes 98312 | tf_op jit(solution)/shard_map/ppermute | solution.py:39
  197.5 9.5 %collective-permute-start.25 = (f32[128,64]{1,0:T(8,128)S(1)}, f32[128,64]{1,0:T(8,128)S(1)}, u32[]{:S(2)}, u32[]{:S(2)}) collective-permute-start(f32[128,64]{1,0:T(8,128)S(1)} %add.64), channel_id=1, source_target_pairs={{0,32},{16,48},{32,64},{48,80},{64,96},{80,112},{96,0},{112,16},{1... | collective-permute-start | bytes 98312 | tf_op jit(solution)/shard_map/ppermute | solution.py:39
  198.8 8.2 %collective-permute-start.26 = (f32[128,64]{1,0:T(8,128)S(1)}, f32[128,64]{1,0:T(8,128)S(1)}, u32[]{:S(2)}, u32[]{:S(2)}) collective-permute-start(f32[128,64]{1,0:T(8,128)S(1)} %add.64), channel_id=1, source_target_pairs={{0,96},{16,112},{32,0},{48,16},{64,32},{80,48},{96,64},{112,80},{1... | collective-permute-start | bytes 98312 | tf_op jit(solution)/shard_map/ppermute | solution.py:39
  207.1 7.6 %copy-start.1 = (bf16[8192,128]{1,0:T(8,128)(2,1)S(1)}, bf16[8192,128]{1,0:T(8,128)(2,1)}, u32[]{:S(2)}) copy-start(bf16[8192,128]{1,0:T(8,128)(2,1)} %param.7) | copy-start | bytes 6291460
  (6 other events, 6.4 us)
Sparse Core Ops, SparseCore 0:
  10.3 54.0 all-gather.2
  119.4 79.6 reduce-scatter.1

commit v3 on v2

--- a/solution.py
+++ b/solution.py
@@ -11,8 +11,8 @@
 TILE = 2048
 WIDE = 2048
 LONG = 4096
-VMEM = 40 * 1024 * 1024
-PART = 1024
+VMEM = 24 * 1024 * 1024
+PART = 2048
 F32 = jnp.float32
 BF16 = jnp.bfloat16
 HI = lax.Precision.HIGHEST
@@ -188,6 +188,7 @@
         ),
         out_shape=jax.ShapeDtypeStruct((flat, 2 * piece), BF16),
         cost_estimate=cost(4 * piece * SIDE * flat * HD, 18 * piece * HD * 2),
+        compiler_params=pltpu.CompilerParams(vmem_limit_bytes=VMEM),
         name="input_parts",
     )(spots, *gathered, cots)
 

time: 222 us -> 221 us (level)
  Pallas kernels: 59 us -> 53.8 us
  other arithmetic: 6.55 us -> 9.62 us
    pallas_call x1, Pallas kernels: 12.2 us -> 7.43 us  [input_parts(): pl.pallas_call(input_kernel, grid_spec=pltpu.PrefetchScalarGridSpec(num_s...]
    convert_element_type x2, other arithmetic: 3.01 us -> 6.07 us  [scatter_far(): sum_down = step((high(rest) + high(got_down)).astype(BF16), -1)]
    unnamed x49 -> x43, local copies, waits for them, and re-layouts: 8.34 us -> 9.81 us
  transfers between devices with their start and end apart: 30 -> 30, of which waited for: 14 -> 15; matrix products, arithmetic and copies ran while one was open for 8% -> 9% of each run, Pallas kernels for 24% -> 22%
where the time goes in v3:
time: 221 us; the launch traced here: 220 us
  waiting for transfers between devices  77.4 us (35%)
  Pallas kernels  53.8 us (24%)
  starting transfers between devices  48 us (22%)
  local copies, waits for them, and re-layouts  17.3 us (8%)
  between operations  14.3 us (6%)
  other arithmetic  9.62 us (4%)
    ppermute x16, waiting for transfers between devices, along_tensor(): return lax.ppermute(array, 'tensor', perm)  57.3 us
    ppermute x16, starting transfers between devices, along_tensor(): return lax.ppermute(array, 'tensor', perm)  24.5 us
    ppermute x11, starting transfers between devices, along_dp(): return lax.ppermute(array, 'dp', perm)  18.4 us
    ppermute x11, waiting for transfers between devices, along_dp(): return lax.ppermute(array, 'dp', perm)  17 us
    pallas_call x2, Pallas kernels, grad_parts(): pl.pallas_call(grad_kernel, grid=(width // TILE,), in_specs=[cols_spec(pi...  10.8 us
    pallas_call x2, Pallas kernels, merge(): pl.pallas_call(merge_kernel, grid=(steps,), in_specs=[shifted(HD), cols_s...  9.88 us
    unnamed x43, local copies, waits for them, and re-layouts  9.81 us
    pallas_call x1, Pallas kernels, input_parts(): pl.pallas_call(input_kernel, grid_spec=pltpu.PrefetchScalarGridSpec(num_s...  7.43 us
  transfers between devices with their start and end apart: 30, of which 15 were waited for; matrix products, arithmetic and copies ran while one was open for 9% of the time, Pallas kernels for 22%

profile of v3, /device:TPU:1, one launch (start us, length us, event | category | flops | bytes accessed | tf_op | source)
XLA Modules:
  0.0 220.4 jit_solution(14852201048966103089)
XLA Ops:
  7.2 1.5 copy-done
  9.8 1.7 fusion
  11.6 2.2 collective-permute-start
  13.8 1.5 collective-permute-start.1
  15.3 5.0 %all-to-all-start = ((bf16[4,512,128]{2,1,0:T(8,128)(2,1)}), bf16[4,512,128]{2,1,0:T(8,128)(2,1)S(1)}, u32[]{:S(2)}, u32[]{:S(2)}) async-start(bf16[4,512,128]{2,1,0:T(8,128)(2,1)} %bitcast.2), calls=%async_computation | async-start | bytes 1048576 | tf_op jit(solution)/shard_map/all_to_all | solution.py:415
  20.3 4.1 %copy.12 = bf16[8192,128]{0,1:T(8,128)(2,1)} copy(bf16[8192,128]{1,0:T(8,128)(2,1)} %param.8) | data formatting | bytes 4194304 | tf_op args[3]
  25.1 3.1 %all-to-all-done.cots = bf16[4,512,128]{2,1,0:T(8,128)(2,1)S(1)} async-done(((bf16[4,512,128]{2,1,0:T(8,128)(2,1)}), bf16[4,512,128]{2,1,0:T(8,128)(2,1)S(1)}, u32[]{:S(2)}, u32[]{:S(2)}) %all-to-all-start) | async-done | bytes 524320 | tf_op jit(solution)/shard_map/all_to_all | solution.py:415
  28.2 9.9 %collective-permute-done.a3 = bf16[128,4096]{1,0:T(8,128)(2,1)} collective-permute-done((bf16[128,4096]{1,0:T(8,128)(2,1)S(1)}, bf16[128,4096]{1,0:T(8,128)(2,1)}, u32[]{:S(2)}, u32[]{:S(2)}) %collective-permute-start) | collective-permute-done | bytes 1048608 | tf_op jit(solution)/shard_map/ppermute | solution.py:30
  41.1 1.9 collective-permute-start.3
  43.7 2.1 turn_cots.1.cturn
  45.8 6.8 %collective-permute-done.2.a2lo = bf16[64,4096]{1,0:T(8,128)(2,1)S(1)} collective-permute-done((bf16[64,4096]{1,0:T(8,128)(2,1)S(1)}, bf16[64,4096]{1,0:T(8,128)(2,1)S(1)}, u32[]{:S(2)}, u32[]{:S(2)}) %collective-permute-start.2) | collective-permute-done | bytes 524320 | tf_op jit(solution)/shard_map/ppermute | solution.py:30
  53.7 2.4 %collective-permute-start.5 = (bf16[128,4096]{1,0:T(8,128)(2,1)S(1)}, bf16[128,4096]{1,0:T(8,128)(2,1)}, u32[]{:S(2)}, u32[]{:S(2)}) collective-permute-start(bf16[128,4096]{1,0:T(8,128)(2,1)S(1)} %get-tuple-element.97.a0), channel_id=1, source_target_pairs={{0,3},{1,0},{2,1},{3,2},{4,7},{5,4},{6,5},{7,6},{8,11},{9,8},{10,9... | collective-permute-start | bytes 3145736 | tf_op jit(solution)/shard_map/ppermute | solution.py:30
  56.1 5.4 %grad_parts.2 = (bf16[256,2048]{1,0:T(8,128)(2,1)}, bf16[256,2048]{1,0:T(8,128)(2,1)}, bf16[256,2048]{1,0:T(8,128)(2,1)}) custom-call(bf16[128,4096]{1,0:T(8,128)(2,1)} %copy-done.11, bf16[128,4096]{1,0:T(8,128)(2,1)} %collective-permute-done.1.a1, bf16[64,4096]{1,0:T(8,128)(2,1)} %copy-done.19, bf16[64,4096]{1,0:T(8,128)(2,1)} %collective-permute-done.3.a2hi, ...), custom_call_target="tpu_custom_call" | custom-call | flops 2147483648 | bytes 9437184 | tf_op jit(solution)/shard_map/grad_parts/pallas_call | solution.py:147
  61.5 1.4 collective-permute-start.6
  62.9 2.2 collective-permute-start.7
  65.1 12.0 %collective-permute-done.4.a3 = bf16[128,4096]{1,0:T(8,128)(2,1)} collective-permute-done((bf16[128,4096]{1,0:T(8,128)(2,1)S(1)}, bf16[128,4096]{1,0:T(8,128)(2,1)}, u32[]{:S(2)}, u32[]{:S(2)}) %collective-permute-start.4) | collective-permute-done | bytes 1048608 | tf_op jit(solution)/shard_map/ppermute | solution.py:30
  77.1 8.7 %collective-permute-done.6.pl_hi = bf16[256,2048]{1,0:T(8,128)(2,1)S(1)} collective-permute-done((bf16[256,2048]{1,0:T(8,128)(2,1)}, bf16[256,2048]{1,0:T(8,128)(2,1)S(1)}, u32[]{:S(2)}, u32[]{:S(2)}) %collective-permute-start.6) | collective-permute-done | bytes 1048608 | tf_op jit(solution)/shard_map/ppermute | solution.py:30
  85.7 3.7 %collective-permute-start.12 = (bf16[4,4096,128]{2,1,0:T(8,128)(2,1)}, bf16[4,4096,128]{2,1,0:T(8,128)(2,1)S(1)}, u32[]{:S(2)}, u32[]{:S(2)}) collective-permute-start(bf16[4,4096,128]{2,1,0:T(8,128)(2,1)} %bitcast.9), channel_id=1, source_target_pairs={{0,16},{16,0},{32,48},{48,32},{64,80},{80,64},{96,112},{112,96},{1... | collective-permute-start | bytes 12582920 | tf_op jit(solution)/shard_map/ppermute | solution.py:39
  92.0 2.7 %add_convert_fusion.3 = (bf16[128,2048]{1,0:T(8,128)(2,1)}, bf16[128,2048]{1,0:T(8,128)(2,1)}) fusion(bf16[256,2048]{1,0:T(8,128)(2,1)} %collective-permute-done.7.pl_lo, bf16[256,2048]{1,0:T(8,128)(2,1)} %get-tuple-element.79, bf16[256,2048]{1,0:T(8,128)(2,1)S(1)} %collective-permute-done.6.pl_hi), kind=kLoop, calls=%fused_computation.3 | loop fusion | flops 2097152 | bytes 3145728 | tf_op jit(solution)/shard_map/convert_element_type | solution.py:371
  95.7 1.8 collective-permute-start.11
  97.5 2.7 %collective-permute-start.9 = (bf16[64,4096]{1,0:T(8,128)(2,1)S(1)}, bf16[64,4096]{1,0:T(8,128)(2,1)}, u32[]{:S(2)}, u32[]{:S(2)}) collective-permute-start(bf16[64,4096]{1,0:T(8,128)(2,1)S(1)} %slice.61), channel_id=1, source_target_pairs={{0,3},{1,0},{2,1},{3,2},{4,7},{5,4},{6,5},{7,6},{8,11},{9,8},{10,9... | collective-permute-start | bytes 1572872 | tf_op jit(solution)/shard_map/ppermute | solution.py:30
  100.2 7.4 %input_parts.1 = bf16[512,8192]{1,0:T(8,128)(2,1)S(1)} custom-call(s32[3]{0:T(128)S(1)} %copy-done.9, bf16[4,4096,128]{2,1,0:T(8,128)(2,1)S(1)} %bitcast.10, bf16[4,4096,128]{2,1,0:T(8,128)(2,1)S(1)} %collective-permute-done.12.theirs, bf16[4,512,128]{2,1,0:T(8,128)(2,1)S(1)} %copy-done.5), custom_call_target="tpu_custom_call" | custom-call | flops 4294967296 | bytes 18874368 | tf_op jit(solution)/shard_map/input_parts/pallas_call | solution.py:177
  107.6 3.3 %copy-done.3 = bf16[512,8192]{1,0:T(8,128)(2,1)} copy-done((bf16[512,8192]{1,0:T(8,128)(2,1)}, bf16[512,8192]{1,0:T(8,128)(2,1)S(1)}, u32[]{:S(2)}) %copy-start.3) | copy-done | bytes 8388632
  111.5 5.4 %grad_parts.3 = (bf16[256,2048]{1,0:T(8,128)(2,1)}, bf16[256,2048]{1,0:T(8,128)(2,1)}, bf16[256,2048]{1,0:T(8,128)(2,1)}) custom-call(bf16[128,4096]{1,0:T(8,128)(2,1)} %copy-done.12, bf16[128,4096]{1,0:T(8,128)(2,1)} %collective-permute-done.5.a1, bf16[64,4096]{1,0:T(8,128)(2,1)} %collective-permute-done.8.a2lo, ...), custom_call_target="tpu_custom_call" | custom-call | flops 2147483648 | bytes 9437184 | tf_op jit(solution)/shard_map/grad_parts/pallas_call | solution.py:147
  117.0 2.7 %collective-permute-start.14 = (bf16[256,2048]{1,0:T(8,128)(2,1)}, bf16[256,2048]{1,0:T(8,128)(2,1)S(1)}, u32[]{:S(2)}, u32[]{:S(2)}) collective-permute-start(bf16[256,2048]{1,0:T(8,128)(2,1)} %get-tuple-element.91), channel_id=1, source_target_pairs={{0,12},{1,13},{2,14},{3,15},{4,0},{5,1},{6,2},{7,3},{8,4},{9,5},{1... | collective-permute-start | bytes 3145736 | tf_op jit(solution)/shard_map/ppermute | solution.py:30
  119.7 3.7 %own_part.3.own = f32[128,4096]{1,0:T(8,128)} custom-call(bf16[128,4096]{1,0:T(8,128)(2,1)} %copy-done.12, bf16[128,4096]{1,0:T(8,128)(2,1)} %collective-permute-done.5.a1, bf16[64,4096]{1,0:T(8,128)(2,1)} %collective-permute-done.8.a2lo, bf16[64,4096]{1,0:T(8,128)(2,1)} %collective-permute-done.9.a2hi, bf16[128,4096]{1,0:T(8,128)(2,1)} %collective-permute-done.4.a3, ...), custom_call_target="tpu_custom_call" | custom-call | flops 536870912 | bytes 6291456 | tf_op jit(solution)/shard_map/own_part/pallas_call | solution.py:109
  123.4 3.7 %own_part.2.own = f32[128,4096]{1,0:T(8,128)} custom-call(bf16[128,4096]{1,0:T(8,128)(2,1)} %copy-done.11, bf16[128,4096]{1,0:T(8,128)(2,1)} %collective-permute-done.1.a1, bf16[64,4096]{1,0:T(8,128)(2,1)} %copy-done.19, bf16[64,4096]{1,0:T(8,128)(2,1)} %collective-permute-done.3.a2hi, bf16[128,4096]{1,0:T(8,128)(2,1)} %collective-permute-done.a3, ...), custom_call_target="tpu_custom_call" | custom-call | flops 536870912 | bytes 6291456 | tf_op jit(solution)/shard_map/own_part/pallas_call | solution.py:109
  127.1 14.5 %collective-permute-done.13.pl_hi = bf16[256,2048]{1,0:T(8,128)(2,1)S(1)} collective-permute-done((bf16[256,2048]{1,0:T(8,128)(2,1)}, bf16[256,2048]{1,0:T(8,128)(2,1)S(1)}, u32[]{:S(2)}, u32[]{:S(2)}) %collective-permute-start.13) | collective-permute-done | bytes 1048608 | tf_op jit(solution)/shard_map/ppermute | solution.py:30
  141.6 3.3 %add_convert_fusion.1 = (bf16[128,2048]{1,0:T(8,128)(2,1)}, bf16[128,2048]{1,0:T(8,128)(2,1)}) fusion(bf16[256,2048]{1,0:T(8,128)(2,1)S(1)} %collective-permute-done.14.pl_lo, bf16[256,2048]{1,0:T(8,128)(2,1)} %get-tuple-element.105, bf16[256,2048]{1,0:T(8,128)(2,1)S(1)} %collective-permute-done.13.pl_hi), kind=kLoop, calls=%fused_computation.1 | loop fusion | flops 2097152 | bytes 3145728 | tf_op jit(solution)/shard_map/convert_element_type | solution.py:371
  144.9 2.7 %collective-permute-start.16 = (bf16[128,2048]{1,0:T(8,128)(2,1)}, bf16[128,2048]{1,0:T(8,128)(2,1)}, u32[]{:S(2)}, u32[]{:S(2)}) collective-permute-start(bf16[128,2048]{1,0:T(8,128)(2,1)} %get-tuple-element.136), channel_id=1, source_target_pairs={{0,12},{1,13},{2,14},{3,15},{4,0},{5,1},{6,2},{7,3},{8,4},{9,5},{1... | collective-permute-start | bytes 1572872 | tf_op jit(solution)/shard_map/ppermute | solution.py:30
  147.6 4.9 %merge.2 = (f32[128,8192]{1,0:T(8,128)}, f32[32,8192]{1,0:T(8,128)}, bf16[32,8192]{1,0:T(8,128)(2,1)}) custom-call(bf16[128,8192]{1,0:T(8,128)(2,1)} %bitcast.11, f32[128,4096]{1,0:T(8,128)} %own_part.2.own, bf16[256,2048]{1,0:T(8,128)(2,1)} %collective-permute-done.7.pl_lo, bf16[256,2048]{1,0:T(8,128)(2,1)} %copy-done.13, bf16[128,2048]{1,0:T(8,128)(2,1)} %copy-done.16, ...), custom_call_target="tpu_custom_call" | custom-call | flops 201326592 | bytes 7340032 | tf_op jit(solution)/shard_map/merge/pallas_call | solution.py:228
  152.5 4.9 %collective-permute-done.15.su_lo = bf16[128,2048]{1,0:T(8,128)(2,1)S(1)} collective-permute-done((bf16[128,2048]{1,0:T(8,128)(2,1)}, bf16[128,2048]{1,0:T(8,128)(2,1)S(1)}, u32[]{:S(2)}, u32[]{:S(2)}) %collective-permute-start.15) | collective-permute-done | bytes 524320 | tf_op jit(solution)/shard_map/ppermute | solution.py:30
  158.2 5.0 %merge.3 = (f32[128,8192]{1,0:T(8,128)}, f32[32,8192]{1,0:T(8,128)}, bf16[32,8192]{1,0:T(8,128)(2,1)}) custom-call(bf16[128,8192]{1,0:T(8,128)(2,1)} %bitcast.12, f32[128,4096]{1,0:T(8,128)} %own_part.3.own, bf16[256,2048]{1,0:T(8,128)(2,1)} %copy-done.15, bf16[256,2048]{1,0:T(8,128)(2,1)} %copy-done.14, ...), custom_call_target="tpu_custom_call", output_to_operand_aliasing={{0}: (7, {}), {1}: (8, {}), {2}: (9, {})} | custom-call | flops 201326592 | bytes 7340032 | tf_op jit(solution)/shard_map/merge/pallas_call | solution.py:228
  163.2 3.3 %collective-permute-start.17 = (bf16[32,8192]{1,0:T(8,128)(2,1)}, bf16[32,8192]{1,0:T(8,128)(2,1)S(1)}, u32[]{:S(2)}, u32[]{:S(2)}) collective-permute-start(bf16[32,8192]{1,0:T(8,128)(2,1)} %get-tuple-element.127), channel_id=1, source_target_pairs={{0,16},{16,0},{32,48},{48,32},{64,80},{80,64},{96,112},{112,96},{1... | collective-permute-start | bytes 1572872 | tf_op jit(solution)/shard_map/ppermute | solution.py:39
  166.5 1.7 collective-permute-done.17
  168.2 1.3 add_convert_fusion
  169.6 1.3 collective-permute-start.18
  170.9 1.8 collective-permute-start.20
  172.7 4.6 %collective-permute-done.18 = bf16[16,8192]{1,0:T(8,128)(2,1)S(1)} collective-permute-done((bf16[16,8192]{1,0:T(8,128)(2,1)S(1)}, bf16[16,8192]{1,0:T(8,128)(2,1)S(1)}, u32[]{:S(2)}, u32[]{:S(2)}) %collective-permute-start.18) | collective-permute-done | bytes 262176 | tf_op jit(solution)/shard_map/ppermute | solution.py:39
  177.3 2.1 collective-permute-done.20
  179.5 1.9 collective-permute-start.19
  181.4 5.9 %collective-permute-done.19 = bf16[16,8192]{1,0:T(8,128)(2,1)S(1)} collective-permute-done((bf16[16,8192]{1,0:T(8,128)(2,1)S(1)}, bf16[16,8192]{1,0:T(8,128)(2,1)S(1)}, u32[]{:S(2)}, u32[]{:S(2)}) %collective-permute-start.19) | collective-permute-done | bytes 262176 | tf_op jit(solution)/shard_map/ppermute | solution.py:39
  187.8 2.6 %collective-permute-start.22 = (bf16[32,8192]{1,0:T(8,128)(2,1)S(1)}, bf16[32,8192]{1,0:T(8,128)(2,1)S(1)}, u32[]{:S(2)}, u32[]{:S(2)}) collective-permute-start(bf16[32,8192]{1,0:T(8,128)(2,1)S(1)} %pad_maximum_fusion.mine.refs_3_), channel_id=1, source_target_pairs={{0,16},{16,0},{32,48},{48,32},{64,80},{80,64},{96,112},{112,96},{1... | collective-permute-start | bytes 1572872 | tf_op jit(solution)/shard_map/ppermute | solution.py:39
  190.3 1.5 collective-permute-done.22.theirs.refs_4_
  191.9 2.5 %gram.1 = (f32[128,64]{1,0:T(8,128)S(1)}, f32[64,64]{1,0:T(8,128)S(1)}) custom-call(s32[3]{0:T(128)S(1)} %copy-done.9, bf16[32,8192]{1,0:T(8,128)(2,1)S(1)} %pad_maximum_fusion.mine.refs_3_, bf16[32,8192]{1,0:T(8,128)(2,1)S(1)} %collective-permute-done.22.theirs.refs_4_, f32[128,8192]{1,0:T(8,128)S(1)} %copy-done.2), custom_call_target="tpu_custom_call" | custom-call | flops 603979776 | bytes 6291456 | tf_op jit(solution)/shard_map/gram/pallas_call | solution.py:265
  197.7 1.4 collective-permute-start.26
  199.1 6.8 %inverse_factor.1.refs_1_ = f32[64,64]{1,0:T(8,128)} custom-call(f32[64,64]{1,0:T(8,128)} %copy-done.10), custom_call_target="tpu_custom_call" | custom-call | flops 104857600 | bytes 65536 | tf_op jit(solution)/shard_map/inverse_factor/pallas_call | solution.py:296
  206.6 6.9 %final.1 = (f32[64,128]{1,0:T(8,128)}, bf16[8192,128]{1,0:T(8,128)(2,1)}, bf16[8192,128]{1,0:T(8,128)(2,1)}) custom-call(s32[3]{0:T(128)} %pad_add_fusion.spots.refs_0_, f32[64,64]{1,0:T(8,128)} %inverse_factor.1.refs_1_, f32[128,64]{1,0:T(8,128)} %add_add_fusion.refs_2_, bf16[32,8192]{1,0:T(8,128)(2,1)} %copy-done.6, bf16[32,8192]{1,0:T(8,128)(2,1)} %copy-done.8, ...), custom_call_target="tpu_custom_call" | custom-call | flops 402653184 | bytes 12582912 | tf_op jit(solution)/shard_map/final/pallas_call | solution.py:322
  (87 shorter events, 16.3 us)
Async XLA Ops:
  7.2 78.5 %all-gather.3.cloned.1.call-start = ((), (), s32[]{:S(2)}) async-start(), calls=%async_computation.3 | async-start | bytes 5242880 | tf_op jit(solution)/shard_map/all_gather | solution.py:419
  11.6 12.9 %copy-start.11 = (bf16[128,4096]{1,0:T(8,128)(2,1)}, bf16[128,4096]{1,0:T(8,128)(2,1)S(1)}, u32[]{:S(2)}) copy-start(bf16[128,4096]{1,0:T(8,128)(2,1)S(1)} %get-tuple-element.92.a0) | copy-start | bytes 3145732
  11.6 42.2 %copy-start.12 = (bf16[128,4096]{1,0:T(8,128)(2,1)}, bf16[128,4096]{1,0:T(8,128)(2,1)S(1)}, u32[]{:S(2)}) copy-start(bf16[128,4096]{1,0:T(8,128)(2,1)S(1)} %get-tuple-element.97.a0) | copy-start | bytes 3145732
  11.6 26.5 %collective-permute-start = (bf16[128,4096]{1,0:T(8,128)(2,1)S(1)}, bf16[128,4096]{1,0:T(8,128)(2,1)}, u32[]{:S(2)}, u32[]{:S(2)}) collective-permute-start(bf16[128,4096]{1,0:T(8,128)(2,1)S(1)} %get-tuple-element.92.a0), channel_id=1, source_target_pairs={{0,1},{1,2},{2,3},{3,0},{4,5},{5,6},{6,7},{7,4},{8,9},{9,10},{10,1... | collective-permute-start | bytes 3145736 | tf_op jit(solution)/shard_map/ppermute | solution.py:30
  13.8 24.3 %collective-permute-start.1 = (bf16[128,4096]{1,0:T(8,128)(2,1)S(1)}, bf16[128,4096]{1,0:T(8,128)(2,1)}, u32[]{:S(2)}, u32[]{:S(2)}) collective-permute-start(bf16[128,4096]{1,0:T(8,128)(2,1)S(1)} %get-tuple-element.92.a0), channel_id=1, source_target_pairs={{0,3},{1,0},{2,1},{3,2},{4,7},{5,4},{6,5},{7,6},{8,11},{9,8},{10,9... | collective-permute-start | bytes 3145736 | tf_op jit(solution)/shard_map/ppermute | solution.py:30
  15.3 12.9 %all-to-all-start = ((bf16[4,512,128]{2,1,0:T(8,128)(2,1)}), bf16[4,512,128]{2,1,0:T(8,128)(2,1)S(1)}, u32[]{:S(2)}, u32[]{:S(2)}) async-start(bf16[4,512,128]{2,1,0:T(8,128)(2,1)} %bitcast.2), calls=%async_computation | async-start | bytes 1048576 | tf_op jit(solution)/shard_map/all_to_all | solution.py:415
  20.3 193.2 %reduce-scatter.2.cloned.1.call-start = ((), (), s32[]{:S(2)}) async-start(), calls=%async_computation.2 | async-start | bytes 10485760 | tf_op jit(solution)/shard_map/reduce_scatter | solution.py:446
  20.3 4.1 %copy-start.20 = (f32[128,64]{0,1:T(8,128)S(1)}, f32[128,64]{0,1:T(8,128)}, u32[]{:S(2)}) copy-start(f32[128,64]{0,1:T(8,128)} %param.9) | copy-start | bytes 98308
  28.2 15.5 %copy-start.4 = (bf16[4,512,128]{2,1,0:T(8,128)(2,1)}, bf16[4,512,128]{2,1,0:T(8,128)(2,1)S(1)}, u32[]{:S(2)}) copy-start(bf16[4,512,128]{2,1,0:T(8,128)(2,1)S(1)} %all-to-all-done.cots) | copy-start | bytes 1572868
  39.1 13.4 %collective-permute-start.2 = (bf16[64,4096]{1,0:T(8,128)(2,1)S(1)}, bf16[64,4096]{1,0:T(8,128)(2,1)S(1)}, u32[]{:S(2)}, u32[]{:S(2)}) collective-permute-start(bf16[64,4096]{1,0:T(8,128)(2,1)S(1)} %slice.58), channel_id=1, source_target_pairs={{0,1},{1,2},{2,3},{3,0},{4,5},{5,6},{6,7},{7,4},{8,9},{9,10},{10,1... | collective-permute-start | bytes 1572872 | tf_op jit(solution)/shard_map/ppermute | solution.py:30
  41.1 11.5 %collective-permute-start.3 = (bf16[64,4096]{1,0:T(8,128)(2,1)S(1)}, bf16[64,4096]{1,0:T(8,128)(2,1)}, u32[]{:S(2)}, u32[]{:S(2)}) collective-permute-start(bf16[64,4096]{1,0:T(8,128)(2,1)S(1)} %slice.59), channel_id=1, source_target_pairs={{0,3},{1,0},{2,1},{3,2},{4,7},{5,4},{6,5},{7,6},{8,11},{9,8},{10,9... | collective-permute-start | bytes 1572872 | tf_op jit(solution)/shard_map/ppermute | solution.py:30
  52.5 3.6 %copy-start.19 = (bf16[64,4096]{1,0:T(8,128)(2,1)}, bf16[64,4096]{1,0:T(8,128)(2,1)S(1)}, u32[]{:S(2)}) copy-start(bf16[64,4096]{1,0:T(8,128)(2,1)S(1)} %collective-permute-done.2.a2lo) | copy-start | bytes 1572868
  52.6 24.5 %collective-permute-start.4 = (bf16[128,4096]{1,0:T(8,128)(2,1)S(1)}, bf16[128,4096]{1,0:T(8,128)(2,1)}, u32[]{:S(2)}, u32[]{:S(2)}) collective-permute-start(bf16[128,4096]{1,0:T(8,128)(2,1)S(1)} %get-tuple-element.97.a0), channel_id=1, source_target_pairs={{0,1},{1,2},{2,3},{3,0},{4,5},{5,6},{6,7},{7,4},{8,9},{9,10},{10,1... | collective-permute-start | bytes 3145736 | tf_op jit(solution)/shard_map/ppermute | solution.py:30
  53.7 23.3 %collective-permute-start.5 = (bf16[128,4096]{1,0:T(8,128)(2,1)S(1)}, bf16[128,4096]{1,0:T(8,128)(2,1)}, u32[]{:S(2)}, u32[]{:S(2)}) collective-permute-start(bf16[128,4096]{1,0:T(8,128)(2,1)S(1)} %get-tuple-element.97.a0), channel_id=1, source_target_pairs={{0,3},{1,0},{2,1},{3,2},{4,7},{5,4},{6,5},{7,6},{8,11},{9,8},{10,9... | collective-permute-start | bytes 3145736 | tf_op jit(solution)/shard_map/ppermute | solution.py:30
  61.5 24.2 %collective-permute-start.6 = (bf16[256,2048]{1,0:T(8,128)(2,1)}, bf16[256,2048]{1,0:T(8,128)(2,1)S(1)}, u32[]{:S(2)}, u32[]{:S(2)}) collective-permute-start(bf16[256,2048]{1,0:T(8,128)(2,1)} %get-tuple-element.73), channel_id=1, source_target_pairs={{0,4},{1,5},{2,6},{3,7},{4,8},{5,9},{6,10},{7,11},{8,12},{9,13},{1... | collective-permute-start | bytes 3145736 | tf_op jit(solution)/shard_map/ppermute | solution.py:30
  62.9 22.8 %collective-permute-start.7 = (bf16[256,2048]{1,0:T(8,128)(2,1)}, bf16[256,2048]{1,0:T(8,128)(2,1)}, u32[]{:S(2)}, u32[]{:S(2)}) collective-permute-start(bf16[256,2048]{1,0:T(8,128)(2,1)} %get-tuple-element.76), channel_id=1, source_target_pairs={{0,12},{1,13},{2,14},{3,15},{4,0},{5,1},{6,2},{7,3},{8,4},{9,5},{1... | collective-permute-start | bytes 3145736 | tf_op jit(solution)/shard_map/ppermute | solution.py:30
  85.7 9.0 %copy-start.13 = (bf16[256,2048]{1,0:T(8,128)(2,1)}, bf16[256,2048]{1,0:T(8,128)(2,1)S(1)}, u32[]{:S(2)}) copy-start(bf16[256,2048]{1,0:T(8,128)(2,1)S(1)} %collective-permute-done.6.pl_hi) | copy-start | bytes 3145732
  85.7 14.4 %collective-permute-start.12 = (bf16[4,4096,128]{2,1,0:T(8,128)(2,1)}, bf16[4,4096,128]{2,1,0:T(8,128)(2,1)S(1)}, u32[]{:S(2)}, u32[]{:S(2)}) collective-permute-start(bf16[4,4096,128]{2,1,0:T(8,128)(2,1)} %bitcast.9), channel_id=1, source_target_pairs={{0,16},{16,0},{32,48},{48,32},{64,80},{80,64},{96,112},{112,96},{1... | collective-permute-start | bytes 12582920 | tf_op jit(solution)/shard_map/ppermute | solution.py:39
  89.4 10.7 %copy-start.7 = (bf16[16384,128]{1,0:T(8,128)(2,1)S(1)}, bf16[16384,128]{1,0:T(8,128)(2,1)}, u32[]{:S(2)}) copy-start(bf16[16384,128]{1,0:T(8,128)(2,1)} %all-gather.3.cloned.1.call-done) | copy-start | bytes 12582916
  90.7 9.5 %copy-start.5 = (bf16[4,512,128]{2,1,0:T(8,128)(2,1)S(1)}, bf16[4,512,128]{2,1,0:T(8,128)(2,1)}, u32[]{:S(2)}) copy-start(bf16[4,512,128]{2,1,0:T(8,128)(2,1)} %copy-done.4) | copy-start | bytes 1572868
  90.7 9.5 %copy-start.9 = (s32[3]{0:T(128)S(1)}, s32[3]{0:T(128)}, u32[]{:S(2)}) copy-start(s32[3]{0:T(128)} %pad_add_fusion.spots.refs_0_) | copy-start | bytes 40
  94.7 16.2 %collective-permute-start.10 = (bf16[128,2048]{1,0:T(8,128)(2,1)}, bf16[128,2048]{1,0:T(8,128)(2,1)S(1)}, u32[]{:S(2)}, u32[]{:S(2)}) collective-permute-start(bf16[128,2048]{1,0:T(8,128)(2,1)} %get-tuple-element.139), channel_id=1, source_target_pairs={{0,4},{1,5},{2,6},{3,7},{4,8},{5,9},{6,10},{7,11},{8,12},{9,13},{1... | collective-permute-start | bytes 1572872 | tf_op jit(solution)/shard_map/ppermute | solution.py:30
  95.7 15.2 %collective-permute-start.11 = (bf16[128,2048]{1,0:T(8,128)(2,1)}, bf16[128,2048]{1,0:T(8,128)(2,1)S(1)}, u32[]{:S(2)}, u32[]{:S(2)}) collective-permute-start(bf16[128,2048]{1,0:T(8,128)(2,1)} %get-tuple-element.138), channel_id=1, source_target_pairs={{0,12},{1,13},{2,14},{3,15},{4,0},{5,1},{6,2},{7,3},{8,4},{9,5},{1... | collective-permute-start | bytes 1572872 | tf_op jit(solution)/shard_map/ppermute | solution.py:30
  97.5 14.0 %collective-permute-start.8 = (bf16[64,4096]{1,0:T(8,128)(2,1)S(1)}, bf16[64,4096]{1,0:T(8,128)(2,1)}, u32[]{:S(2)}, u32[]{:S(2)}) collective-permute-start(bf16[64,4096]{1,0:T(8,128)(2,1)S(1)} %slice.60), channel_id=1, source_target_pairs={{0,1},{1,2},{2,3},{3,0},{4,5},{5,6},{6,7},{7,4},{8,9},{9,10},{10,1... | collective-permute-start | bytes 1572872 | tf_op jit(solution)/shard_map/ppermute | solution.py:30
  97.5 14.0 %collective-permute-start.9 = (bf16[64,4096]{1,0:T(8,128)(2,1)S(1)}, bf16[64,4096]{1,0:T(8,128)(2,1)}, u32[]{:S(2)}, u32[]{:S(2)}) collective-permute-start(bf16[64,4096]{1,0:T(8,128)(2,1)S(1)} %slice.61), channel_id=1, source_target_pairs={{0,3},{1,0},{2,1},{3,2},{4,7},{5,4},{6,5},{7,6},{8,11},{9,8},{10,9... | collective-permute-start | bytes 1572872 | tf_op jit(solution)/shard_map/ppermute | solution.py:30
  107.6 3.3 %copy-start.3 = (bf16[512,8192]{1,0:T(8,128)(2,1)}, bf16[512,8192]{1,0:T(8,128)(2,1)S(1)}, u32[]{:S(2)}) copy-start(bf16[512,8192]{1,0:T(8,128)(2,1)S(1)} %input_parts.1) | copy-start | bytes 25165828
  110.9 6.0 %copy-start.16 = (bf16[128,2048]{1,0:T(8,128)(2,1)}, bf16[128,2048]{1,0:T(8,128)(2,1)S(1)}, u32[]{:S(2)}) copy-start(bf16[128,2048]{1,0:T(8,128)(2,1)S(1)} %collective-permute-done.10.su_lo) | copy-start | bytes 1572868
  110.9 6.0 %copy-start.17 = (bf16[128,2048]{1,0:T(8,128)(2,1)}, bf16[128,2048]{1,0:T(8,128)(2,1)S(1)}, u32[]{:S(2)}) copy-start(bf16[128,2048]{1,0:T(8,128)(2,1)S(1)} %collective-permute-done.11.su_hi) | copy-start | bytes 1572868
  116.9 24.6 %collective-permute-start.13 = (bf16[256,2048]{1,0:T(8,128)(2,1)}, bf16[256,2048]{1,0:T(8,128)(2,1)S(1)}, u32[]{:S(2)}, u32[]{:S(2)}) collective-permute-start(bf16[256,2048]{1,0:T(8,128)(2,1)} %get-tuple-element.88), channel_id=1, source_target_pairs={{0,4},{1,5},{2,6},{3,7},{4,8},{5,9},{6,10},{7,11},{8,12},{9,13},{1... | collective-permute-start | bytes 3145736 | tf_op jit(solution)/shard_map/ppermute | solution.py:30
  117.0 24.5 %collective-permute-start.14 = (bf16[256,2048]{1,0:T(8,128)(2,1)}, bf16[256,2048]{1,0:T(8,128)(2,1)S(1)}, u32[]{:S(2)}, u32[]{:S(2)}) collective-permute-start(bf16[256,2048]{1,0:T(8,128)(2,1)} %get-tuple-element.91), channel_id=1, source_target_pairs={{0,12},{1,13},{2,14},{3,15},{4,0},{5,1},{6,2},{7,3},{8,4},{9,5},{1... | collective-permute-start | bytes 3145736 | tf_op jit(solution)/shard_map/ppermute | solution.py:30
  141.6 10.9 %copy-start.14 = (bf16[256,2048]{1,0:T(8,128)(2,1)}, bf16[256,2048]{1,0:T(8,128)(2,1)S(1)}, u32[]{:S(2)}) copy-start(bf16[256,2048]{1,0:T(8,128)(2,1)S(1)} %collective-permute-done.13.pl_hi) | copy-start | bytes 3145732
  141.6 10.9 %copy-start.15 = (bf16[256,2048]{1,0:T(8,128)(2,1)}, bf16[256,2048]{1,0:T(8,128)(2,1)S(1)}, u32[]{:S(2)}) copy-start(bf16[256,2048]{1,0:T(8,128)(2,1)S(1)} %collective-permute-done.14.pl_lo) | copy-start | bytes 3145732
  144.9 12.5 %collective-permute-start.15 = (bf16[128,2048]{1,0:T(8,128)(2,1)}, bf16[128,2048]{1,0:T(8,128)(2,1)S(1)}, u32[]{:S(2)}, u32[]{:S(2)}) collective-permute-start(bf16[128,2048]{1,0:T(8,128)(2,1)} %get-tuple-element.137), channel_id=1, source_target_pairs={{0,4},{1,5},{2,6},{3,7},{4,8},{5,9},{6,10},{7,11},{8,12},{9,13},{1... | collective-permute-start | bytes 1572872 | tf_op jit(solution)/shard_map/ppermute | solution.py:30
  144.9 12.5 %collective-permute-start.16 = (bf16[128,2048]{1,0:T(8,128)(2,1)}, bf16[128,2048]{1,0:T(8,128)(2,1)}, u32[]{:S(2)}, u32[]{:S(2)}) collective-permute-start(bf16[128,2048]{1,0:T(8,128)(2,1)} %get-tuple-element.136), channel_id=1, source_target_pairs={{0,12},{1,13},{2,14},{3,15},{4,0},{5,1},{6,2},{7,3},{8,4},{9,5},{1... | collective-permute-start | bytes 1572872 | tf_op jit(solution)/shard_map/ppermute | solution.py:30
  163.2 5.0 %collective-permute-start.17 = (bf16[32,8192]{1,0:T(8,128)(2,1)}, bf16[32,8192]{1,0:T(8,128)(2,1)S(1)}, u32[]{:S(2)}, u32[]{:S(2)}) collective-permute-start(bf16[32,8192]{1,0:T(8,128)(2,1)} %get-tuple-element.127), channel_id=1, source_target_pairs={{0,16},{16,0},{32,48},{48,32},{64,80},{80,64},{96,112},{112,96},{1... | collective-permute-start | bytes 1572872 | tf_op jit(solution)/shard_map/ppermute | solution.py:39
  169.6 7.7 %collective-permute-start.18 = (bf16[16,8192]{1,0:T(8,128)(2,1)S(1)}, bf16[16,8192]{1,0:T(8,128)(2,1)S(1)}, u32[]{:S(2)}, u32[]{:S(2)}) collective-permute-start(bf16[16,8192]{1,0:T(8,128)(2,1)S(1)} %get-tuple-element.142), channel_id=1, source_target_pairs={{0,32},{16,48},{32,0},{48,16},{64,96},{80,112},{96,64},{112,80},{1... | collective-permute-start | bytes 786440 | tf_op jit(solution)/shard_map/ppermute | solution.py:39
  170.9 21.0 %copy-start.2 = (f32[128,8192]{1,0:T(8,128)S(1)}, f32[128,8192]{1,0:T(8,128)}, u32[]{:S(2)}) copy-start(f32[128,8192]{1,0:T(8,128)} %get-tuple-element.128.merged.refs_5_) | copy-start | bytes 12582916
  170.9 8.5 %collective-permute-start.20 = (bf16[16,8192]{1,0:T(8,128)(2,1)S(1)}, bf16[16,8192]{1,0:T(8,128)(2,1)S(1)}, u32[]{:S(2)}, u32[]{:S(2)}) collective-permute-start(bf16[16,8192]{1,0:T(8,128)(2,1)S(1)} %get-tuple-element.143), channel_id=1, source_target_pairs={{0,96},{16,112},{32,64},{48,80},{64,32},{80,48},{96,0},{112,16},{1... | collective-permute-start | bytes 786440 | tf_op jit(solution)/shard_map/ppermute | solution.py:39
  179.5 7.8 %collective-permute-start.19 = (bf16[16,8192]{1,0:T(8,128)(2,1)S(1)}, bf16[16,8192]{1,0:T(8,128)(2,1)S(1)}, u32[]{:S(2)}, u32[]{:S(2)}) collective-permute-start(bf16[16,8192]{1,0:T(8,128)(2,1)S(1)} %get-tuple-element.140), channel_id=1, source_target_pairs={{0,96},{16,112},{32,64},{48,80},{64,32},{80,48},{96,0},{112,16},{1... | collective-permute-start | bytes 786440 | tf_op jit(solution)/shard_map/ppermute | solution.py:39
  181.4 6.2 %collective-permute-start.21 = (bf16[16,8192]{1,0:T(8,128)(2,1)S(1)}, bf16[16,8192]{1,0:T(8,128)(2,1)S(1)}, u32[]{:S(2)}, u32[]{:S(2)}) collective-permute-start(bf16[16,8192]{1,0:T(8,128)(2,1)S(1)} %get-tuple-element.141), channel_id=1, source_target_pairs={{0,32},{16,48},{32,0},{48,16},{64,96},{80,112},{96,64},{112,80},{1... | collective-permute-start | bytes 786440 | tf_op jit(solution)/shard_map/ppermute | solution.py:39
  187.7 6.7 %copy-start.6 = (bf16[32,8192]{1,0:T(8,128)(2,1)}, bf16[32,8192]{1,0:T(8,128)(2,1)S(1)}, u32[]{:S(2)}) copy-start(bf16[32,8192]{1,0:T(8,128)(2,1)S(1)} %pad_maximum_fusion.mine.refs_3_) | copy-start | bytes 1572868
  187.8 4.1 %collective-permute-start.22 = (bf16[32,8192]{1,0:T(8,128)(2,1)S(1)}, bf16[32,8192]{1,0:T(8,128)(2,1)S(1)}, u32[]{:S(2)}, u32[]{:S(2)}) collective-permute-start(bf16[32,8192]{1,0:T(8,128)(2,1)S(1)} %pad_maximum_fusion.mine.refs_3_), channel_id=1, source_target_pairs={{0,16},{16,0},{32,48},{48,32},{64,80},{80,64},{96,112},{112,96},{1... | collective-permute-start | bytes 1572872 | tf_op jit(solution)/shard_map/ppermute | solution.py:39
  194.4 4.7 %copy-start.10 = (f32[64,64]{1,0:T(8,128)}, f32[64,64]{1,0:T(8,128)S(1)}, u32[]{:S(2)}) copy-start(f32[64,64]{1,0:T(8,128)S(1)} %get-tuple-element.129.gram) | copy-start | bytes 49156
  194.4 1.3 collective-permute-start.23
  195.8 10.2 %collective-permute-start.24 = (f32[128,64]{1,0:T(8,128)S(1)}, f32[128,64]{1,0:T(8,128)S(1)}, u32[]{:S(2)}, u32[]{:S(2)}) collective-permute-start(f32[128,64]{1,0:T(8,128)S(1)} %add.64), channel_id=1, source_target_pairs={{0,64},{16,80},{32,96},{48,112},{64,0},{80,16},{96,32},{112,48},{1... | collective-permute-start | bytes 98312 | tf_op jit(solution)/shard_map/ppermute | solution.py:39
  196.5 9.5 %collective-permute-start.25 = (f32[128,64]{1,0:T(8,128)S(1)}, f32[128,64]{1,0:T(8,128)S(1)}, u32[]{:S(2)}, u32[]{:S(2)}) collective-permute-start(f32[128,64]{1,0:T(8,128)S(1)} %add.64), channel_id=1, source_target_pairs={{0,32},{16,48},{32,64},{48,80},{64,96},{80,112},{96,0},{112,16},{1... | collective-permute-start | bytes 98312 | tf_op jit(solution)/shard_map/ppermute | solution.py:39
  197.7 8.2 %collective-permute-start.26 = (f32[128,64]{1,0:T(8,128)S(1)}, f32[128,64]{1,0:T(8,128)S(1)}, u32[]{:S(2)}, u32[]{:S(2)}) collective-permute-start(f32[128,64]{1,0:T(8,128)S(1)} %add.64), channel_id=1, source_target_pairs={{0,96},{16,112},{32,0},{48,16},{64,32},{80,48},{96,64},{112,80},{1... | collective-permute-start | bytes 98312 | tf_op jit(solution)/shard_map/ppermute | solution.py:39
  206.0 7.6 %copy-start.1 = (bf16[8192,128]{1,0:T(8,128)(2,1)S(1)}, bf16[8192,128]{1,0:T(8,128)(2,1)}, u32[]{:S(2)}) copy-start(bf16[8192,128]{1,0:T(8,128)(2,1)} %param.7) | copy-start | bytes 6291460
  (3 other events, 4.9 us)
Sparse Core Ops, SparseCore 0:
  10.3 54.0 all-gather.2
  117.1 81.4 reduce-scatter.1
